TPU v7x, 32 devices: a whole 2x2x4 slice. The times are simulated.
32 devices in a mesh: segment: 4 (over y, x), patch: 8 (over z, core).
Axes of the slice: x: 2, y: 2, z: 4, core: 2. Of those that a mesh axis runs over, the one named last changes fastest.
Arguments:
- features: bfloat16 [4, 2, 320, 32, 128], P('segment', None, None, 'patch'), may hold values from -48 to 48, as said below
- latent: float32 [2, 4, 32, 128], P(None, None, 'patch'), may hold values from -48 to 48
- plan_pos: int32 [2], replicated, may hold values from 0 to 9
- blocks_used: int32 [4], P('segment'), may hold values from 1 to 2, as said below
- conv1_w: bfloat16 [4, 2, 9, 320, 320], P('segment'), may hold values from -0.109375 to 0.109375
- conv2_w: bfloat16 [4, 2, 9, 320, 320], P('segment'), may hold values from -0.109375 to 0.109375
- norm_gain: float32 [4, 2, 2, 320], P('segment'), may hold values from 0.25 to 1.75
- norm_shift: float32 [4, 2, 2, 320], P('segment'), may hold values from -3 to 3
- in_w: bfloat16 [9, 320, 4], replicated, may hold values from -1 to 1
- head_w: bfloat16 [9, 4, 320], replicated, may hold values from -0.109375 to 0.109375
- head_gain: float32 [320], replicated, may hold values from 0.25 to 1.75
- head_shift: float32 [320], replicated, may hold values from -3 to 3
Outputs:
- latent_out: float32 [2, 4, 32, 128], P(None, None, 'patch', 'segment')
- features_out: bfloat16 [4, 2, 320, 32, 128], P('segment', None, None, 'patch')
Inputs may be any that keep to these rules, and one draw needn't show every extreme that they name: `features`: every entry lies within the range; row magnitudes vary over the rows. `blocks_used`: each section holds 1 or 2 blocks; both counts occur.
All inputs are finite; a program needn't handle non-finite values.
Results may differ from a plain program's by a relative error of at most 0.0075.
Values may be sent and summed in bfloat16 or wider, within the bound.
No kernel may reach another device: no remote copies, remote signals or barrier semaphores. Data moves between devices by JAX's collectives and lax.ppermute only.
A program may use at most 64 MiB of HBM per device.

v0:
```python
import functools

import jax
import jax.numpy as jnp
from jax import lax
from jax.experimental import pallas as pl
from jax.experimental.pallas import tpu as pltpu
from jax.sharding import PartitionSpec as P

GROUPS = 32
STEPS = 2
SCHED = 12
CORES = 2

epsilon = 1e-05
sigma_top = 3.0
sigma_low = 0.1
rho_power = 7.0

F32 = jnp.float32
BF16 = jnp.bfloat16
VMEM_LIMIT = 24 * 1024 * 1024


def sigma_at(position):
    fraction = position.astype(F32) / (SCHED - 1)
    top_root = sigma_top ** (1.0 / rho_power)
    low_root = sigma_low ** (1.0 / rho_power)
    return (top_root + fraction * (low_root - top_root)) ** rho_power


def dot(a, b):
    return lax.dot_general(a, b, (((1,), (0,)), ((), ())), preferred_element_type=F32)


def split3(x):
    hi = x.astype(BF16)
    rest = x - hi.astype(F32)
    mid = rest.astype(BF16)
    lo = (rest - mid.astype(F32)).astype(BF16)
    return hi, mid, lo


def group_sum(x, gather):
    parts = jnp.concatenate(split3(x), axis=0)
    return jnp.sum(dot(gather, parts), axis=1, keepdims=True)


def expand(x, spread):
    return dot(spread, jnp.concatenate(split3(x), axis=0))


def tile_sum(tiles):
    total = tiles[0]
    for tile in tiles[1:]:
        total = total + tile
    return total


def pivot_of(tiles, gather, spread, count):
    mean = group_sum(tile_sum(tiles), gather) / (count * len(tiles))
    return mean, expand(jnp.broadcast_to(mean, (GROUPS, 128)), spread)


def add_deviations(sums, tiles, center):
    first, second = sums
    for tile in tiles:
        dev = tile - center
        first = dev if first is None else first + dev
        second = dev * dev if second is None else second + dev * dev
    return first, second


def finish_stats(pivot, sums, gather, count):
    wide = dot(gather, jnp.concatenate(split3(jnp.concatenate(sums, axis=1)), axis=0))
    first = jnp.sum(wide[:, :128], axis=1, keepdims=True)
    second = jnp.sum(wide[:, 128:], axis=1, keepdims=True)
    return pivot + first / count, jnp.maximum(second - first * first / count, 0.0)


def encode_stats(mean, square):
    lane = lax.broadcasted_iota(jnp.int32, (GROUPS, 128), 1) // 16
    out = jnp.zeros((GROUPS, 128), F32)
    for slot, part in enumerate(split3(mean) + split3(square)):
        out = jnp.where(lane == slot, part.astype(F32), out)
    return out.astype(BF16)


def decode_stats(message):
    wide = message.astype(F32)
    take = [wide[:, 16 * k : 16 * k + 1] for k in range(6)]
    return take[0] + take[1] + take[2], take[3] + take[4] + take[5]


def combine_stats(messages, count):
    pairs = [decode_stats(m) for m in messages]
    mean = sum(p[0] for p in pairs) / len(pairs)
    square = sum(p[1] for p in pairs)
    for p in pairs:
        square = square + count * (p[0] - mean) * (p[0] - mean)
    return mean, lax.rsqrt(square / (count * len(pairs)) + epsilon)


def channel_moments(mean, scale, spread):
    both = jnp.concatenate(
        [jnp.broadcast_to(mean, (GROUPS, 128)), jnp.broadcast_to(scale, (GROUPS, 128))], axis=1
    )
    wide = expand(both, spread)
    return wide[:, :128], wide[:, 128:]


def silu(v):
    half = 0.5 * v
    return half + half * jnp.tanh(half)


def shift_cols(t):
    lane = lax.broadcasted_iota(jnp.int32, t.shape, 1)
    before = jnp.where(lane == 0, 0.0, pltpu.roll(t, 1, 1))
    after = jnp.where(lane == 127, 0.0, pltpu.roll(t, 127, 1))
    return before, after


def fill_row(r, last, tile, moments, flags, patches):
    center, scale, shift = moments
    chans = center.shape[0]
    main = chans // 128 * 128
    tail = chans - main
    t = silu((tile - center) * scale + shift)
    if r == 0:
        t = jnp.where(flags[0] > 0, t, 0.0)
    if r == last:
        t = jnp.where(flags[1] > 0, t, 0.0)
    before, after = shift_cols(t)
    lanes = pl.ds(r * 128, 128)
    for j, piece in enumerate((before, t, after)):
        piece = piece.astype(BF16)
        patches[pl.ds(j * main, main), lanes] = piece[:main]
        patches[pl.ds(3 * main + j * tail, tail), lanes] = piece[main:]


def conv_rows(patches, weight, start, rows):
    depth = weight.shape[1] // 9
    main = depth // 128 * 128
    parts = ((0, 3 * main), (3 * main, 3 * (depth - main)))
    pieces = [
        patches[pl.ds(low, size), pl.ds((start + i) * 128, rows * 128)]
        for low, size in parts
        for i in range(3)
    ]
    return dot(weight[...], jnp.concatenate(pieces, axis=0))


CHUNK = 4


def conv_all(tiles, moments, flags, patches, weight, store, gather, spread):
    rows = len(tiles) - 2
    chans = weight.shape[0]
    filled = 0
    per_row = count_of(chans, 128)
    sums = (None, None)
    for start in range(0, rows, CHUNK):
        while filled < start + CHUNK + 2:
            fill_row(filled, rows + 1, tiles[filled](), moments, flags, patches)
            filled += 1
        kept = store(start, CHUNK, conv_rows(patches, weight, start, CHUNK))
        kept = [kept[:, r * 128 : (r + 1) * 128] for r in range(CHUNK)]
        if start == 0:
            pivot, center = pivot_of(kept, gather, spread, per_row)
        sums = add_deviations(sums, kept, center)
    return encode_stats(*finish_stats(pivot, sums, gather, per_row * rows))


def write_messages(out, stats, top_msg, bot_msg, st_msg):
    chans, cells = out.shape
    st_msg[...] = stats
    for ref, start in ((top_msg, 0), (bot_msg, cells - 128)):
        ref[pl.ds(0, chans), :] = out[:, pl.ds(start, 128)].astype(BF16)
        ref[pl.ds(chans, GROUPS), :] = stats


def pack_kernel(first, second, *outs):
    chans = first.shape[3]
    main = chans // 128 * 128
    tail = chans - main
    for n in range(4):
        pieces = []
        for t in range(9):
            tap = (first, second)[n % 2][0, n // 2, t]
            outs[n][:, pl.ds(t * main, main)] = tap[:, :main]
            pieces.append(tap[:, main:])
        outs[n][:, pl.ds(9 * main, 9 * tail)] = jnp.concatenate(pieces, axis=1)


def count_of(chans, cells):
    return float(chans // GROUPS * cells)


def row_tile(ref, r):
    return lambda: ref[:, pl.ds(r * 128, 128)].astype(F32)


def enter_kernel(own, gather, spread, top_msg, bot_msg, st_msg):
    chans, cells = own.shape
    tiles = [own[:, pl.ds(start, 128)].astype(F32) for start in range(0, cells, 128)]
    per_row = count_of(chans, 128)
    pivot, center = pivot_of(tiles[:2], gather[...], spread[...], per_row)
    sums = add_deviations((None, None), tiles, center)
    stats = encode_stats(*finish_stats(pivot, sums, gather[...], per_row * len(tiles)))
    write_messages(own, stats, top_msg, bot_msg, st_msg)


def pair_kernel(ints, kept, other, out):
    lat = kept.shape[0]
    first = ints[5] == 0
    out[0:lat, :] = jnp.where(first, kept[...], other[...])
    out[lat:, :] = jnp.where(first, other[...], kept[...])


def column(params, k):
    return params[:, k : k + 1]


def gathered(up, down, others, count):
    chans = up.shape[0] - GROUPS
    messages = [up[pl.ds(chans, GROUPS), :], down[pl.ds(chans, GROUPS), :]]
    return combine_stats(messages + [ref[...] for ref in others], count)


def head_kernel(params, own, up, down, weight, spread, *rest):
    others, (out, forward) = rest[:-2], rest[-2:]
    latent = None
    if out.shape[0] == 8:
        others, latent = others[:-1], others[-1]
    chans, cells = own.shape
    rows = cells // 128
    mean, root = gathered(up, down, others, count_of(chans, cells))
    stats = encode_stats(mean, root)
    for ref, low in ((up, 0), (down, 128)):
        forward[pl.ds(0, chans), pl.ds(low, 128)] = ref[pl.ds(0, chans), :]
        forward[pl.ds(chans, GROUPS), pl.ds(low, 128)] = stats
    center, scale = channel_moments(mean, root, spread[...])
    scale = scale * column(params, 8)
    shift = column(params, 9)
    tiles = [row_tile(own, r) for r in range(rows)]
    sums = []
    for tile in tiles:
        act = silu((tile() - center) * scale + shift).astype(BF16)
        y = dot(weight[...], act)
        before, _ = shift_cols(y[0:24])
        _, after = shift_cols(y[48:72])
        sums.append(before + y[24:48] + after)
    for r in range(-1, rows + 1):
        acc = jnp.zeros((8, 128), F32)
        for i in range(3):
            if 0 <= r + i - 1 < rows:
                acc = acc + sums[r + i - 1][8 * i : 8 * i + 8]
        if latent is not None and 0 <= r < rows:
            acc = acc + latent[:, pl.ds(r * 128, 128)]
        out[:, pl.ds((r + 1) * 128, 128)] = acc[: out.shape[0]]


def first_kernel(first_step, chips, ints, floats, params, *rest):
    parts, rest = rest[:chips], rest[chips:]
    if not first_step:
        latent_in, rest = rest[0], rest[1:]
    in_weight, own, forward, weight, gather, spread = rest[:6]
    out, source, latent_out, lat_keep, lat_send, top_msg, bot_msg, st_msg = rest[6:14]
    patches, wide, moments, noise, field, entry = rest[14:]
    chans, cells = own.shape
    rows = cells // 128
    full = chips * rows
    flags = (ints[0], ints[1])
    section, place = ints[2], ints[3]

    @pl.when(section == 0)
    def _():
        noise[...] = jnp.zeros_like(noise)
        for d in range(chips):
            owner = lax.rem(place - d + chips, chips)
            lanes = pl.ds(pl.multiple_of(owner * cells, 128), cells + 256)
            height = parts[d].shape[0]
            noise[:height, lanes] = noise[:height, lanes] + parts[d][...]
        change, root = floats[0], floats[1]
        field[...] = jnp.zeros_like(field)
        for r in range(full):
            piece = noise[:, pl.ds((r + 1) * 128, 128)]
            if first_step:
                old = pltpu.roll(piece, 4, 0)
            else:
                old = latent_in[:, pl.ds(r * 128, 128)]
            new = old + change * piece
            latent_out[:, pl.ds(r * 128, 128)] = new
            scaled = (new / root).astype(BF16).astype(F32)
            before, after = shift_cols(scaled)
            lanes = pl.ds((r + 1) * 128, 128)
            field[pl.ds(0, 8), lanes] = before
            field[pl.ds(8, 8), lanes] = scaled
            field[pl.ds(16, 8), lanes] = after
        half = cells // CORES
        for ref, which in ((lat_keep, ints[5]), (lat_send, 1 - ints[5])):
            begin = pl.multiple_of(place * cells + which * half, 128)
            ref[...] = latent_out[: ref.shape[0], pl.ds(begin, half)]
        sums = (None, None)
        per_row = count_of(chans, 128)
        for z in range(chips):
            taps = [field[:, pl.ds((z * rows + i) * 128, cells)] for i in range(3)]
            rows_out = dot(in_weight[...], jnp.concatenate(taps, axis=0).astype(BF16)).astype(BF16)
            entry[:, pl.ds(z * cells + 128, cells)] = rows_out
            kept = [rows_out[:, r * 128 : (r + 1) * 128].astype(F32) for r in range(rows)]
            if z == 0:
                pivot, center = pivot_of(kept, gather[...], spread[...], per_row)
            sums = add_deviations(sums, kept, center)
        entry[:, pl.ds(0, 128)] = jnp.zeros((chans, 128), BF16)
        entry[:, pl.ds(full * 128 + 128, 128)] = jnp.zeros((chans, 128), BF16)
        count = per_row * full
        mean, square = finish_stats(pivot, sums, gather[...], count)
        scale = lax.rsqrt(square / count + epsilon)
        moments[:, 0:128], moments[:, 128:256] = channel_moments(mean, scale, spread[...])
        wide[...] = entry[:, pl.ds(pl.multiple_of(place * cells, 128), cells + 256)]

    @pl.when(section != 0)
    def _():
        latent_out[...] = jnp.zeros_like(latent_out)
        lat_keep[...] = jnp.zeros_like(lat_keep)
        lat_send[...] = jnp.zeros_like(lat_send)
        mean, scale = decode_stats(forward[pl.ds(chans, GROUPS), pl.ds(0, 128)])
        moments[:, 0:128], moments[:, 128:256] = channel_moments(mean, scale, spread[...])
        wide[:, pl.ds(0, 128)] = forward[pl.ds(0, chans), pl.ds(0, 128)]
        wide[:, pl.ds(128, cells)] = own[...]
        wide[:, pl.ds(cells + 128, 128)] = forward[pl.ds(0, chans), pl.ds(128, 128)]

    source[...] = wide[:, pl.ds(128, cells)]
    tiles = [row_tile(wide, r) for r in range(rows + 2)]
    known = (moments[:, 0:128], moments[:, 128:256] * column(params, 0), column(params, 1))

    def store(start, count, acc):
        out[:, pl.ds(start * 128, count * 128)] = acc
        return acc

    stats_out = conv_all(tiles, known, flags, patches, weight, store, gather[...], spread[...])
    write_messages(out, stats_out, top_msg, bot_msg, st_msg)


def conv_kernel(index, residual, last, ints, params, own, up, down, weight, gather, spread, *rest):
    rest = list(rest)
    base = rest.pop(0) if residual else None
    patches = rest.pop()
    others, (out, top_msg, bot_msg, st_msg) = rest[:-4], rest[-4:]
    chans, cells = own.shape
    rows = cells // 128
    mean, root = gathered(up, down, others, count_of(chans, cells))
    center, scale = channel_moments(mean, root, spread[...])
    tiles = [lambda: up[pl.ds(0, chans), :].astype(F32)]
    tiles += [row_tile(own, r) for r in range(rows)]
    tiles += [lambda: down[pl.ds(0, chans), :].astype(F32)]
    known = (center, scale * column(params, 2 * index), column(params, 2 * index + 1))

    def store(start, count, acc):
        lanes = pl.ds(start * 128, count * 128)
        if residual:
            old = base[:, lanes].astype(F32)
            acc = (old + acc).astype(BF16).astype(F32)
        if last:
            acc = jnp.where(ints[4] >= 2, acc, old)
        out[:, lanes] = acc.astype(out.dtype)
        return acc

    stats_out = conv_all(
        tiles, known, (ints[0], ints[1]), patches, weight, store, gather[...], spread[...]
    )
    write_messages(out, stats_out, top_msg, bot_msg, st_msg)


VM = pl.BlockSpec(memory_space=pltpu.VMEM)
SM = pl.BlockSpec(memory_space=pltpu.SMEM)
HB = pl.BlockSpec(memory_space=pl.ANY)


def call(kernel, outs, in_specs, scratch, flops):
    return pl.pallas_call(
        kernel,
        out_shape=outs,
        in_specs=in_specs,
        out_specs=jax.tree.map(lambda _: VM, outs),
        scratch_shapes=scratch,
        compiler_params=pltpu.CompilerParams(vmem_limit_bytes=VMEM_LIMIT),
        cost_estimate=pl.CostEstimate(flops=flops, bytes_accessed=4_000_000, transcendentals=0),
    )


def sds(shape, dtype):
    return jax.ShapeDtypeStruct(shape, dtype)


def per_device(
    features,
    latent,
    plan_pos,
    blocks_used,
    conv1_w,
    conv2_w,
    norm_gain,
    norm_shift,
    in_w,
    head_w,
    head_gain,
    head_shift,
):
    sections = lax.axis_size("segment")
    patches = lax.axis_size("patch")
    chips = patches // CORES
    section = lax.axis_index("segment")
    core = lax.rem(lax.axis_index("patch"), CORES)
    place = lax.axis_index("patch") // CORES
    _, batch, chans, own_rows, cols = features.shape
    rows = CORES * own_rows
    half = own_rows * cols
    cells = rows * cols
    joint = ("segment", "patch")

    swap_pairs = [(p, p ^ 1) for p in range(patches)]

    def swap(x):
        return lax.ppermute(x, "patch", swap_pairs)

    def around(x, by):
        pairs = [
            (CORES * z + c, CORES * ((z + by) % chips) + c)
            for z in range(chips)
            for c in range(CORES)
        ]
        return lax.ppermute(x, "patch", pairs)

    def device(s, z, c):
        return s * patches + CORES * (z % chips) + c

    def every(shift_section):
        return [
            (s, z, c) for s in shift_section for z in range(chips) for c in range(CORES)
        ]

    def onward(x):
        pairs = [(device(s, z, c), device(s + 1, z, c)) for s, z, c in every(range(sections - 1))]
        return lax.ppermute(x, joint, pairs)

    def to_first(x, by):
        pairs = [
            (device(s, z, c), device((s + 1) % sections, z + by, c))
            for s, z, c in every(range(sections))
        ]
        return lax.ppermute(x, joint, pairs)

    group_of = jnp.arange(chans) // (chans // GROUPS)
    member = (jnp.arange(GROUPS)[:, None] == group_of[None, :]).astype(BF16)
    gather = jnp.tile(member, (1, 3))
    spread = jnp.tile(member.T, (1, 3))

    lat = latent.shape[1]
    ints = jnp.stack(
        [
            (place > 0).astype(jnp.int32),
            (place < chips - 1).astype(jnp.int32),
            section.astype(jnp.int32),
            place.astype(jnp.int32),
            blocks_used[0],
            core.astype(jnp.int32),
        ]
    )

    def pick(x, which):
        return lax.dynamic_index_in_dim(x, which, 0, keepdims=False)

    stats_shape = sds((GROUPS, 128), BF16)
    rows_shape = sds((chans + GROUPS, 128), BF16)
    wide_shape = sds((chans, cells), F32)
    half_shape = sds((chans, cells), BF16)
    conv_flops = 2 * 9 * chans * chans * cells
    conv_scratch = [pltpu.VMEM((3 * chans, cells + 256), BF16)]

    first_core = core == 0
    mine = pick(features[0], core)
    other = swap(pick(features[0], 1 - core))
    own = jnp.concatenate(
        [jnp.where(first_core, mine, other), jnp.where(first_core, other, mine)], axis=1
    ).reshape(chans, cells)
    messages = call(
        enter_kernel, (rows_shape, rows_shape, stats_shape), [VM] * 3, [], 10_000_000
    )(own, gather, spread)

    conv1_w, conv2_w, norm_gain, norm_shift, in_w, head_w, latent, _ = lax.optimization_barrier(
        (conv1_w, conv2_w, norm_gain, norm_shift, in_w, head_w, latent, messages[2])
    )
    params = jnp.stack(
        [x[0, k, q] for k in range(2) for q in range(2) for x in (norm_gain, norm_shift)]
        + [head_gain, head_shift]
        + [jnp.zeros((chans,), F32)] * 6
    ).T
    kernels = call(
        pack_kernel, (sds((chans, 9 * chans), BF16),) * 4, [VM, VM], [], 10_000_000
    )(conv1_w, conv2_w)
    head_packed = jnp.zeros((3, 3, 8, chans), BF16)
    head_packed = head_packed.at[:, :, :lat].set(
        jnp.transpose(head_w.reshape(3, 3, lat, chans), (1, 0, 2, 3))
    ).reshape(72, chans)
    in_packed = jnp.zeros((chans, 3, 3, 8), BF16)
    in_packed = in_packed.at[:, :, :, :lat].set(
        jnp.transpose(in_w.reshape(3, 3, chans, lat), (2, 0, 1, 3))
    ).reshape(chans, 72)
    mine = pick(latent, core)
    other = swap(pick(latent, 1 - core))
    latent_rows = jnp.concatenate(
        [jnp.where(core == 0, mine, other), jnp.where(core == 0, other, mine)], axis=1
    ).reshape(lat, cells)
    latent_rows = jnp.concatenate([jnp.zeros((8 - lat, cells), F32), latent_rows], axis=0)
    position = pick(plan_pos, core)
    sigmas = [sigma_at(position + step) for step in range(STEPS + 1)]
    floats = [
        jnp.stack([sigmas[step + 1] - sigmas[step], jnp.sqrt(sigmas[step + 1] ** 2 + 1.0)])
        for step in range(STEPS)
    ]
    full_latent = None

    def exchange(top_msg, bot_msg, st_msg):
        up = around(bot_msg, 1)
        down = around(top_msg, chips - 1)
        return up, down, [st_msg] + [around(st_msg, d) for d in range(2, chips - 1)]

    for step in range(STEPS):
        first_step = step == 0
        own_next = onward(own)
        up, down, others = exchange(*messages)
        height = 8 if first_step else lat
        extra = [latent_rows] if first_step else []
        noise, forward = call(
            head_kernel,
            (sds((height, cells + 256), F32), sds((chans + GROUPS, 256), BF16)),
            [VM] * (6 + len(others) + len(extra)),
            [],
            300_000_000,
        )(params, own, up, down, head_packed, spread, *others, *extra)
        parts = [to_first(noise, d) for d in range(chips)]
        forward_next = onward(forward)
        extra = [] if first_step else [full_latent]
        middle, source, full_latent, lat_keep, lat_send, *messages = call(
            functools.partial(first_kernel, first_step, chips),
            (
                wide_shape,
                half_shape,
                sds((8, chips * cells), F32),
                sds((lat, half), F32),
                sds((lat, half), F32),
                rows_shape,
                rows_shape,
                stats_shape,
            ),
            [SM, SM] + [VM] * (7 + chips + len(extra)),
            conv_scratch
            + [
                pltpu.VMEM((chans, cells + 256), BF16),
                pltpu.VMEM((chans, 256), F32),
                pltpu.VMEM((8, chips * cells + 256), F32),
                pltpu.VMEM((24, chips * cells + 256), F32),
                pltpu.VMEM((chans, chips * cells + 256), BF16),
            ],
            conv_flops,
        )(
            ints,
            floats[step],
            params,
            *parts,
            *extra,
            in_packed,
            own_next,
            forward_next,
            kernels[0],
            gather,
            spread,
        )

        if step == STEPS - 1:
            latents = call(
                pair_kernel, sds((CORES * lat, half), F32), [SM, VM, VM], [], 100_000
            )(ints, lat_keep, swap(lat_send))
            shares = [latents] + [
                lax.ppermute(
                    latents, "segment", [(q, (q + s) % sections) for q in range(sections)]
                )
                for s in range(1, sections)
            ]

        def conv(index, own, messages, base, last=False):
            up, down, others = exchange(*messages)
            extra = [] if base is None else [base]
            return call(
                functools.partial(conv_kernel, index, base is not None, last),
                (wide_shape if base is None else half_shape, rows_shape, rows_shape, stats_shape),
                [SM] + [VM] * (7 + len(extra) + len(others)),
                conv_scratch,
                conv_flops,
            )(ints, params, own, up, down, kernels[index], gather, spread, *extra, *others)

        one, *messages = conv(1, middle, messages, source)
        middle, *messages = conv(2, one, messages, None)
        own, *messages = conv(3, middle, messages, one, True)

    own, *shares = lax.optimization_barrier((own, *shares))
    low, high = own[:, :half], own[:, half:]
    mine = jnp.where(first_core, low, high)
    other = swap(jnp.where(first_core, high, low))
    pair = jnp.where(first_core, jnp.stack([mine, other]), jnp.stack([other, mine]))
    features_out = pair.reshape(1, batch, chans, own_rows, cols)
    share = cols // sections
    latent_out = None
    for s, piece in enumerate(shares):
        piece = piece.reshape(batch, lat, own_rows, cols)[..., s * share : (s + 1) * share]
        latent_out = piece if latent_out is None else jnp.where(section == s, piece, latent_out)
    return (latent_out, features_out)


def solution(mesh):
    placed = (
        P("segment", None, None, "patch", None),
        P(None, None, "patch", None),
        P(),
        P("segment"),
        P("segment", None, None, None, None),
        P("segment", None, None, None, None),
        P("segment", None, None, None),
        P("segment", None, None, None),
        P(),
        P(),
        P(),
        P(),
    )
    return jax.shard_map(
        per_device,
        mesh=mesh,
        in_specs=placed,
        out_specs=(P(None, None, "patch", "segment"), P("segment", None, None, "patch", None)),
        check_vma=False,
    )
```

profile of v0, /device:TPU:1, one launch (start us, length us, event | category | flops | bytes accessed | tf_op | source)
XLA Modules:
  0.0 160.7 jit_solution(5297817773057442786)
XLA Ops:
  4.5 4.6 %collective-permute-start.9 = (bf16[320,1024]{1,0:T(8,128)(2,1)S(1)}, bf16[320,1024]{1,0:T(8,128)(2,1)S(1)}, u32[]{:S(2)}, u32[]{:S(2)}) collective-permute-start(bf16[320,1024]{1,0:T(8,128)(2,1)S(1)} %bitcast.51), channel_id=1, source_target_pairs={{0,8},{1,9},{2,10},{3,11},{4,12},{5,13},{6,14},{7,15},{8,16},{9,17... | collective-permute-start | bytes 1966088 | tf_op jit(solution)/shard_map/ppermute | solution.py:446
  10.0 2.4 %collective-permute-start.3 = (bf16[32,128]{1,0:T(8,128)(2,1)S(1)}, bf16[32,128]{1,0:T(8,128)(2,1)S(1)}, u32[]{:S(2)}, u32[]{:S(2)}) collective-permute-start(bf16[32,128]{1,0:T(8,128)(2,1)S(1)} %get-tuple-element.83.rest_0_), channel_id=1, source_target_pairs={{0,4},{1,5},{2,6},{3,7},{4,0},{5,1},{6,2},{7,3},{8,12},{9,13},{10,... | collective-permute-start | bytes 24584 | tf_op jit(solution)/shard_map/ppermute | solution.py:434
  16.6 2.7 %collective-permute-done.1.up = bf16[352,128]{1,0:T(8,128)(2,1)S(1)} collective-permute-done((bf16[352,128]{1,0:T(8,128)(2,1)S(1)}, bf16[352,128]{1,0:T(8,128)(2,1)S(1)}, u32[]{:S(2)}, u32[]{:S(2)}) %collective-permute-start.1) | collective-permute-done | bytes 90144 | tf_op jit(solution)/shard_map/ppermute | solution.py:434
  21.6 3.1 %collective-permute-start.10 = (bf16[352,256]{1,0:T(8,128)(2,1)S(1)}, bf16[352,256]{1,0:T(8,128)(2,1)S(1)}, u32[]{:S(2)}, u32[]{:S(2)}) collective-permute-start(bf16[352,256]{1,0:T(8,128)(2,1)S(1)} %get-tuple-element.92), channel_id=1, source_target_pairs={{0,8},{1,9},{2,10},{3,11},{4,12},{5,13},{6,14},{7,15},{8,16},{9,17... | collective-permute-start | bytes 540680 | tf_op jit(solution)/shard_map/ppermute | solution.py:446
  29.3 3.7 %collective-permute-start.8 = (f32[8,1280]{1,0:T(8,128)S(1)}, f32[8,1280]{1,0:T(8,128)S(1)}, u32[]{:S(2)}, u32[]{:S(2)}) collective-permute-start(f32[8,1280]{1,0:T(8,128)S(1)} %get-tuple-element.90), channel_id=1, source_target_pairs={{0,14},{1,15},{2,8},{3,9},{4,10},{5,11},{6,12},{7,13},{8,22},{9,23... | collective-permute-start | bytes 122888 | tf_op jit(solution)/shard_map/ppermute | solution.py:453
  34.0 2.3 %copy-done = bf16[1,2,9,320,320]{4,3,2,1,0:T(8,128)(2,1)S(1)} copy-done((bf16[1,2,9,320,320]{4,3,2,1,0:T(8,128)(2,1)S(1)}, bf16[1,2,9,320,320]{4,3,2,1,0:T(8,128)(2,1)}, u32[]{:S(2)}) %copy-start) | copy-done | bytes 3686424
  36.3 2.3 %copy-done.1 = bf16[1,2,9,320,320]{4,3,2,1,0:T(8,128)(2,1)S(1)} copy-done((bf16[1,2,9,320,320]{4,3,2,1,0:T(8,128)(2,1)S(1)}, bf16[1,2,9,320,320]{4,3,2,1,0:T(8,128)(2,1)}, u32[]{:S(2)}) %copy-start.1) | copy-done | bytes 3686424
  39.3 6.7 %shard_map.134 = (f32[320,1024]{1,0:T(8,128)S(1)}, bf16[320,1024]{1,0:T(8,128)(2,1)S(1)}, f32[8,4096]{1,0:T(8,128)S(1)}, f32[4,512]{1,0:T(4,128)}, f32[4,512]{1,...) custom-call(s32[6]{0:T(128)S(1)} %stack.78.ints, ...), custom_call_target="tpu_custom_call" | custom-call | flops 1887436800 | bytes 4000000 | tf_op jit(solution)/shard_map/pallas_call | solution.py:546
  46.1 3.2 %collective-permute-start.12 = (bf16[352,128]{1,0:T(8,128)(2,1)S(1)}, bf16[352,128]{1,0:T(8,128)(2,1)S(1)}, u32[]{:S(2)}, u32[]{:S(2)}) collective-permute-start(bf16[352,128]{1,0:T(8,128)(2,1)S(1)} %get-tuple-element.98), channel_id=1, source_target_pairs={{0,6},{1,7},{2,0},{3,1},{4,2},{5,3},{6,4},{7,5},{8,14},{9,15},{10,... | collective-permute-start | bytes 270344 | tf_op jit(solution)/shard_map/ppermute | solution.py:434
  49.3 3.5 %collective-permute-done.13.rest_2_ = bf16[32,128]{1,0:T(8,128)(2,1)S(1)} collective-permute-done((bf16[32,128]{1,0:T(8,128)(2,1)S(1)}, bf16[32,128]{1,0:T(8,128)(2,1)S(1)}, u32[]{:S(2)}, u32[]{:S(2)}) %collective-permute-start.13) | collective-permute-done | bytes 8224 | tf_op jit(solution)/shard_map/ppermute | solution.py:434
  52.8 4.4 %shard_map.135 = (bf16[320,1024]{1,0:T(8,128)(2,1)S(1)}, bf16[352,128]{1,0:T(8,128)(2,1)S(1)}, bf16[352,128]{1,0:T(8,128)(2,1)S(1)}, bf16[32,128]{1,0:T(8,128)(2,1)S(1)}) custom-call(s32[6]{0:T(128)S(1)} %stack.78.ints, f32[320,16]{1,0:T(8,128)S(1)} %bitcast.56, f32[320,1024]{1,0:T(8,128)S(1)} %get-tuple-element.96.own, ...), custom_call_target="tpu_custom_call" | custom-call | flops 1887436800 | bytes 4000000 | tf_op jit(solution)/shard_map/pallas_call | solution.py:596
  57.3 3.3 %collective-permute-start.15 = (bf16[352,128]{1,0:T(8,128)(2,1)S(1)}, bf16[352,128]{1,0:T(8,128)(2,1)S(1)}, u32[]{:S(2)}, u32[]{:S(2)}) collective-permute-start(bf16[352,128]{1,0:T(8,128)(2,1)S(1)} %get-tuple-element.104), channel_id=1, source_target_pairs={{0,6},{1,7},{2,0},{3,1},{4,2},{5,3},{6,4},{7,5},{8,14},{9,15},{10,... | collective-permute-start | bytes 270344 | tf_op jit(solution)/shard_map/ppermute | solution.py:434
  60.5 3.4 %collective-permute-done.16.rest_1_ = bf16[32,128]{1,0:T(8,128)(2,1)S(1)} collective-permute-done((bf16[32,128]{1,0:T(8,128)(2,1)S(1)}, bf16[32,128]{1,0:T(8,128)(2,1)S(1)}, u32[]{:S(2)}, u32[]{:S(2)}) %collective-permute-start.16) | collective-permute-done | bytes 8224 | tf_op jit(solution)/shard_map/ppermute | solution.py:434
  63.9 4.3 %shard_map.136 = (f32[320,1024]{1,0:T(8,128)S(1)}, bf16[352,128]{1,0:T(8,128)(2,1)S(1)}, bf16[352,128]{1,0:T(8,128)(2,1)S(1)}, bf16[32,128]{1,0:T(8,128)(2,1)S(1)}) custom-call(s32[6]{0:T(128)S(1)} %stack.78.ints, f32[320,16]{1,0:T(8,128)S(1)} %bitcast.57, bf16[320,1024]{1,0:T(8,128)(2,1)S(1)} %get-tuple-element.102.own.rest_0_, ...), custom_call_target="tpu_custom_call" | custom-call | flops 1887436800 | bytes 4000000 | tf_op jit(solution)/shard_map/pallas_call | solution.py:596
  68.3 3.3 %collective-permute-start.18 = (bf16[352,128]{1,0:T(8,128)(2,1)S(1)}, bf16[352,128]{1,0:T(8,128)(2,1)S(1)}, u32[]{:S(2)}, u32[]{:S(2)}) collective-permute-start(bf16[352,128]{1,0:T(8,128)(2,1)S(1)} %get-tuple-element.109), channel_id=1, source_target_pairs={{0,6},{1,7},{2,0},{3,1},{4,2},{5,3},{6,4},{7,5},{8,14},{9,15},{10,... | collective-permute-start | bytes 270344 | tf_op jit(solution)/shard_map/ppermute | solution.py:434
  71.6 3.4 %collective-permute-done.19.rest_2_ = bf16[32,128]{1,0:T(8,128)(2,1)S(1)} collective-permute-done((bf16[32,128]{1,0:T(8,128)(2,1)S(1)}, bf16[32,128]{1,0:T(8,128)(2,1)S(1)}, u32[]{:S(2)}, u32[]{:S(2)}) %collective-permute-start.19) | collective-permute-done | bytes 8224 | tf_op jit(solution)/shard_map/ppermute | solution.py:434
  75.0 4.4 %shard_map.137 = (bf16[320,1024]{1,0:T(8,128)(2,1)S(1)}, bf16[352,128]{1,0:T(8,128)(2,1)S(1)}, bf16[352,128]{1,0:T(8,128)(2,1)S(1)}, bf16[32,128]{1,0:T(8,128)(2,1)S(1)}) custom-call(s32[6]{0:T(128)S(1)} %stack.78.ints, f32[320,16]{1,0:T(8,128)S(1)} %bitcast.58, f32[320,1024]{1,0:T(8,128)S(1)} %get-tuple-element.107.own, ...), custom_call_target="tpu_custom_call" | custom-call | flops 1887436800 | bytes 4000000 | tf_op jit(solution)/shard_map/pallas_call | solution.py:596
  80.8 3.3 %collective-permute-start.21 = (bf16[352,128]{1,0:T(8,128)(2,1)S(1)}, bf16[352,128]{1,0:T(8,128)(2,1)S(1)}, u32[]{:S(2)}, u32[]{:S(2)}) collective-permute-start(bf16[352,128]{1,0:T(8,128)(2,1)S(1)} %get-tuple-element.114), channel_id=1, source_target_pairs={{0,6},{1,7},{2,0},{3,1},{4,2},{5,3},{6,4},{7,5},{8,14},{9,15},{10,... | collective-permute-start | bytes 270344 | tf_op jit(solution)/shard_map/ppermute | solution.py:434
  84.1 3.4 %collective-permute-done.22.rest_1_ = bf16[32,128]{1,0:T(8,128)(2,1)S(1)} collective-permute-done((bf16[32,128]{1,0:T(8,128)(2,1)S(1)}, bf16[32,128]{1,0:T(8,128)(2,1)S(1)}, u32[]{:S(2)}, u32[]{:S(2)}) %collective-permute-start.22) | collective-permute-done | bytes 8224 | tf_op jit(solution)/shard_map/ppermute | solution.py:434
  88.6 3.7 %collective-permute-start.28 = (bf16[352,256]{1,0:T(8,128)(2,1)S(1)}, bf16[352,256]{1,0:T(8,128)(2,1)S(1)}, u32[]{:S(2)}, u32[]{:S(2)}) collective-permute-start(bf16[352,256]{1,0:T(8,128)(2,1)S(1)} %get-tuple-element.118), channel_id=1, source_target_pairs={{0,8},{1,9},{2,10},{3,11},{4,12},{5,13},{6,14},{7,15},{8,16},{9,17... | collective-permute-start | bytes 540680 | tf_op jit(solution)/shard_map/ppermute | solution.py:446
  94.6 3.0 %collective-permute-done.23.rest_0_ = f32[4,1280]{1,0:T(4,128)S(1)} collective-permute-done((f32[4,1280]{1,0:T(4,128)S(1)}, f32[4,1280]{1,0:T(4,128)S(1)}, u32[]{:S(2)}, u32[]{:S(2)}) %collective-permute-start.23) | collective-permute-done | bytes 20512 | tf_op jit(solution)/shard_map/ppermute | solution.py:453
  97.6 3.7 %collective-permute-start.26 = (f32[4,1280]{1,0:T(4,128)S(1)}, f32[4,1280]{1,0:T(4,128)S(1)}, u32[]{:S(2)}, u32[]{:S(2)}) collective-permute-start(f32[4,1280]{1,0:T(4,128)S(1)} %get-tuple-element.116), channel_id=1, source_target_pairs={{0,14},{1,15},{2,8},{3,9},{4,10},{5,11},{6,12},{7,13},{8,22},{9,23... | collective-permute-start | bytes 61448 | tf_op jit(solution)/shard_map/ppermute | solution.py:453
  102.2 6.9 %shard_map.139 = (f32[320,1024]{1,0:T(8,128)S(1)}, bf16[320,1024]{1,0:T(8,128)(2,1)S(1)}, f32[8,4096]{1,0:T(8,128)}, f32[4,512]{1,0:T(4,128)S(1)}, f32[4,512]{1,...) custom-call(s32[6]{0:T(128)S(1)} %stack.78.ints, ...), custom_call_target="tpu_custom_call" | custom-call | flops 1887436800 | bytes 4000000 | tf_op jit(solution)/shard_map/pallas_call | solution.py:546
  109.1 3.3 %collective-permute-start.30 = (bf16[352,128]{1,0:T(8,128)(2,1)S(1)}, bf16[352,128]{1,0:T(8,128)(2,1)S(1)}, u32[]{:S(2)}, u32[]{:S(2)}) collective-permute-start(bf16[352,128]{1,0:T(8,128)(2,1)S(1)} %get-tuple-element.121), channel_id=1, source_target_pairs={{0,6},{1,7},{2,0},{3,1},{4,2},{5,3},{6,4},{7,5},{8,14},{9,15},{10,... | collective-permute-start | bytes 270344 | tf_op jit(solution)/shard_map/ppermute | solution.py:434
  112.6 3.1 %collective-permute-done.31.rest_2_ = bf16[32,128]{1,0:T(8,128)(2,1)S(1)} collective-permute-done((bf16[32,128]{1,0:T(8,128)(2,1)S(1)}, bf16[32,128]{1,0:T(8,128)(2,1)S(1)}, u32[]{:S(2)}, u32[]{:S(2)}) %collective-permute-start.31) | collective-permute-done | bytes 8224 | tf_op jit(solution)/shard_map/ppermute | solution.py:434
  115.8 4.3 %shard_map.140 = (bf16[320,1024]{1,0:T(8,128)(2,1)S(1)}, bf16[352,128]{1,0:T(8,128)(2,1)S(1)}, bf16[352,128]{1,0:T(8,128)(2,1)S(1)}, bf16[32,128]{1,0:T(8,128)(2,1)S(1)}) custom-call(s32[6]{0:T(128)S(1)} %stack.78.ints, f32[320,16]{1,0:T(8,128)S(1)} %bitcast.61, f32[320,1024]{1,0:T(8,128)S(1)} %get-tuple-element.119.own, ...), custom_call_target="tpu_custom_call" | custom-call | flops 1887436800 | bytes 4000000 | tf_op jit(solution)/shard_map/pallas_call | solution.py:596
  120.5 2.9 %collective-permute-start.33 = (bf16[352,128]{1,0:T(8,128)(2,1)S(1)}, bf16[352,128]{1,0:T(8,128)(2,1)S(1)}, u32[]{:S(2)}, u32[]{:S(2)}) collective-permute-start(bf16[352,128]{1,0:T(8,128)(2,1)S(1)} %get-tuple-element.126), channel_id=1, source_target_pairs={{0,6},{1,7},{2,0},{3,1},{4,2},{5,3},{6,4},{7,5},{8,14},{9,15},{10,... | collective-permute-start | bytes 270344 | tf_op jit(solution)/shard_map/ppermute | solution.py:434
  123.4 3.4 %collective-permute-done.34.rest_1_ = bf16[32,128]{1,0:T(8,128)(2,1)S(1)} collective-permute-done((bf16[32,128]{1,0:T(8,128)(2,1)S(1)}, bf16[32,128]{1,0:T(8,128)(2,1)S(1)}, u32[]{:S(2)}, u32[]{:S(2)}) %collective-permute-start.34) | collective-permute-done | bytes 8224 | tf_op jit(solution)/shard_map/ppermute | solution.py:434
  126.9 4.3 %shard_map.141 = (f32[320,1024]{1,0:T(8,128)S(1)}, bf16[352,128]{1,0:T(8,128)(2,1)S(1)}, bf16[352,128]{1,0:T(8,128)(2,1)S(1)}, bf16[32,128]{1,0:T(8,128)(2,1)S(1)}) custom-call(s32[6]{0:T(128)S(1)} %stack.78.ints, f32[320,16]{1,0:T(8,128)S(1)} %bitcast.62, bf16[320,1024]{1,0:T(8,128)(2,1)S(1)} %get-tuple-element.124.own.rest_0_, ...), custom_call_target="tpu_custom_call" | custom-call | flops 1887436800 | bytes 4000000 | tf_op jit(solution)/shard_map/pallas_call | solution.py:596
  131.9 2.5 %collective-permute-start.36 = (bf16[352,128]{1,0:T(8,128)(2,1)S(1)}, bf16[352,128]{1,0:T(8,128)(2,1)S(1)}, u32[]{:S(2)}, u32[]{:S(2)}) collective-permute-start(bf16[352,128]{1,0:T(8,128)(2,1)S(1)} %get-tuple-element.130), channel_id=1, source_target_pairs={{0,6},{1,7},{2,0},{3,1},{4,2},{5,3},{6,4},{7,5},{8,14},{9,15},{10,... | collective-permute-start | bytes 270344 | tf_op jit(solution)/shard_map/ppermute | solution.py:434
  134.5 13.6 %collective-permute-start.38 = (f32[4,512]{1,0:T(4,128)S(1)}, f32[4,512]{1,0:T(4,128)S(1)}, u32[]{:S(2)}, u32[]{:S(2)}) collective-permute-start(f32[4,512]{1,0:T(4,128)S(1)} %get-tuple-element.134), channel_id=1, source_target_pairs={{0,1},{1,0},{2,3},{3,2},{4,5},{5,4},{6,7},{7,6},{8,9},{9,8},{10,11... | collective-permute-start | bytes 24584 | tf_op jit(solution)/shard_map/ppermute | solution.py:426
  151.9 5.1 %shard_map.142 = (bf16[320,1024]{1,0:T(8,128)(2,1)S(1)}, bf16[352,128]{1,0:T(8,128)(2,1)}, bf16[352,128]{1,0:T(8,128)(2,1)}, bf16[32,128]{1,0:T(8,128)(2,1)}) custom-call(s32[6]{0:T(128)S(1)} %stack.78.ints, f32[320,16]{1,0:T(8,128)S(1)} %bitcast.63, f32[320,1024]{1,0:T(8,128)S(1)} %get-tuple-element.128.own, ...), custom_call_target="tpu_custom_call" | custom-call | flops 1887436800 | bytes 4000000 | tf_op jit(solution)/shard_map/pallas_call | solution.py:596
  (125 shorter events, 29.7 us)
Async XLA Ops:
  4.5 34.9 %collective-permute-start.9 = (bf16[320,1024]{1,0:T(8,128)(2,1)S(1)}, bf16[320,1024]{1,0:T(8,128)(2,1)S(1)}, u32[]{:S(2)}, u32[]{:S(2)}) collective-permute-start(bf16[320,1024]{1,0:T(8,128)(2,1)S(1)} %bitcast.51), channel_id=1, source_target_pairs={{0,8},{1,9},{2,10},{3,11},{4,12},{5,13},{6,14},{7,15},{8,16},{9,17... | collective-permute-start | bytes 1966088 | tf_op jit(solution)/shard_map/ppermute | solution.py:446
  10.0 6.6 %collective-permute-start.3 = (bf16[32,128]{1,0:T(8,128)(2,1)S(1)}, bf16[32,128]{1,0:T(8,128)(2,1)S(1)}, u32[]{:S(2)}, u32[]{:S(2)}) collective-permute-start(bf16[32,128]{1,0:T(8,128)(2,1)S(1)} %get-tuple-element.83.rest_0_), channel_id=1, source_target_pairs={{0,4},{1,5},{2,6},{3,7},{4,0},{5,1},{6,2},{7,3},{8,12},{9,13},{10,... | collective-permute-start | bytes 24584 | tf_op jit(solution)/shard_map/ppermute | solution.py:434
  13.2 6.1 %collective-permute-start.1 = (bf16[352,128]{1,0:T(8,128)(2,1)S(1)}, bf16[352,128]{1,0:T(8,128)(2,1)S(1)}, u32[]{:S(2)}, u32[]{:S(2)}) collective-permute-start(bf16[352,128]{1,0:T(8,128)(2,1)S(1)} %get-tuple-element.86), channel_id=1, source_target_pairs={{0,2},{1,3},{2,4},{3,5},{4,6},{5,7},{6,0},{7,1},{8,10},{9,11},{10,... | collective-permute-start | bytes 270344 | tf_op jit(solution)/shard_map/ppermute | solution.py:434
  14.5 6.0 %collective-permute-start.2 = (bf16[352,128]{1,0:T(8,128)(2,1)S(1)}, bf16[352,128]{1,0:T(8,128)(2,1)S(1)}, u32[]{:S(2)}, u32[]{:S(2)}) collective-permute-start(bf16[352,128]{1,0:T(8,128)(2,1)S(1)} %get-tuple-element.87), channel_id=1, source_target_pairs={{0,6},{1,7},{2,0},{3,1},{4,2},{5,3},{6,4},{7,5},{8,14},{9,15},{10,... | collective-permute-start | bytes 270344 | tf_op jit(solution)/shard_map/ppermute | solution.py:434
  21.6 17.7 %collective-permute-start.10 = (bf16[352,256]{1,0:T(8,128)(2,1)S(1)}, bf16[352,256]{1,0:T(8,128)(2,1)S(1)}, u32[]{:S(2)}, u32[]{:S(2)}) collective-permute-start(bf16[352,256]{1,0:T(8,128)(2,1)S(1)} %get-tuple-element.92), channel_id=1, source_target_pairs={{0,8},{1,9},{2,10},{3,11},{4,12},{5,13},{6,14},{7,15},{8,16},{9,17... | collective-permute-start | bytes 540680 | tf_op jit(solution)/shard_map/ppermute | solution.py:446
  27.8 11.5 %collective-permute-start.6 = (f32[8,1280]{1,0:T(8,128)S(1)}, f32[8,1280]{1,0:T(8,128)S(1)}, u32[]{:S(2)}, u32[]{:S(2)}) collective-permute-start(f32[8,1280]{1,0:T(8,128)S(1)} %get-tuple-element.90), channel_id=1, source_target_pairs={{0,10},{1,11},{2,12},{3,13},{4,14},{5,15},{6,8},{7,9},{8,18},{9,19... | collective-permute-start | bytes 122888 | tf_op jit(solution)/shard_map/ppermute | solution.py:453
  27.9 11.4 %collective-permute-start.7 = (f32[8,1280]{1,0:T(8,128)S(1)}, f32[8,1280]{1,0:T(8,128)S(1)}, u32[]{:S(2)}, u32[]{:S(2)}) collective-permute-start(f32[8,1280]{1,0:T(8,128)S(1)} %get-tuple-element.90), channel_id=1, source_target_pairs={{0,12},{1,13},{2,14},{3,15},{4,8},{5,9},{6,10},{7,11},{8,20},{9,21... | collective-permute-start | bytes 122888 | tf_op jit(solution)/shard_map/ppermute | solution.py:453
  29.3 10.0 %collective-permute-start.8 = (f32[8,1280]{1,0:T(8,128)S(1)}, f32[8,1280]{1,0:T(8,128)S(1)}, u32[]{:S(2)}, u32[]{:S(2)}) collective-permute-start(f32[8,1280]{1,0:T(8,128)S(1)} %get-tuple-element.90), channel_id=1, source_target_pairs={{0,14},{1,15},{2,8},{3,9},{4,10},{5,11},{6,12},{7,13},{8,22},{9,23... | collective-permute-start | bytes 122888 | tf_op jit(solution)/shard_map/ppermute | solution.py:453
  46.0 6.8 %collective-permute-start.11 = (bf16[352,128]{1,0:T(8,128)(2,1)S(1)}, bf16[352,128]{1,0:T(8,128)(2,1)S(1)}, u32[]{:S(2)}, u32[]{:S(2)}) collective-permute-start(bf16[352,128]{1,0:T(8,128)(2,1)S(1)} %get-tuple-element.97), channel_id=1, source_target_pairs={{0,2},{1,3},{2,4},{3,5},{4,6},{5,7},{6,0},{7,1},{8,10},{9,11},{10,... | collective-permute-start | bytes 270344 | tf_op jit(solution)/shard_map/ppermute | solution.py:434
  46.1 6.7 %collective-permute-start.12 = (bf16[352,128]{1,0:T(8,128)(2,1)S(1)}, bf16[352,128]{1,0:T(8,128)(2,1)S(1)}, u32[]{:S(2)}, u32[]{:S(2)}) collective-permute-start(bf16[352,128]{1,0:T(8,128)(2,1)S(1)} %get-tuple-element.98), channel_id=1, source_target_pairs={{0,6},{1,7},{2,0},{3,1},{4,2},{5,3},{6,4},{7,5},{8,14},{9,15},{10,... | collective-permute-start | bytes 270344 | tf_op jit(solution)/shard_map/ppermute | solution.py:434
  57.2 6.7 %collective-permute-start.14 = (bf16[352,128]{1,0:T(8,128)(2,1)S(1)}, bf16[352,128]{1,0:T(8,128)(2,1)S(1)}, u32[]{:S(2)}, u32[]{:S(2)}) collective-permute-start(bf16[352,128]{1,0:T(8,128)(2,1)S(1)} %get-tuple-element.103), channel_id=1, source_target_pairs={{0,2},{1,3},{2,4},{3,5},{4,6},{5,7},{6,0},{7,1},{8,10},{9,11},{10,... | collective-permute-start | bytes 270344 | tf_op jit(solution)/shard_map/ppermute | solution.py:434
  57.3 6.7 %collective-permute-start.15 = (bf16[352,128]{1,0:T(8,128)(2,1)S(1)}, bf16[352,128]{1,0:T(8,128)(2,1)S(1)}, u32[]{:S(2)}, u32[]{:S(2)}) collective-permute-start(bf16[352,128]{1,0:T(8,128)(2,1)S(1)} %get-tuple-element.104), channel_id=1, source_target_pairs={{0,6},{1,7},{2,0},{3,1},{4,2},{5,3},{6,4},{7,5},{8,14},{9,15},{10,... | collective-permute-start | bytes 270344 | tf_op jit(solution)/shard_map/ppermute | solution.py:434
  68.2 6.7 %collective-permute-start.17 = (bf16[352,128]{1,0:T(8,128)(2,1)S(1)}, bf16[352,128]{1,0:T(8,128)(2,1)S(1)}, u32[]{:S(2)}, u32[]{:S(2)}) collective-permute-start(bf16[352,128]{1,0:T(8,128)(2,1)S(1)} %get-tuple-element.108), channel_id=1, source_target_pairs={{0,2},{1,3},{2,4},{3,5},{4,6},{5,7},{6,0},{7,1},{8,10},{9,11},{10,... | collective-permute-start | bytes 270344 | tf_op jit(solution)/shard_map/ppermute | solution.py:434
  68.3 6.7 %collective-permute-start.18 = (bf16[352,128]{1,0:T(8,128)(2,1)S(1)}, bf16[352,128]{1,0:T(8,128)(2,1)S(1)}, u32[]{:S(2)}, u32[]{:S(2)}) collective-permute-start(bf16[352,128]{1,0:T(8,128)(2,1)S(1)} %get-tuple-element.109), channel_id=1, source_target_pairs={{0,6},{1,7},{2,0},{3,1},{4,2},{5,3},{6,4},{7,5},{8,14},{9,15},{10,... | collective-permute-start | bytes 270344 | tf_op jit(solution)/shard_map/ppermute | solution.py:434
  79.4 22.8 %collective-permute-start.27 = (bf16[320,1024]{1,0:T(8,128)(2,1)S(1)}, bf16[320,1024]{1,0:T(8,128)(2,1)S(1)}, u32[]{:S(2)}, u32[]{:S(2)}) collective-permute-start(bf16[320,1024]{1,0:T(8,128)(2,1)S(1)} %get-tuple-element.112.own), channel_id=1, source_target_pairs={{0,8},{1,9},{2,10},{3,11},{4,12},{5,13},{6,14},{7,15},{8,16},{9,17... | collective-permute-start | bytes 1966088 | tf_op jit(solution)/shard_map/ppermute | solution.py:446
  80.7 6.7 %collective-permute-start.20 = (bf16[352,128]{1,0:T(8,128)(2,1)S(1)}, bf16[352,128]{1,0:T(8,128)(2,1)S(1)}, u32[]{:S(2)}, u32[]{:S(2)}) collective-permute-start(bf16[352,128]{1,0:T(8,128)(2,1)S(1)} %get-tuple-element.113), channel_id=1, source_target_pairs={{0,2},{1,3},{2,4},{3,5},{4,6},{5,7},{6,0},{7,1},{8,10},{9,11},{10,... | collective-permute-start | bytes 270344 | tf_op jit(solution)/shard_map/ppermute | solution.py:434
  80.8 6.7 %collective-permute-start.21 = (bf16[352,128]{1,0:T(8,128)(2,1)S(1)}, bf16[352,128]{1,0:T(8,128)(2,1)S(1)}, u32[]{:S(2)}, u32[]{:S(2)}) collective-permute-start(bf16[352,128]{1,0:T(8,128)(2,1)S(1)} %get-tuple-element.114), channel_id=1, source_target_pairs={{0,6},{1,7},{2,0},{3,1},{4,2},{5,3},{6,4},{7,5},{8,14},{9,15},{10,... | collective-permute-start | bytes 270344 | tf_op jit(solution)/shard_map/ppermute | solution.py:434
  88.6 13.6 %collective-permute-start.28 = (bf16[352,256]{1,0:T(8,128)(2,1)S(1)}, bf16[352,256]{1,0:T(8,128)(2,1)S(1)}, u32[]{:S(2)}, u32[]{:S(2)}) collective-permute-start(bf16[352,256]{1,0:T(8,128)(2,1)S(1)} %get-tuple-element.118), channel_id=1, source_target_pairs={{0,8},{1,9},{2,10},{3,11},{4,12},{5,13},{6,14},{7,15},{8,16},{9,17... | collective-permute-start | bytes 540680 | tf_op jit(solution)/shard_map/ppermute | solution.py:446
  92.3 5.3 %collective-permute-start.23 = (f32[4,1280]{1,0:T(4,128)S(1)}, f32[4,1280]{1,0:T(4,128)S(1)}, u32[]{:S(2)}, u32[]{:S(2)}) collective-permute-start(f32[4,1280]{1,0:T(4,128)S(1)} %get-tuple-element.116), channel_id=1, source_target_pairs={{0,8},{1,9},{2,10},{3,11},{4,12},{5,13},{6,14},{7,15},{8,16},{9,17... | collective-permute-start | bytes 61448 | tf_op jit(solution)/shard_map/ppermute | solution.py:453
  93.0 8.3 %collective-permute-start.24 = (f32[4,1280]{1,0:T(4,128)S(1)}, f32[4,1280]{1,0:T(4,128)S(1)}, u32[]{:S(2)}, u32[]{:S(2)}) collective-permute-start(f32[4,1280]{1,0:T(4,128)S(1)} %get-tuple-element.116), channel_id=1, source_target_pairs={{0,10},{1,11},{2,12},{3,13},{4,14},{5,15},{6,8},{7,9},{8,18},{9,19... | collective-permute-start | bytes 61448 | tf_op jit(solution)/shard_map/ppermute | solution.py:453
  93.1 8.3 %collective-permute-start.25 = (f32[4,1280]{1,0:T(4,128)S(1)}, f32[4,1280]{1,0:T(4,128)S(1)}, u32[]{:S(2)}, u32[]{:S(2)}) collective-permute-start(f32[4,1280]{1,0:T(4,128)S(1)} %get-tuple-element.116), channel_id=1, source_target_pairs={{0,12},{1,13},{2,14},{3,15},{4,8},{5,9},{6,10},{7,11},{8,20},{9,21... | collective-permute-start | bytes 61448 | tf_op jit(solution)/shard_map/ppermute | solution.py:453
  97.6 4.6 %collective-permute-start.26 = (f32[4,1280]{1,0:T(4,128)S(1)}, f32[4,1280]{1,0:T(4,128)S(1)}, u32[]{:S(2)}, u32[]{:S(2)}) collective-permute-start(f32[4,1280]{1,0:T(4,128)S(1)} %get-tuple-element.116), channel_id=1, source_target_pairs={{0,14},{1,15},{2,8},{3,9},{4,10},{5,11},{6,12},{7,13},{8,22},{9,23... | collective-permute-start | bytes 61448 | tf_op jit(solution)/shard_map/ppermute | solution.py:453
  109.1 6.7 %collective-permute-start.29 = (bf16[352,128]{1,0:T(8,128)(2,1)S(1)}, bf16[352,128]{1,0:T(8,128)(2,1)S(1)}, u32[]{:S(2)}, u32[]{:S(2)}) collective-permute-start(bf16[352,128]{1,0:T(8,128)(2,1)S(1)} %get-tuple-element.120), channel_id=1, source_target_pairs={{0,2},{1,3},{2,4},{3,5},{4,6},{5,7},{6,0},{7,1},{8,10},{9,11},{10,... | collective-permute-start | bytes 270344 | tf_op jit(solution)/shard_map/ppermute | solution.py:434
  109.1 6.7 %collective-permute-start.30 = (bf16[352,128]{1,0:T(8,128)(2,1)S(1)}, bf16[352,128]{1,0:T(8,128)(2,1)S(1)}, u32[]{:S(2)}, u32[]{:S(2)}) collective-permute-start(bf16[352,128]{1,0:T(8,128)(2,1)S(1)} %get-tuple-element.121), channel_id=1, source_target_pairs={{0,6},{1,7},{2,0},{3,1},{4,2},{5,3},{6,4},{7,5},{8,14},{9,15},{10,... | collective-permute-start | bytes 270344 | tf_op jit(solution)/shard_map/ppermute | solution.py:434
  120.1 6.7 %collective-permute-start.32 = (bf16[352,128]{1,0:T(8,128)(2,1)S(1)}, bf16[352,128]{1,0:T(8,128)(2,1)S(1)}, u32[]{:S(2)}, u32[]{:S(2)}) collective-permute-start(bf16[352,128]{1,0:T(8,128)(2,1)S(1)} %get-tuple-element.125), channel_id=1, source_target_pairs={{0,2},{1,3},{2,4},{3,5},{4,6},{5,7},{6,0},{7,1},{8,10},{9,11},{10,... | collective-permute-start | bytes 270344 | tf_op jit(solution)/shard_map/ppermute | solution.py:434
  120.5 6.3 %collective-permute-start.33 = (bf16[352,128]{1,0:T(8,128)(2,1)S(1)}, bf16[352,128]{1,0:T(8,128)(2,1)S(1)}, u32[]{:S(2)}, u32[]{:S(2)}) collective-permute-start(bf16[352,128]{1,0:T(8,128)(2,1)S(1)} %get-tuple-element.126), channel_id=1, source_target_pairs={{0,6},{1,7},{2,0},{3,1},{4,2},{5,3},{6,4},{7,5},{8,14},{9,15},{10,... | collective-permute-start | bytes 270344 | tf_op jit(solution)/shard_map/ppermute | solution.py:434
  131.2 20.7 %collective-permute-start.35 = (bf16[352,128]{1,0:T(8,128)(2,1)S(1)}, bf16[352,128]{1,0:T(8,128)(2,1)S(1)}, u32[]{:S(2)}, u32[]{:S(2)}) collective-permute-start(bf16[352,128]{1,0:T(8,128)(2,1)S(1)} %get-tuple-element.129), channel_id=1, source_target_pairs={{0,2},{1,3},{2,4},{3,5},{4,6},{5,7},{6,0},{7,1},{8,10},{9,11},{10,... | collective-permute-start | bytes 270344 | tf_op jit(solution)/shard_map/ppermute | solution.py:434
  131.9 19.9 %collective-permute-start.36 = (bf16[352,128]{1,0:T(8,128)(2,1)S(1)}, bf16[352,128]{1,0:T(8,128)(2,1)S(1)}, u32[]{:S(2)}, u32[]{:S(2)}) collective-permute-start(bf16[352,128]{1,0:T(8,128)(2,1)S(1)} %get-tuple-element.130), channel_id=1, source_target_pairs={{0,6},{1,7},{2,0},{3,1},{4,2},{5,3},{6,4},{7,5},{8,14},{9,15},{10,... | collective-permute-start | bytes 270344 | tf_op jit(solution)/shard_map/ppermute | solution.py:434
  134.5 14.4 %collective-permute-start.38 = (f32[4,512]{1,0:T(4,128)S(1)}, f32[4,512]{1,0:T(4,128)S(1)}, u32[]{:S(2)}, u32[]{:S(2)}) collective-permute-start(f32[4,512]{1,0:T(4,128)S(1)} %get-tuple-element.134), channel_id=1, source_target_pairs={{0,1},{1,0},{2,3},{3,2},{4,5},{5,4},{6,7},{7,6},{8,9},{9,8},{10,11... | collective-permute-start | bytes 24584 | tf_op jit(solution)/shard_map/ppermute | solution.py:426
  149.4 7.5 %collective-permute-start.39 = (f32[8,512]{1,0:T(8,128)S(1)}, f32[8,512]{1,0:T(8,128)S(1)}, u32[]{:S(2)}, u32[]{:S(2)}) collective-permute-start(f32[8,512]{1,0:T(8,128)S(1)} %shard_map.143), channel_id=1, source_target_pairs={{0,8},{8,16},{16,24},{24,0},{1,9},{9,17},{17,25},{25,1},{2,10},{10... | collective-permute-start | bytes 49160 | tf_op jit(solution)/shard_map/ppermute | solution.py:587
  149.5 7.5 %collective-permute-start.40 = (f32[8,512]{1,0:T(8,128)S(1)}, f32[8,512]{1,0:T(8,128)S(1)}, u32[]{:S(2)}, u32[]{:S(2)}) collective-permute-start(f32[8,512]{1,0:T(8,128)S(1)} %shard_map.143), channel_id=1, source_target_pairs={{0,16},{8,24},{16,0},{24,8},{1,17},{9,25},{17,1},{25,9},{2,18},{10... | collective-permute-start | bytes 49160 | tf_op jit(solution)/shard_map/ppermute | solution.py:587
  151.5 5.5 %collective-permute-start.41 = (f32[8,512]{1,0:T(8,128)S(1)}, f32[8,512]{1,0:T(8,128)S(1)}, u32[]{:S(2)}, u32[]{:S(2)}) collective-permute-start(f32[8,512]{1,0:T(8,128)S(1)} %shard_map.143), channel_id=1, source_target_pairs={{0,24},{8,0},{16,8},{24,16},{1,25},{9,1},{17,9},{25,17},{2,26},{10... | collective-permute-start | bytes 49160 | tf_op jit(solution)/shard_map/ppermute | solution.py:587
  (20 other events, 132.8 us)
where the time goes:
time: 161 us
  starting transfers between devices  69.3 us (43%)
  Pallas kernels  45 us (28%)
  waiting for transfers between devices  31.1 us (19%)
  local copies, waits for them, and re-layouts  8.67 us (5%)
  between operations  3.7 us (2%)
  other arithmetic  2.89 us (2%)
    ppermute x24, starting transfers between devices, around(): return lax.ppermute(x, 'patch', pairs)  29.1 us
    pallas_call x6, Pallas kernels, conv(): call(functools.partial(conv_kernel, index, base is not None, last), (wide...  26.8 us
    ppermute x24, waiting for transfers between devices, around(): return lax.ppermute(x, 'patch', pairs)  26 us
    ppermute x4, starting transfers between devices, swap(): return lax.ppermute(x, 'patch', swap_pairs)  15.3 us
    pallas_call x2, Pallas kernels, per_device(): call(functools.partial(first_kernel, first_step, chips), (wide_shape, hal...  13.6 us
    ppermute x4, starting transfers between devices, onward(): return lax.ppermute(x, joint, pairs)  12.7 us
    ppermute x8, starting transfers between devices, to_first(): return lax.ppermute(x, joint, pairs)  11.7 us
    unnamed x20, local copies, waits for them, and re-layouts  4.67 us
  transfers between devices with their start and end apart: 43, of which 13 were waited for; matrix products, arithmetic and copies ran while one was open for 2% of the time, Pallas kernels for 6%

commit v1 on v0

--- a/solution.py
+++ b/solution.py
@@ -2,6 +2,7 @@
 
 import jax
 import jax.numpy as jnp
+import numpy as np
 from jax import lax
 from jax.experimental import pallas as pl
 from jax.experimental.pallas import tpu as pltpu
@@ -41,9 +42,12 @@
     return hi, mid, lo
 
 
+def group_lanes(x, gather):
+    return dot(gather, jnp.concatenate(split3(x)[:2], axis=0))
+
+
 def group_sum(x, gather):
-    parts = jnp.concatenate(split3(x), axis=0)
-    return jnp.sum(dot(gather, parts), axis=1, keepdims=True)
+    return jnp.sum(group_lanes(x, gather), axis=1, keepdims=True)
 
 
 def expand(x, spread):
@@ -72,7 +76,7 @@
 
 
 def finish_stats(pivot, sums, gather, count):
-    wide = dot(gather, jnp.concatenate(split3(jnp.concatenate(sums, axis=1)), axis=0))
+    wide = group_lanes(jnp.concatenate(sums, axis=1), gather)
     first = jnp.sum(wide[:, :128], axis=1, keepdims=True)
     second = jnp.sum(wide[:, 128:], axis=1, keepdims=True)
     return pivot + first / count, jnp.maximum(second - first * first / count, 0.0)
@@ -154,7 +158,7 @@
 CHUNK = 4
 
 
-def conv_all(tiles, moments, flags, patches, weight, store, gather, spread):
+def conv_all(tiles, moments, flags, patches, weight, store, gather=None, spread=None):
     rows = len(tiles) - 2
     chans = weight.shape[0]
     filled = 0
@@ -165,10 +169,14 @@
             fill_row(filled, rows + 1, tiles[filled](), moments, flags, patches)
             filled += 1
         kept = store(start, CHUNK, conv_rows(patches, weight, start, CHUNK))
+        if gather is None:
+            continue
         kept = [kept[:, r * 128 : (r + 1) * 128] for r in range(CHUNK)]
         if start == 0:
             pivot, center = pivot_of(kept, gather, spread, per_row)
         sums = add_deviations(sums, kept, center)
+    if gather is None:
+        return None
     return encode_stats(*finish_stats(pivot, sums, gather, per_row * rows))
 
 
@@ -180,17 +188,19 @@
         ref[pl.ds(chans, GROUPS), :] = stats
 
 
-def pack_kernel(first, second, *outs):
-    chans = first.shape[3]
+def pack_kernel(block, taps_in, out, taps, sem):
+    copy = pltpu.make_async_copy(taps_in.at[0, block], taps, sem)
+    copy.start()
+    copy.wait()
+    chans = taps.shape[1]
     main = chans // 128 * 128
     tail = chans - main
-    for n in range(4):
-        pieces = []
-        for t in range(9):
-            tap = (first, second)[n % 2][0, n // 2, t]
-            outs[n][:, pl.ds(t * main, main)] = tap[:, :main]
-            pieces.append(tap[:, main:])
-        outs[n][:, pl.ds(9 * main, 9 * tail)] = jnp.concatenate(pieces, axis=1)
+    pieces = []
+    for t in range(9):
+        tap = taps[t]
+        out[:, pl.ds(t * main, main)] = tap[:, :main]
+        pieces.append(tap[:, main:])
+    out[:, pl.ds(9 * main, 9 * tail)] = jnp.concatenate(pieces, axis=1)
 
 
 def count_of(chans, cells):
@@ -228,8 +238,8 @@
     return combine_stats(messages + [ref[...] for ref in others], count)
 
 
-def head_kernel(params, own, up, down, weight, spread, *rest):
-    others, (out, forward) = rest[:-2], rest[-2:]
+def head_kernel(early, params, own, up, down, weight, spread, *rest):
+    others, (out, forward) = rest[: len(rest) - 2 - early], rest[-2:]
     latent = None
     if out.shape[0] == 8:
         others, latent = others[:-1], others[-1]
@@ -347,7 +357,10 @@
     rest = list(rest)
     base = rest.pop(0) if residual else None
     patches = rest.pop()
-    others, (out, top_msg, bot_msg, st_msg) = rest[:-4], rest[-4:]
+    final = last == "final"
+    given = 1 if final else 4
+    others, outs = rest[:-given], rest[-given:]
+    out = outs[0]
     chans, cells = own.shape
     rows = cells // 128
     mean, root = gathered(up, down, others, count_of(chans, cells))
@@ -367,10 +380,10 @@
         out[:, lanes] = acc.astype(out.dtype)
         return acc
 
-    stats_out = conv_all(
-        tiles, known, (ints[0], ints[1]), patches, weight, store, gather[...], spread[...]
-    )
-    write_messages(out, stats_out, top_msg, bot_msg, st_msg)
+    sums = () if final else (gather[...], spread[...])
+    stats_out = conv_all(tiles, known, (ints[0], ints[1]), patches, weight, store, *sums)
+    if not final:
+        write_messages(out, stats_out, *outs[1:])
 
 
 VM = pl.BlockSpec(memory_space=pltpu.VMEM)
@@ -425,49 +438,56 @@
     def swap(x):
         return lax.ppermute(x, "patch", swap_pairs)
 
-    def around(x, by):
+    def by_core(m, l):
+        return CORES * (l % chips) + m
+
+    def by_chips(m, l):
+        return m * chips + ((l % chips) ^ ((l % chips) >> 1))
+
+    blocks = [(m, l) for m in range(CORES) for l in range(chips)]
+
+    def around(layout, x, by):
+        return lax.ppermute(x, "patch", [(layout(m, l), layout(m, l + by)) for m, l in blocks])
+
+    def onward(source, target, x):
         pairs = [
-            (CORES * z + c, CORES * ((z + by) % chips) + c)
-            for z in range(chips)
-            for c in range(CORES)
-        ]
-        return lax.ppermute(x, "patch", pairs)
-
-    def device(s, z, c):
-        return s * patches + CORES * (z % chips) + c
-
-    def every(shift_section):
-        return [
-            (s, z, c) for s in shift_section for z in range(chips) for c in range(CORES)
-        ]
-
-    def onward(x):
-        pairs = [(device(s, z, c), device(s + 1, z, c)) for s, z, c in every(range(sections - 1))]
-        return lax.ppermute(x, joint, pairs)
-
-    def to_first(x, by):
-        pairs = [
-            (device(s, z, c), device((s + 1) % sections, z + by, c))
-            for s, z, c in every(range(sections))
+            (s * patches + source(m, l), (s + 1) % sections * patches + target(m, l))
+            for s in range(sections)
+            for m, l in blocks
         ]
         return lax.ppermute(x, joint, pairs)
 
-    group_of = jnp.arange(chans) // (chans // GROUPS)
-    member = (jnp.arange(GROUPS)[:, None] == group_of[None, :]).astype(BF16)
-    gather = jnp.tile(member, (1, 3))
-    spread = jnp.tile(member.T, (1, 3))
+    def to_first(source, target, x, by):
+        pairs = [
+            (s * patches + source(m, l), (s + 1) % sections * patches + target(m, l + by))
+            for s in range(sections)
+            for m, l in blocks
+        ]
+        return lax.ppermute(x, joint, pairs)
+
+    group_of = np.arange(chans) // (chans // GROUPS)
+    member = (np.arange(GROUPS)[:, None] == group_of[None, :]).astype(np.float32)
+    gather = jnp.asarray(np.tile(member, (1, 2)), BF16)
+    spread = jnp.asarray(np.tile(member.T, (1, 3)), BF16)
 
     lat = latent.shape[1]
-    ints = jnp.stack(
-        [
-            (place > 0).astype(jnp.int32),
-            (place < chips - 1).astype(jnp.int32),
-            section.astype(jnp.int32),
-            place.astype(jnp.int32),
-            blocks_used[0],
-            core.astype(jnp.int32),
-        ]
-    )
+    group, rank = lax.axis_index("patch") // chips, lax.rem(lax.axis_index("patch"), chips)
+    turn = 1
+    while turn < chips:
+        rank = rank ^ (rank >> turn)
+        turn *= 2
+
+    def describe(row_block):
+        return jnp.stack(
+            [
+                (row_block > 0).astype(jnp.int32),
+                (row_block < chips - 1).astype(jnp.int32),
+                section.astype(jnp.int32),
+                row_block.astype(jnp.int32),
+                blocks_used[0],
+                core.astype(jnp.int32),
+            ]
+        )
 
     def pick(x, which):
         return lax.dynamic_index_in_dim(x, which, 0, keepdims=False)
@@ -489,17 +509,25 @@
         enter_kernel, (rows_shape, rows_shape, stats_shape), [VM] * 3, [], 10_000_000
     )(own, gather, spread)
 
-    conv1_w, conv2_w, norm_gain, norm_shift, in_w, head_w, latent, _ = lax.optimization_barrier(
-        (conv1_w, conv2_w, norm_gain, norm_shift, in_w, head_w, latent, messages[2])
-    )
+    given = (conv1_w, conv2_w, norm_gain, norm_shift, in_w, head_w, head_gain, head_shift)
+    *given, latent, plan_pos, _ = lax.optimization_barrier((*given, latent, plan_pos, messages[2]))
+    conv1_w, conv2_w, norm_gain, norm_shift, in_w, head_w, head_gain, head_shift = given
     params = jnp.stack(
         [x[0, k, q] for k in range(2) for q in range(2) for x in (norm_gain, norm_shift)]
         + [head_gain, head_shift]
         + [jnp.zeros((chans,), F32)] * 6
     ).T
-    kernels = call(
-        pack_kernel, (sds((chans, 9 * chans), BF16),) * 4, [VM, VM], [], 10_000_000
-    )(conv1_w, conv2_w)
+    kernels = [
+        call(
+            functools.partial(pack_kernel, block),
+            sds((chans, 9 * chans), BF16),
+            [HB],
+            [pltpu.VMEM(taps.shape[2:], BF16), pltpu.SemaphoreType.DMA(())],
+            10_000_000,
+        )(taps)
+        for block in range(2)
+        for taps in (conv1_w, conv2_w)
+    ]
     head_packed = jnp.zeros((3, 3, 8, chans), BF16)
     head_packed = head_packed.at[:, :, :lat].set(
         jnp.transpose(head_w.reshape(3, 3, lat, chans), (1, 0, 2, 3))
@@ -514,35 +542,44 @@
         [jnp.where(core == 0, mine, other), jnp.where(core == 0, other, mine)], axis=1
     ).reshape(lat, cells)
     latent_rows = jnp.concatenate([jnp.zeros((8 - lat, cells), F32), latent_rows], axis=0)
-    position = pick(plan_pos, core)
-    sigmas = [sigma_at(position + step) for step in range(STEPS + 1)]
-    floats = [
-        jnp.stack([sigmas[step + 1] - sigmas[step], jnp.sqrt(sigmas[step + 1] ** 2 + 1.0)])
-        for step in range(STEPS)
-    ]
+    layouts = (by_core,) * (STEPS + 1)
+    described = {by_core: describe(place), by_chips: describe(rank)}
+    floats = []
+    for step in range(STEPS):
+        position = pick(plan_pos, core if layouts[step + 1] is by_core else group) + step
+        now, later = sigma_at(position), sigma_at(position + 1)
+        floats.append(jnp.stack([later - now, jnp.sqrt(later * later + 1.0)]))
     full_latent = None
 
-    def exchange(top_msg, bot_msg, st_msg):
-        up = around(bot_msg, 1)
-        down = around(top_msg, chips - 1)
-        return up, down, [st_msg] + [around(st_msg, d) for d in range(2, chips - 1)]
+    def exchange(layout, top_msg, bot_msg, st_msg):
+        up = around(layout, bot_msg, 1)
+        down = around(layout, top_msg, chips - 1)
+        return up, down, [st_msg] + [around(layout, st_msg, d) for d in range(2, chips - 1)]
 
     for step in range(STEPS):
         first_step = step == 0
-        own_next = onward(own)
-        up, down, others = exchange(*messages)
+        before, layout = layouts[step], layouts[step + 1]
+        ints = described[layout]
+        own_next = onward(before, layout, own)
+        up, down, others = exchange(before, *messages)
         height = 8 if first_step else lat
         extra = [latent_rows] if first_step else []
+        early = []
         noise, forward = call(
-            head_kernel,
+            functools.partial(head_kernel, len(early)),
             (sds((height, cells + 256), F32), sds((chans + GROUPS, 256), BF16)),
-            [VM] * (6 + len(others) + len(extra)),
+            [VM] * (6 + len(others) + len(extra)) + [HB] * len(early),
             [],
             300_000_000,
-        )(params, own, up, down, head_packed, spread, *others, *extra)
-        parts = [to_first(noise, d) for d in range(chips)]
-        forward_next = onward(forward)
-        extra = [] if first_step else [full_latent]
+        )(params, own, up, down, head_packed, spread, *others, *extra, *early)
+        parts = [to_first(before, layout, noise, d) for d in range(chips)]
+        forward_next = onward(before, layout, forward)
+        extra = []
+        if not first_step:
+            extra = [full_latent]
+            if before is not layout:
+                moves = [(before(m, l), layout(m, l)) for m, l in blocks]
+                extra = [lax.ppermute(full_latent, "patch", moves)]
         middle, source, full_latent, lat_keep, lat_send, *messages = call(
             functools.partial(first_kernel, first_step, chips),
             (
@@ -591,11 +628,15 @@
             ]
 
         def conv(index, own, messages, base, last=False):
-            up, down, others = exchange(*messages)
+            up, down, others = exchange(layout, *messages)
             extra = [] if base is None else [base]
             return call(
                 functools.partial(conv_kernel, index, base is not None, last),
-                (wide_shape if base is None else half_shape, rows_shape, rows_shape, stats_shape),
+                (
+                    (half_shape,)
+                    if last == "final"
+                    else (wide_shape if base is None else half_shape, rows_shape, rows_shape, stats_shape)
+                ),
                 [SM] + [VM] * (7 + len(extra) + len(others)),
                 conv_scratch,
                 conv_flops,
@@ -603,7 +644,9 @@
 
         one, *messages = conv(1, middle, messages, source)
         middle, *messages = conv(2, one, messages, None)
-        own, *messages = conv(3, middle, messages, one, True)
+        own, *messages = conv(
+            3, middle, messages, one, "final" if step == STEPS - 1 else "last"
+        )
 
     own, *shares = lax.optimization_barrier((own, *shares))
     low, high = own[:, :half], own[:, half:]

time: 161 us -> 153 us (0.950)
  starting transfers between devices: 69.3 us -> 61.7 us
  local copies, waits for them, and re-layouts: 8.67 us -> 4.87 us
  waiting for transfers between devices: 31.1 us -> 34.1 us
    ppermute x4, starting transfers between devices: 12.7 us -> 3.78 us  [onward(): return lax.ppermute(x, joint, pairs)]
    unnamed x20 -> x32, local copies, waits for them, and re-layouts: 4.67 us -> 2.46 us
    ppermute x8, waiting for transfers between devices: 3.85 us -> 5.84 us  [to_first(): return lax.ppermute(x, joint, pairs)]
    pallas_call x9 -> x12, Pallas kernels: 29.9 us -> 29.5 us  [the longest x6 25 us: conv(): call(functools.partial(conv_kernel, index, base is not None, last), (half...]
  transfers between devices with their start and end apart: 43 -> 43, of which waited for: 13 -> 15; matrix products, arithmetic and copies ran while one was open for 2% -> 1% of each run, Pallas kernels for 6% -> 6%
where the time goes in v1:
time: 153 us
  starting transfers between devices  61.7 us (40%)
  Pallas kernels  44.2 us (29%)
  waiting for transfers between devices  34.1 us (22%)
  local copies, waits for them, and re-layouts  4.87 us (3%)
  between operations  4.13 us (3%)
  other arithmetic  3.83 us (3%)
    ppermute x24, starting transfers between devices, around(): lax.ppermute(x, 'patch', [(layout(m, l), layout(m, l + by)) for m, l in b...  29.6 us
    ppermute x24, waiting for transfers between devices, around(): lax.ppermute(x, 'patch', [(layout(m, l), layout(m, l + by)) for m, l in b...  25.4 us
    pallas_call x6, Pallas kernels, conv(): call(functools.partial(conv_kernel, index, base is not None, last), (half...  25 us
    ppermute x4, starting transfers between devices, swap(): return lax.ppermute(x, 'patch', swap_pairs)  14.6 us
    pallas_call x2, Pallas kernels, per_device(): call(functools.partial(first_kernel, first_step, chips), (wide_shape, hal...  13.3 us
    ppermute x8, starting transfers between devices, to_first(): return lax.ppermute(x, joint, pairs)  13.1 us
    ppermute x8, waiting for transfers between devices, to_first(): return lax.ppermute(x, joint, pairs)  5.84 us
    ppermute x4, starting transfers between devices, onward(): return lax.ppermute(x, joint, pairs)  3.78 us
  transfers between devices with their start and end apart: 43, of which 15 were waited for; matrix products, arithmetic and copies ran while one was open for 1% of the time, Pallas kernels for 6%

profile of v1, /device:TPU:1, one launch (start us, length us, event | category | flops | bytes accessed | tf_op | source)
XLA Modules:
  0.0 152.8 jit_solution(9979299785112811377)
XLA Ops:
  5.3 2.4 %collective-permute-start.9 = (bf16[320,1024]{1,0:T(8,128)(2,1)S(1)}, bf16[320,1024]{1,0:T(8,128)(2,1)S(1)}, u32[]{:S(2)}, u32[]{:S(2)}) collective-permute-start(bf16[320,1024]{1,0:T(8,128)(2,1)S(1)} %bitcast.54), channel_id=1, source_target_pairs={{0,8},{2,10},{4,12},{6,14},{1,9},{3,11},{5,13},{7,15},{8,16},{10,1... | collective-permute-start | bytes 1966088 | tf_op jit(solution)/shard_map/ppermute | solution.py:458
  8.5 2.4 %collective-permute-start.3 = (bf16[32,128]{1,0:T(8,128)(2,1)S(1)}, bf16[32,128]{1,0:T(8,128)(2,1)S(1)}, u32[]{:S(2)}, u32[]{:S(2)}) collective-permute-start(bf16[32,128]{1,0:T(8,128)(2,1)S(1)} %get-tuple-element.81.rest_0_), channel_id=1, source_target_pairs={{0,4},{2,6},{4,0},{6,2},{1,5},{3,7},{5,1},{7,3},{8,12},{10,14},{12... | collective-permute-start | bytes 24584 | tf_op jit(solution)/shard_map/ppermute | solution.py:450
  15.5 2.7 %collective-permute-done.1.up = bf16[352,128]{1,0:T(8,128)(2,1)S(1)} collective-permute-done((bf16[352,128]{1,0:T(8,128)(2,1)S(1)}, bf16[352,128]{1,0:T(8,128)(2,1)S(1)}, u32[]{:S(2)}, u32[]{:S(2)}) %collective-permute-start.1) | collective-permute-done | bytes 90144 | tf_op jit(solution)/shard_map/ppermute | solution.py:450
  26.1 2.7 %collective-permute-start.7 = (f32[8,1280]{1,0:T(8,128)S(1)}, f32[8,1280]{1,0:T(8,128)S(1)}, u32[]{:S(2)}, u32[]{:S(2)}) collective-permute-start(f32[8,1280]{1,0:T(8,128)S(1)} %get-tuple-element.91), channel_id=1, source_target_pairs={{0,12},{2,14},{4,8},{6,10},{1,13},{3,15},{5,9},{7,11},{8,20},{10,2... | collective-permute-start | bytes 122888 | tf_op jit(solution)/shard_map/ppermute | solution.py:466
  28.8 3.0 %collective-permute-start.8 = (f32[8,1280]{1,0:T(8,128)S(1)}, f32[8,1280]{1,0:T(8,128)S(1)}, u32[]{:S(2)}, u32[]{:S(2)}) collective-permute-start(f32[8,1280]{1,0:T(8,128)S(1)} %get-tuple-element.91), channel_id=1, source_target_pairs={{0,14},{2,8},{4,10},{6,12},{1,15},{3,9},{5,11},{7,13},{8,22},{10,1... | collective-permute-start | bytes 122888 | tf_op jit(solution)/shard_map/ppermute | solution.py:466
  32.1 2.3 %copy-done = bf16[1,2,9,320,320]{4,3,2,1,0:T(8,128)(2,1)S(1)} copy-done((bf16[1,2,9,320,320]{4,3,2,1,0:T(8,128)(2,1)S(1)}, bf16[1,2,9,320,320]{4,3,2,1,0:T(8,128)(2,1)}, u32[]{:S(2)}) %copy-start) | copy-done | bytes 3686424
  35.0 6.6 %shard_map.152 = (f32[320,1024]{1,0:T(8,128)S(1)}, bf16[320,1024]{1,0:T(8,128)(2,1)S(1)}, f32[8,4096]{1,0:T(8,128)S(1)}, f32[4,512]{1,0:T(4,128)}, f32[4,512]{1,...) custom-call(s32[6]{0:T(128)S(1)} %stack.78.ints, ...), custom_call_target="tpu_custom_call" | custom-call | flops 1887436800 | bytes 4000000 | tf_op jit(solution)/shard_map/pallas_call | solution.py:583
  42.4 2.4 %collective-permute-start.12 = (bf16[352,128]{1,0:T(8,128)(2,1)S(1)}, bf16[352,128]{1,0:T(8,128)(2,1)S(1)}, u32[]{:S(2)}, u32[]{:S(2)}) collective-permute-start(bf16[352,128]{1,0:T(8,128)(2,1)S(1)} %get-tuple-element.97), channel_id=1, source_target_pairs={{0,6},{2,0},{4,2},{6,4},{1,7},{3,1},{5,3},{7,5},{8,14},{10,8},{12,... | collective-permute-start | bytes 270344 | tf_op jit(solution)/shard_map/ppermute | solution.py:450
  45.4 4.0 %collective-permute-done.13.rest_2_ = bf16[32,128]{1,0:T(8,128)(2,1)S(1)} collective-permute-done((bf16[32,128]{1,0:T(8,128)(2,1)S(1)}, bf16[32,128]{1,0:T(8,128)(2,1)S(1)}, u32[]{:S(2)}, u32[]{:S(2)}) %collective-permute-start.13) | collective-permute-done | bytes 8224 | tf_op jit(solution)/shard_map/ppermute | solution.py:450
  49.4 4.3 %shard_map.154 = (bf16[320,1024]{1,0:T(8,128)(2,1)S(1)}, bf16[352,128]{1,0:T(8,128)(2,1)S(1)}, bf16[352,128]{1,0:T(8,128)(2,1)S(1)}, bf16[32,128]{1,0:T(8,128)(2,1)S(1)}) custom-call(s32[6]{0:T(128)S(1)} %stack.78.ints, f32[320,16]{1,0:T(8,128)S(1)} %bitcast.59, f32[320,1024]{1,0:T(8,128)S(1)} %get-tuple-element.95.own, ...), custom_call_target="tpu_custom_call" | custom-call | flops 1887436800 | bytes 4000000 | tf_op jit(solution)/shard_map/pallas_call | solution.py:633
  53.9 3.3 %collective-permute-start.15 = (bf16[352,128]{1,0:T(8,128)(2,1)S(1)}, bf16[352,128]{1,0:T(8,128)(2,1)S(1)}, u32[]{:S(2)}, u32[]{:S(2)}) collective-permute-start(bf16[352,128]{1,0:T(8,128)(2,1)S(1)} %get-tuple-element.103), channel_id=1, source_target_pairs={{0,6},{2,0},{4,2},{6,4},{1,7},{3,1},{5,3},{7,5},{8,14},{10,8},{12,... | collective-permute-start | bytes 270344 | tf_op jit(solution)/shard_map/ppermute | solution.py:450
  57.8 2.9 %collective-permute-done.16.rest_1_ = bf16[32,128]{1,0:T(8,128)(2,1)S(1)} collective-permute-done((bf16[32,128]{1,0:T(8,128)(2,1)S(1)}, bf16[32,128]{1,0:T(8,128)(2,1)S(1)}, u32[]{:S(2)}, u32[]{:S(2)}) %collective-permute-start.16) | collective-permute-done | bytes 8224 | tf_op jit(solution)/shard_map/ppermute | solution.py:450
  60.7 4.2 %shard_map.156 = (f32[320,1024]{1,0:T(8,128)S(1)}, bf16[352,128]{1,0:T(8,128)(2,1)S(1)}, bf16[352,128]{1,0:T(8,128)(2,1)S(1)}, bf16[32,128]{1,0:T(8,128)(2,1)S(1)}) custom-call(s32[6]{0:T(128)S(1)} %stack.78.ints, f32[320,16]{1,0:T(8,128)S(1)} %bitcast.60, bf16[320,1024]{1,0:T(8,128)(2,1)S(1)} %get-tuple-element.101.own.rest_0_, ...), custom_call_target="tpu_custom_call" | custom-call | flops 1887436800 | bytes 4000000 | tf_op jit(solution)/shard_map/pallas_call | solution.py:633
  64.9 3.3 %collective-permute-start.18 = (bf16[352,128]{1,0:T(8,128)(2,1)S(1)}, bf16[352,128]{1,0:T(8,128)(2,1)S(1)}, u32[]{:S(2)}, u32[]{:S(2)}) collective-permute-start(bf16[352,128]{1,0:T(8,128)(2,1)S(1)} %get-tuple-element.107), channel_id=1, source_target_pairs={{0,6},{2,0},{4,2},{6,4},{1,7},{3,1},{5,3},{7,5},{8,14},{10,8},{12,... | collective-permute-start | bytes 270344 | tf_op jit(solution)/shard_map/ppermute | solution.py:450
  68.7 2.8 %collective-permute-done.19.rest_2_ = bf16[32,128]{1,0:T(8,128)(2,1)S(1)} collective-permute-done((bf16[32,128]{1,0:T(8,128)(2,1)S(1)}, bf16[32,128]{1,0:T(8,128)(2,1)S(1)}, u32[]{:S(2)}, u32[]{:S(2)}) %collective-permute-start.19) | collective-permute-done | bytes 8224 | tf_op jit(solution)/shard_map/ppermute | solution.py:450
  71.6 4.4 %shard_map.158 = (bf16[320,1024]{1,0:T(8,128)(2,1)S(1)}, bf16[352,128]{1,0:T(8,128)(2,1)S(1)}, bf16[352,128]{1,0:T(8,128)(2,1)S(1)}, bf16[32,128]{1,0:T(8,128)(2,1)S(1)}) custom-call(s32[6]{0:T(128)S(1)} %stack.78.ints, f32[320,16]{1,0:T(8,128)S(1)} %bitcast.61, f32[320,1024]{1,0:T(8,128)S(1)} %get-tuple-element.105.own, ...), custom_call_target="tpu_custom_call" | custom-call | flops 1887436800 | bytes 4000000 | tf_op jit(solution)/shard_map/pallas_call | solution.py:633
  76.1 3.3 %collective-permute-start.21 = (bf16[352,128]{1,0:T(8,128)(2,1)S(1)}, bf16[352,128]{1,0:T(8,128)(2,1)S(1)}, u32[]{:S(2)}, u32[]{:S(2)}) collective-permute-start(bf16[352,128]{1,0:T(8,128)(2,1)S(1)} %get-tuple-element.111), channel_id=1, source_target_pairs={{0,6},{2,0},{4,2},{6,4},{1,7},{3,1},{5,3},{7,5},{8,14},{10,8},{12,... | collective-permute-start | bytes 270344 | tf_op jit(solution)/shard_map/ppermute | solution.py:450
  79.4 3.4 %collective-permute-done.22.rest_1_ = bf16[32,128]{1,0:T(8,128)(2,1)S(1)} collective-permute-done((bf16[32,128]{1,0:T(8,128)(2,1)S(1)}, bf16[32,128]{1,0:T(8,128)(2,1)S(1)}, u32[]{:S(2)}, u32[]{:S(2)}) %collective-permute-start.22) | collective-permute-done | bytes 8224 | tf_op jit(solution)/shard_map/ppermute | solution.py:450
  85.3 2.8 %collective-permute-start.24 = (f32[4,1280]{1,0:T(4,128)S(1)}, f32[4,1280]{1,0:T(4,128)S(1)}, u32[]{:S(2)}, u32[]{:S(2)}) collective-permute-start(f32[4,1280]{1,0:T(4,128)S(1)} %get-tuple-element.113), channel_id=1, source_target_pairs={{0,10},{2,12},{4,14},{6,8},{1,11},{3,13},{5,15},{7,9},{8,18},{10,2... | collective-permute-start | bytes 61448 | tf_op jit(solution)/shard_map/ppermute | solution.py:466
  88.1 2.0 %collective-permute-start.25 = (f32[4,1280]{1,0:T(4,128)S(1)}, f32[4,1280]{1,0:T(4,128)S(1)}, u32[]{:S(2)}, u32[]{:S(2)}) collective-permute-start(f32[4,1280]{1,0:T(4,128)S(1)} %get-tuple-element.113), channel_id=1, source_target_pairs={{0,12},{2,14},{4,8},{6,10},{1,13},{3,15},{5,9},{7,11},{8,20},{10,2... | collective-permute-start | bytes 61448 | tf_op jit(solution)/shard_map/ppermute | solution.py:466
  90.1 2.0 %collective-permute-done.23.rest_0_ = f32[4,1280]{1,0:T(4,128)S(1)} collective-permute-done((f32[4,1280]{1,0:T(4,128)S(1)}, f32[4,1280]{1,0:T(4,128)S(1)}, u32[]{:S(2)}, u32[]{:S(2)}) %collective-permute-start.23) | collective-permute-done | bytes 20512 | tf_op jit(solution)/shard_map/ppermute | solution.py:466
  93.6 3.1 %collective-permute-done.26.rest_3_ = f32[4,1280]{1,0:T(4,128)S(1)} collective-permute-done((f32[4,1280]{1,0:T(4,128)S(1)}, f32[4,1280]{1,0:T(4,128)S(1)}, u32[]{:S(2)}, u32[]{:S(2)}) %collective-permute-start.26) | collective-permute-done | bytes 20512 | tf_op jit(solution)/shard_map/ppermute | solution.py:466
  96.7 6.7 %shard_map.160 = (f32[320,1024]{1,0:T(8,128)S(1)}, bf16[320,1024]{1,0:T(8,128)(2,1)S(1)}, f32[8,4096]{1,0:T(8,128)}, f32[4,512]{1,0:T(4,128)S(1)}, f32[4,512]{1,...) custom-call(s32[6]{0:T(128)S(1)} %stack.78.ints, ...), custom_call_target="tpu_custom_call" | custom-call | flops 1887436800 | bytes 4000000 | tf_op jit(solution)/shard_map/pallas_call | solution.py:583
  103.5 3.5 %collective-permute-start.30 = (bf16[352,128]{1,0:T(8,128)(2,1)S(1)}, bf16[352,128]{1,0:T(8,128)(2,1)S(1)}, u32[]{:S(2)}, u32[]{:S(2)}) collective-permute-start(bf16[352,128]{1,0:T(8,128)(2,1)S(1)} %get-tuple-element.118), channel_id=1, source_target_pairs={{0,6},{2,0},{4,2},{6,4},{1,7},{3,1},{5,3},{7,5},{8,14},{10,8},{12,... | collective-permute-start | bytes 270344 | tf_op jit(solution)/shard_map/ppermute | solution.py:450
  107.3 3.1 %collective-permute-done.31.rest_2_ = bf16[32,128]{1,0:T(8,128)(2,1)S(1)} collective-permute-done((bf16[32,128]{1,0:T(8,128)(2,1)S(1)}, bf16[32,128]{1,0:T(8,128)(2,1)S(1)}, u32[]{:S(2)}, u32[]{:S(2)}) %collective-permute-start.31) | collective-permute-done | bytes 8224 | tf_op jit(solution)/shard_map/ppermute | solution.py:450
  110.5 4.3 %shard_map.161 = (bf16[320,1024]{1,0:T(8,128)(2,1)S(1)}, bf16[352,128]{1,0:T(8,128)(2,1)S(1)}, bf16[352,128]{1,0:T(8,128)(2,1)S(1)}, bf16[32,128]{1,0:T(8,128)(2,1)S(1)}) custom-call(s32[6]{0:T(128)S(1)} %stack.78.ints, f32[320,16]{1,0:T(8,128)S(1)} %bitcast.64, f32[320,1024]{1,0:T(8,128)S(1)} %get-tuple-element.116.own, ...), custom_call_target="tpu_custom_call" | custom-call | flops 1887436800 | bytes 4000000 | tf_op jit(solution)/shard_map/pallas_call | solution.py:633
  115.2 2.9 %collective-permute-start.33 = (bf16[352,128]{1,0:T(8,128)(2,1)S(1)}, bf16[352,128]{1,0:T(8,128)(2,1)S(1)}, u32[]{:S(2)}, u32[]{:S(2)}) collective-permute-start(bf16[352,128]{1,0:T(8,128)(2,1)S(1)} %get-tuple-element.123), channel_id=1, source_target_pairs={{0,6},{2,0},{4,2},{6,4},{1,7},{3,1},{5,3},{7,5},{8,14},{10,8},{12,... | collective-permute-start | bytes 270344 | tf_op jit(solution)/shard_map/ppermute | solution.py:450
  118.1 3.4 %collective-permute-done.34.rest_1_ = bf16[32,128]{1,0:T(8,128)(2,1)S(1)} collective-permute-done((bf16[32,128]{1,0:T(8,128)(2,1)S(1)}, bf16[32,128]{1,0:T(8,128)(2,1)S(1)}, u32[]{:S(2)}, u32[]{:S(2)}) %collective-permute-start.34) | collective-permute-done | bytes 8224 | tf_op jit(solution)/shard_map/ppermute | solution.py:450
  121.5 4.2 %shard_map.162 = (f32[320,1024]{1,0:T(8,128)S(1)}, bf16[352,128]{1,0:T(8,128)(2,1)S(1)}, bf16[352,128]{1,0:T(8,128)(2,1)S(1)}, bf16[32,128]{1,0:T(8,128)(2,1)S(1)}) custom-call(s32[6]{0:T(128)S(1)} %stack.78.ints, f32[320,16]{1,0:T(8,128)S(1)} %bitcast.65, bf16[320,1024]{1,0:T(8,128)(2,1)S(1)} %get-tuple-element.121.own.rest_0_, ...), custom_call_target="tpu_custom_call" | custom-call | flops 1887436800 | bytes 4000000 | tf_op jit(solution)/shard_map/pallas_call | solution.py:633
  125.7 3.3 %collective-permute-start.36 = (bf16[352,128]{1,0:T(8,128)(2,1)S(1)}, bf16[352,128]{1,0:T(8,128)(2,1)S(1)}, u32[]{:S(2)}, u32[]{:S(2)}) collective-permute-start(bf16[352,128]{1,0:T(8,128)(2,1)S(1)} %get-tuple-element.127), channel_id=1, source_target_pairs={{0,6},{2,0},{4,2},{6,4},{1,7},{3,1},{5,3},{7,5},{8,14},{10,8},{12,... | collective-permute-start | bytes 270344 | tf_op jit(solution)/shard_map/ppermute | solution.py:450
  129.0 12.6 %collective-permute-start.38 = (f32[4,512]{1,0:T(4,128)S(1)}, f32[4,512]{1,0:T(4,128)S(1)}, u32[]{:S(2)}, u32[]{:S(2)}) collective-permute-start(f32[4,512]{1,0:T(4,128)S(1)} %get-tuple-element.130), channel_id=1, source_target_pairs={{0,1},{1,0},{2,3},{3,2},{4,5},{5,4},{6,7},{7,6},{8,9},{9,8},{10,11... | collective-permute-start | bytes 24584 | tf_op jit(solution)/shard_map/ppermute | solution.py:439
  145.4 3.7 %shard_map.163 = bf16[320,1024]{1,0:T(8,128)(2,1)S(1)} custom-call(s32[6]{0:T(128)S(1)} %stack.78.ints, f32[320,16]{1,0:T(8,128)S(1)} %bitcast.66, f32[320,1024]{1,0:T(8,128)S(1)} %get-tuple-element.125.own, bf16[352,128]{1,0:T(8,128)(2,1)S(1)} %collective-permute-done.35.up, bf16[352,128]{1,0:T(8,128)(2,1)S(1)} %collective-permute-done.36.down, ...), custom_call_target="tpu_custom_call" | custom-call | flops 1887436800 | bytes 4000000 | tf_op jit(solution)/shard_map/pallas_call | solution.py:633
  (135 shorter events, 30.9 us)
Async XLA Ops:
  5.3 29.7 %collective-permute-start.9 = (bf16[320,1024]{1,0:T(8,128)(2,1)S(1)}, bf16[320,1024]{1,0:T(8,128)(2,1)S(1)}, u32[]{:S(2)}, u32[]{:S(2)}) collective-permute-start(bf16[320,1024]{1,0:T(8,128)(2,1)S(1)} %bitcast.54), channel_id=1, source_target_pairs={{0,8},{2,10},{4,12},{6,14},{1,9},{3,11},{5,13},{7,15},{8,16},{10,1... | collective-permute-start | bytes 1966088 | tf_op jit(solution)/shard_map/ppermute | solution.py:458
  8.5 7.0 %collective-permute-start.3 = (bf16[32,128]{1,0:T(8,128)(2,1)S(1)}, bf16[32,128]{1,0:T(8,128)(2,1)S(1)}, u32[]{:S(2)}, u32[]{:S(2)}) collective-permute-start(bf16[32,128]{1,0:T(8,128)(2,1)S(1)} %get-tuple-element.81.rest_0_), channel_id=1, source_target_pairs={{0,4},{2,6},{4,0},{6,2},{1,5},{3,7},{5,1},{7,3},{8,12},{10,14},{12... | collective-permute-start | bytes 24584 | tf_op jit(solution)/shard_map/ppermute | solution.py:450
  12.1 6.1 %collective-permute-start.1 = (bf16[352,128]{1,0:T(8,128)(2,1)S(1)}, bf16[352,128]{1,0:T(8,128)(2,1)S(1)}, u32[]{:S(2)}, u32[]{:S(2)}) collective-permute-start(bf16[352,128]{1,0:T(8,128)(2,1)S(1)} %get-tuple-element.87), channel_id=1, source_target_pairs={{0,2},{2,4},{4,6},{6,0},{1,3},{3,5},{5,7},{7,1},{8,10},{10,12},{12... | collective-permute-start | bytes 270344 | tf_op jit(solution)/shard_map/ppermute | solution.py:450
  13.4 6.0 %collective-permute-start.2 = (bf16[352,128]{1,0:T(8,128)(2,1)S(1)}, bf16[352,128]{1,0:T(8,128)(2,1)S(1)}, u32[]{:S(2)}, u32[]{:S(2)}) collective-permute-start(bf16[352,128]{1,0:T(8,128)(2,1)S(1)} %get-tuple-element.88), channel_id=1, source_target_pairs={{0,6},{2,0},{4,2},{6,4},{1,7},{3,1},{5,3},{7,5},{8,14},{10,8},{12,... | collective-permute-start | bytes 270344 | tf_op jit(solution)/shard_map/ppermute | solution.py:450
  20.6 14.4 %collective-permute-start.10 = (bf16[352,256]{1,0:T(8,128)(2,1)S(1)}, bf16[352,256]{1,0:T(8,128)(2,1)S(1)}, u32[]{:S(2)}, u32[]{:S(2)}) collective-permute-start(bf16[352,256]{1,0:T(8,128)(2,1)S(1)} %get-tuple-element.93), channel_id=1, source_target_pairs={{0,8},{2,10},{4,12},{6,14},{1,9},{3,11},{5,13},{7,15},{8,16},{10,1... | collective-permute-start | bytes 540680 | tf_op jit(solution)/shard_map/ppermute | solution.py:458
  21.8 7.0 %collective-permute-start.5 = (f32[8,1280]{1,0:T(8,128)S(1)}, f32[8,1280]{1,0:T(8,128)S(1)}, u32[]{:S(2)}, u32[]{:S(2)}) collective-permute-start(f32[8,1280]{1,0:T(8,128)S(1)} %get-tuple-element.91), channel_id=1, source_target_pairs={{0,8},{2,10},{4,12},{6,14},{1,9},{3,11},{5,13},{7,15},{8,16},{10,1... | collective-permute-start | bytes 122888 | tf_op jit(solution)/shard_map/ppermute | solution.py:466
  25.9 9.0 %collective-permute-start.6 = (f32[8,1280]{1,0:T(8,128)S(1)}, f32[8,1280]{1,0:T(8,128)S(1)}, u32[]{:S(2)}, u32[]{:S(2)}) collective-permute-start(f32[8,1280]{1,0:T(8,128)S(1)} %get-tuple-element.91), channel_id=1, source_target_pairs={{0,10},{2,12},{4,14},{6,8},{1,11},{3,13},{5,15},{7,9},{8,18},{10,2... | collective-permute-start | bytes 122888 | tf_op jit(solution)/shard_map/ppermute | solution.py:466
  26.1 8.8 %collective-permute-start.7 = (f32[8,1280]{1,0:T(8,128)S(1)}, f32[8,1280]{1,0:T(8,128)S(1)}, u32[]{:S(2)}, u32[]{:S(2)}) collective-permute-start(f32[8,1280]{1,0:T(8,128)S(1)} %get-tuple-element.91), channel_id=1, source_target_pairs={{0,12},{2,14},{4,8},{6,10},{1,13},{3,15},{5,9},{7,11},{8,20},{10,2... | collective-permute-start | bytes 122888 | tf_op jit(solution)/shard_map/ppermute | solution.py:466
  28.8 6.1 %collective-permute-start.8 = (f32[8,1280]{1,0:T(8,128)S(1)}, f32[8,1280]{1,0:T(8,128)S(1)}, u32[]{:S(2)}, u32[]{:S(2)}) collective-permute-start(f32[8,1280]{1,0:T(8,128)S(1)} %get-tuple-element.91), channel_id=1, source_target_pairs={{0,14},{2,8},{4,10},{6,12},{1,15},{3,9},{5,11},{7,13},{8,22},{10,1... | collective-permute-start | bytes 122888 | tf_op jit(solution)/shard_map/ppermute | solution.py:466
  41.6 7.8 %collective-permute-start.11 = (bf16[352,128]{1,0:T(8,128)(2,1)S(1)}, bf16[352,128]{1,0:T(8,128)(2,1)S(1)}, u32[]{:S(2)}, u32[]{:S(2)}) collective-permute-start(bf16[352,128]{1,0:T(8,128)(2,1)S(1)} %get-tuple-element.96), channel_id=1, source_target_pairs={{0,2},{2,4},{4,6},{6,0},{1,3},{3,5},{5,7},{7,1},{8,10},{10,12},{12... | collective-permute-start | bytes 270344 | tf_op jit(solution)/shard_map/ppermute | solution.py:450
  42.4 7.0 %collective-permute-start.12 = (bf16[352,128]{1,0:T(8,128)(2,1)S(1)}, bf16[352,128]{1,0:T(8,128)(2,1)S(1)}, u32[]{:S(2)}, u32[]{:S(2)}) collective-permute-start(bf16[352,128]{1,0:T(8,128)(2,1)S(1)} %get-tuple-element.97), channel_id=1, source_target_pairs={{0,6},{2,0},{4,2},{6,4},{1,7},{3,1},{5,3},{7,5},{8,14},{10,8},{12,... | collective-permute-start | bytes 270344 | tf_op jit(solution)/shard_map/ppermute | solution.py:450
  44.8 4.6 %collective-permute-start.13 = (bf16[32,128]{1,0:T(8,128)(2,1)S(1)}, bf16[32,128]{1,0:T(8,128)(2,1)S(1)}, u32[]{:S(2)}, u32[]{:S(2)}) collective-permute-start(bf16[32,128]{1,0:T(8,128)(2,1)S(1)} %get-tuple-element.100.rest_1_), channel_id=1, source_target_pairs={{0,4},{2,6},{4,0},{6,2},{1,5},{3,7},{5,1},{7,3},{8,12},{10,14},{12... | collective-permute-start | bytes 24584 | tf_op jit(solution)/shard_map/ppermute | solution.py:450
  53.7 7.0 %collective-permute-start.14 = (bf16[352,128]{1,0:T(8,128)(2,1)S(1)}, bf16[352,128]{1,0:T(8,128)(2,1)S(1)}, u32[]{:S(2)}, u32[]{:S(2)}) collective-permute-start(bf16[352,128]{1,0:T(8,128)(2,1)S(1)} %get-tuple-element.102), channel_id=1, source_target_pairs={{0,2},{2,4},{4,6},{6,0},{1,3},{3,5},{5,7},{7,1},{8,10},{10,12},{12... | collective-permute-start | bytes 270344 | tf_op jit(solution)/shard_map/ppermute | solution.py:450
  53.9 6.7 %collective-permute-start.15 = (bf16[352,128]{1,0:T(8,128)(2,1)S(1)}, bf16[352,128]{1,0:T(8,128)(2,1)S(1)}, u32[]{:S(2)}, u32[]{:S(2)}) collective-permute-start(bf16[352,128]{1,0:T(8,128)(2,1)S(1)} %get-tuple-element.103), channel_id=1, source_target_pairs={{0,6},{2,0},{4,2},{6,4},{1,7},{3,1},{5,3},{7,5},{8,14},{10,8},{12,... | collective-permute-start | bytes 270344 | tf_op jit(solution)/shard_map/ppermute | solution.py:450
  64.8 6.7 %collective-permute-start.17 = (bf16[352,128]{1,0:T(8,128)(2,1)S(1)}, bf16[352,128]{1,0:T(8,128)(2,1)S(1)}, u32[]{:S(2)}, u32[]{:S(2)}) collective-permute-start(bf16[352,128]{1,0:T(8,128)(2,1)S(1)} %get-tuple-element.106), channel_id=1, source_target_pairs={{0,2},{2,4},{4,6},{6,0},{1,3},{3,5},{5,7},{7,1},{8,10},{10,12},{12... | collective-permute-start | bytes 270344 | tf_op jit(solution)/shard_map/ppermute | solution.py:450
  64.9 6.7 %collective-permute-start.18 = (bf16[352,128]{1,0:T(8,128)(2,1)S(1)}, bf16[352,128]{1,0:T(8,128)(2,1)S(1)}, u32[]{:S(2)}, u32[]{:S(2)}) collective-permute-start(bf16[352,128]{1,0:T(8,128)(2,1)S(1)} %get-tuple-element.107), channel_id=1, source_target_pairs={{0,6},{2,0},{4,2},{6,4},{1,7},{3,1},{5,3},{7,5},{8,14},{10,8},{12,... | collective-permute-start | bytes 270344 | tf_op jit(solution)/shard_map/ppermute | solution.py:450
  76.0 20.7 %collective-permute-start.27 = (bf16[320,1024]{1,0:T(8,128)(2,1)S(1)}, bf16[320,1024]{1,0:T(8,128)(2,1)S(1)}, u32[]{:S(2)}, u32[]{:S(2)}) collective-permute-start(bf16[320,1024]{1,0:T(8,128)(2,1)S(1)} %get-tuple-element.109.own), channel_id=1, source_target_pairs={{0,8},{2,10},{4,12},{6,14},{1,9},{3,11},{5,13},{7,15},{8,16},{10,1... | collective-permute-start | bytes 1966088 | tf_op jit(solution)/shard_map/ppermute | solution.py:458
  76.1 6.7 %collective-permute-start.20 = (bf16[352,128]{1,0:T(8,128)(2,1)S(1)}, bf16[352,128]{1,0:T(8,128)(2,1)S(1)}, u32[]{:S(2)}, u32[]{:S(2)}) collective-permute-start(bf16[352,128]{1,0:T(8,128)(2,1)S(1)} %get-tuple-element.110), channel_id=1, source_target_pairs={{0,2},{2,4},{4,6},{6,0},{1,3},{3,5},{5,7},{7,1},{8,10},{10,12},{12... | collective-permute-start | bytes 270344 | tf_op jit(solution)/shard_map/ppermute | solution.py:450
  76.1 6.7 %collective-permute-start.21 = (bf16[352,128]{1,0:T(8,128)(2,1)S(1)}, bf16[352,128]{1,0:T(8,128)(2,1)S(1)}, u32[]{:S(2)}, u32[]{:S(2)}) collective-permute-start(bf16[352,128]{1,0:T(8,128)(2,1)S(1)} %get-tuple-element.111), channel_id=1, source_target_pairs={{0,6},{2,0},{4,2},{6,4},{1,7},{3,1},{5,3},{7,5},{8,14},{10,8},{12,... | collective-permute-start | bytes 270344 | tf_op jit(solution)/shard_map/ppermute | solution.py:450
  83.9 12.8 %collective-permute-start.28 = (bf16[352,256]{1,0:T(8,128)(2,1)S(1)}, bf16[352,256]{1,0:T(8,128)(2,1)S(1)}, u32[]{:S(2)}, u32[]{:S(2)}) collective-permute-start(bf16[352,256]{1,0:T(8,128)(2,1)S(1)} %get-tuple-element.115), channel_id=1, source_target_pairs={{0,8},{2,10},{4,12},{6,14},{1,9},{3,11},{5,13},{7,15},{8,16},{10,1... | collective-permute-start | bytes 540680 | tf_op jit(solution)/shard_map/ppermute | solution.py:458
  84.0 8.2 %collective-permute-start.23 = (f32[4,1280]{1,0:T(4,128)S(1)}, f32[4,1280]{1,0:T(4,128)S(1)}, u32[]{:S(2)}, u32[]{:S(2)}) collective-permute-start(f32[4,1280]{1,0:T(4,128)S(1)} %get-tuple-element.113), channel_id=1, source_target_pairs={{0,8},{2,10},{4,12},{6,14},{1,9},{3,11},{5,13},{7,15},{8,16},{10,1... | collective-permute-start | bytes 61448 | tf_op jit(solution)/shard_map/ppermute | solution.py:466
  85.3 7.6 %collective-permute-start.24 = (f32[4,1280]{1,0:T(4,128)S(1)}, f32[4,1280]{1,0:T(4,128)S(1)}, u32[]{:S(2)}, u32[]{:S(2)}) collective-permute-start(f32[4,1280]{1,0:T(4,128)S(1)} %get-tuple-element.113), channel_id=1, source_target_pairs={{0,10},{2,12},{4,14},{6,8},{1,11},{3,13},{5,15},{7,9},{8,18},{10,2... | collective-permute-start | bytes 61448 | tf_op jit(solution)/shard_map/ppermute | solution.py:466
  88.1 5.4 %collective-permute-start.25 = (f32[4,1280]{1,0:T(4,128)S(1)}, f32[4,1280]{1,0:T(4,128)S(1)}, u32[]{:S(2)}, u32[]{:S(2)}) collective-permute-start(f32[4,1280]{1,0:T(4,128)S(1)} %get-tuple-element.113), channel_id=1, source_target_pairs={{0,12},{2,14},{4,8},{6,10},{1,13},{3,15},{5,9},{7,11},{8,20},{10,2... | collective-permute-start | bytes 61448 | tf_op jit(solution)/shard_map/ppermute | solution.py:466
  103.4 7.1 %collective-permute-start.29 = (bf16[352,128]{1,0:T(8,128)(2,1)S(1)}, bf16[352,128]{1,0:T(8,128)(2,1)S(1)}, u32[]{:S(2)}, u32[]{:S(2)}) collective-permute-start(bf16[352,128]{1,0:T(8,128)(2,1)S(1)} %get-tuple-element.117), channel_id=1, source_target_pairs={{0,2},{2,4},{4,6},{6,0},{1,3},{3,5},{5,7},{7,1},{8,10},{10,12},{12... | collective-permute-start | bytes 270344 | tf_op jit(solution)/shard_map/ppermute | solution.py:450
  103.5 6.9 %collective-permute-start.30 = (bf16[352,128]{1,0:T(8,128)(2,1)S(1)}, bf16[352,128]{1,0:T(8,128)(2,1)S(1)}, u32[]{:S(2)}, u32[]{:S(2)}) collective-permute-start(bf16[352,128]{1,0:T(8,128)(2,1)S(1)} %get-tuple-element.118), channel_id=1, source_target_pairs={{0,6},{2,0},{4,2},{6,4},{1,7},{3,1},{5,3},{7,5},{8,14},{10,8},{12,... | collective-permute-start | bytes 270344 | tf_op jit(solution)/shard_map/ppermute | solution.py:450
  114.8 6.7 %collective-permute-start.32 = (bf16[352,128]{1,0:T(8,128)(2,1)S(1)}, bf16[352,128]{1,0:T(8,128)(2,1)S(1)}, u32[]{:S(2)}, u32[]{:S(2)}) collective-permute-start(bf16[352,128]{1,0:T(8,128)(2,1)S(1)} %get-tuple-element.122), channel_id=1, source_target_pairs={{0,2},{2,4},{4,6},{6,0},{1,3},{3,5},{5,7},{7,1},{8,10},{10,12},{12... | collective-permute-start | bytes 270344 | tf_op jit(solution)/shard_map/ppermute | solution.py:450
  115.2 6.3 %collective-permute-start.33 = (bf16[352,128]{1,0:T(8,128)(2,1)S(1)}, bf16[352,128]{1,0:T(8,128)(2,1)S(1)}, u32[]{:S(2)}, u32[]{:S(2)}) collective-permute-start(bf16[352,128]{1,0:T(8,128)(2,1)S(1)} %get-tuple-element.123), channel_id=1, source_target_pairs={{0,6},{2,0},{4,2},{6,4},{1,7},{3,1},{5,3},{7,5},{8,14},{10,8},{12,... | collective-permute-start | bytes 270344 | tf_op jit(solution)/shard_map/ppermute | solution.py:450
  125.7 19.7 %collective-permute-start.35 = (bf16[352,128]{1,0:T(8,128)(2,1)S(1)}, bf16[352,128]{1,0:T(8,128)(2,1)S(1)}, u32[]{:S(2)}, u32[]{:S(2)}) collective-permute-start(bf16[352,128]{1,0:T(8,128)(2,1)S(1)} %get-tuple-element.126), channel_id=1, source_target_pairs={{0,2},{2,4},{4,6},{6,0},{1,3},{3,5},{5,7},{7,1},{8,10},{10,12},{12... | collective-permute-start | bytes 270344 | tf_op jit(solution)/shard_map/ppermute | solution.py:450
  125.7 19.6 %collective-permute-start.36 = (bf16[352,128]{1,0:T(8,128)(2,1)S(1)}, bf16[352,128]{1,0:T(8,128)(2,1)S(1)}, u32[]{:S(2)}, u32[]{:S(2)}) collective-permute-start(bf16[352,128]{1,0:T(8,128)(2,1)S(1)} %get-tuple-element.127), channel_id=1, source_target_pairs={{0,6},{2,0},{4,2},{6,4},{1,7},{3,1},{5,3},{7,5},{8,14},{10,8},{12,... | collective-permute-start | bytes 270344 | tf_op jit(solution)/shard_map/ppermute | solution.py:450
  129.0 13.4 %collective-permute-start.38 = (f32[4,512]{1,0:T(4,128)S(1)}, f32[4,512]{1,0:T(4,128)S(1)}, u32[]{:S(2)}, u32[]{:S(2)}) collective-permute-start(f32[4,512]{1,0:T(4,128)S(1)} %get-tuple-element.130), channel_id=1, source_target_pairs={{0,1},{1,0},{2,3},{3,2},{4,5},{5,4},{6,7},{7,6},{8,9},{9,8},{10,11... | collective-permute-start | bytes 24584 | tf_op jit(solution)/shard_map/ppermute | solution.py:439
  142.9 6.1 %collective-permute-start.39 = (f32[8,512]{1,0:T(8,128)S(1)}, f32[8,512]{1,0:T(8,128)S(1)}, u32[]{:S(2)}, u32[]{:S(2)}) collective-permute-start(f32[8,512]{1,0:T(8,128)S(1)} %shard_map.164), channel_id=1, source_target_pairs={{0,8},{8,16},{16,24},{24,0},{1,9},{9,17},{17,25},{25,1},{2,10},{10... | collective-permute-start | bytes 49160 | tf_op jit(solution)/shard_map/ppermute | solution.py:624
  143.0 6.1 %collective-permute-start.40 = (f32[8,512]{1,0:T(8,128)S(1)}, f32[8,512]{1,0:T(8,128)S(1)}, u32[]{:S(2)}, u32[]{:S(2)}) collective-permute-start(f32[8,512]{1,0:T(8,128)S(1)} %shard_map.164), channel_id=1, source_target_pairs={{0,16},{8,24},{16,0},{24,8},{1,17},{9,25},{17,1},{25,9},{2,18},{10... | collective-permute-start | bytes 49160 | tf_op jit(solution)/shard_map/ppermute | solution.py:624
  (26 other events, 204.8 us)

commit v2 on v1

--- a/solution.py
+++ b/solution.py
@@ -24,10 +24,12 @@
 
 
 def sigma_at(position):
-    fraction = position.astype(F32) / (SCHED - 1)
+    fraction = position / (SCHED - 1)
     top_root = sigma_top ** (1.0 / rho_power)
     low_root = sigma_low ** (1.0 / rho_power)
-    return (top_root + fraction * (low_root - top_root)) ** rho_power
+    base = top_root + fraction * (low_root - top_root)
+    square = base * base
+    return base * square * (square * square)
 
 
 def dot(a, b):
@@ -269,10 +271,16 @@
         if latent is not None and 0 <= r < rows:
             acc = acc + latent[:, pl.ds(r * 128, 128)]
         out[:, pl.ds((r + 1) * 128, 128)] = acc[: out.shape[0]]
-
-
-def first_kernel(first_step, chips, ints, floats, params, *rest):
-    parts, rest = rest[:chips], rest[chips:]
+        coded = [part.astype(F32) for part in split3(acc)] + [jnp.zeros((8, 128), F32)]
+        begin = chans + GROUPS + (r + 1) // 2 * 32
+        forward[pl.ds(begin, 32), pl.ds((r + 1) % 2 * 128, 128)] = jnp.concatenate(
+            coded, axis=0
+        ).astype(BF16)
+
+
+def first_kernel(step, chips, ints, plan, params, *rest):
+    first_step = step == 0
+    parts, rest = rest[: chips - 1], rest[chips - 1 :]
     if not first_step:
         latent_in, rest = rest[0], rest[1:]
     in_weight, own, forward, weight, gather, spread = rest[:6]
@@ -290,9 +298,19 @@
         for d in range(chips):
             owner = lax.rem(place - d + chips, chips)
             lanes = pl.ds(pl.multiple_of(owner * cells, 128), cells + 256)
-            height = parts[d].shape[0]
-            noise[:height, lanes] = noise[:height, lanes] + parts[d][...]
-        change, root = floats[0], floats[1]
+            if d > 0:
+                height = parts[d - 1].shape[0]
+                noise[:height, lanes] = noise[:height, lanes] + parts[d - 1][...]
+                continue
+            for r in range(rows + 2):
+                begin = chans + GROUPS + r // 2 * 32
+                coded = forward[pl.ds(begin, 32), pl.ds(r % 2 * 128, 128)].astype(F32)
+                spot = pl.ds(pl.multiple_of(owner * cells + r * 128, 128), 128)
+                noise[:, spot] = noise[:, spot] + coded[0:8] + coded[8:16] + coded[16:24]
+        position = jnp.broadcast_to(plan[ints[6]] + step, (8, 128)).astype(F32)
+        later = sigma_at(position + 1.0)
+        change = later - sigma_at(position)
+        shrink = lax.rsqrt(later * later + 1.0)
         field[...] = jnp.zeros_like(field)
         for r in range(full):
             piece = noise[:, pl.ds((r + 1) * 128, 128)]
@@ -302,7 +320,7 @@
                 old = latent_in[:, pl.ds(r * 128, 128)]
             new = old + change * piece
             latent_out[:, pl.ds(r * 128, 128)] = new
-            scaled = (new / root).astype(BF16).astype(F32)
+            scaled = (new * shrink).astype(BF16).astype(F32)
             before, after = shift_cols(scaled)
             lanes = pl.ds((r + 1) * 128, 128)
             field[pl.ds(0, 8), lanes] = before
@@ -477,7 +495,7 @@
         rank = rank ^ (rank >> turn)
         turn *= 2
 
-    def describe(row_block):
+    def describe(row_block, which):
         return jnp.stack(
             [
                 (row_block > 0).astype(jnp.int32),
@@ -486,6 +504,7 @@
                 row_block.astype(jnp.int32),
                 blocks_used[0],
                 core.astype(jnp.int32),
+                which.astype(jnp.int32),
             ]
         )
 
@@ -543,12 +562,7 @@
     ).reshape(lat, cells)
     latent_rows = jnp.concatenate([jnp.zeros((8 - lat, cells), F32), latent_rows], axis=0)
     layouts = (by_core,) * (STEPS + 1)
-    described = {by_core: describe(place), by_chips: describe(rank)}
-    floats = []
-    for step in range(STEPS):
-        position = pick(plan_pos, core if layouts[step + 1] is by_core else group) + step
-        now, later = sigma_at(position), sigma_at(position + 1)
-        floats.append(jnp.stack([later - now, jnp.sqrt(later * later + 1.0)]))
+    described = {by_core: describe(place, core), by_chips: describe(rank, group)}
     full_latent = None
 
     def exchange(layout, top_msg, bot_msg, st_msg):
@@ -567,12 +581,12 @@
         early = []
         noise, forward = call(
             functools.partial(head_kernel, len(early)),
-            (sds((height, cells + 256), F32), sds((chans + GROUPS, 256), BF16)),
+            (sds((height, cells + 256), F32), sds((chans + GROUPS + (rows + 2) // 2 * 32, 256), BF16)),
             [VM] * (6 + len(others) + len(extra)) + [HB] * len(early),
             [],
             300_000_000,
         )(params, own, up, down, head_packed, spread, *others, *extra, *early)
-        parts = [to_first(before, layout, noise, d) for d in range(chips)]
+        parts = [to_first(before, layout, noise, d) for d in range(1, chips)]
         forward_next = onward(before, layout, forward)
         extra = []
         if not first_step:
@@ -581,7 +595,7 @@
                 moves = [(before(m, l), layout(m, l)) for m, l in blocks]
                 extra = [lax.ppermute(full_latent, "patch", moves)]
         middle, source, full_latent, lat_keep, lat_send, *messages = call(
-            functools.partial(first_kernel, first_step, chips),
+            functools.partial(first_kernel, step, chips),
             (
                 wide_shape,
                 half_shape,
@@ -592,7 +606,7 @@
                 rows_shape,
                 stats_shape,
             ),
-            [SM, SM] + [VM] * (7 + chips + len(extra)),
+            [SM, SM] + [VM] * (6 + chips + len(extra)),
             conv_scratch
             + [
                 pltpu.VMEM((chans, cells + 256), BF16),
@@ -604,7 +618,7 @@
             conv_flops,
         )(
             ints,
-            floats[step],
+            plan_pos,
             params,
             *parts,
             *extra,

time: 153 us -> 148 us (0.967)
  waiting for transfers between devices: 34.1 us -> 30.6 us
  between operations: 4.13 us -> 1.81 us
    ppermute x8 -> x6, waiting for transfers between devices: 5.84 us -> 3.32 us  [to_first(): return lax.ppermute(x, joint, pairs)]
    ppermute x4, starting transfers between devices: 14.6 us -> 16.4 us  [swap(): return lax.ppermute(x, 'patch', swap_pairs)]
    ppermute x8 -> x6, starting transfers between devices: 13.1 us -> 11.3 us  [to_first(): return lax.ppermute(x, joint, pairs)]
  transfers between devices with their start and end apart: 43 -> 41, of which waited for: 15 -> 15; matrix products, arithmetic and copies ran while one was open for 1% -> 1% of each run, Pallas kernels for 6% -> 7%
where the time goes in v2:
time: 148 us; the launch traced here: 147 us
  starting transfers between devices  62.5 us (42%)
  Pallas kernels  44.1 us (30%)
  waiting for transfers between devices  30.6 us (21%)
  local copies, waits for them, and re-layouts  4.24 us (3%)
  other arithmetic  3.68 us (2%)
  between operations  1.81 us (1%)
    ppermute x24, starting transfers between devices, around(): lax.ppermute(x, 'patch', [(layout(m, l), layout(m, l + by)) for m, l in b...  30.2 us
    pallas_call x6, Pallas kernels, conv(): call(functools.partial(conv_kernel, index, base is not None, last), (half...  24.9 us
    ppermute x24, waiting for transfers between devices, around(): lax.ppermute(x, 'patch', [(layout(m, l), layout(m, l + by)) for m, l in b...  24.5 us
    ppermute x4, starting transfers between devices, swap(): return lax.ppermute(x, 'patch', swap_pairs)  16.4 us
    pallas_call x2, Pallas kernels, per_device(): call(functools.partial(first_kernel, step, chips), (wide_shape, half_shap...  13.3 us
    ppermute x6, starting transfers between devices, to_first(): return lax.ppermute(x, joint, pairs)  11.3 us
    ppermute x4, starting transfers between devices, onward(): return lax.ppermute(x, joint, pairs)  4.03 us
    ppermute x6, waiting for transfers between devices, to_first(): return lax.ppermute(x, joint, pairs)  3.32 us
  transfers between devices with their start and end apart: 41, of which 15 were waited for; matrix products, arithmetic and copies ran while one was open for 1% of the time, Pallas kernels for 7%

profile of v2, /device:TPU:1, one launch (start us, length us, event | category | flops | bytes accessed | tf_op | source)
XLA Modules:
  0.0 147.0 jit_solution(169865194736631045)
XLA Ops:
  5.3 2.4 %collective-permute-start.8 = (bf16[320,1024]{1,0:T(8,128)(2,1)S(1)}, bf16[320,1024]{1,0:T(8,128)(2,1)S(1)}, u32[]{:S(2)}, u32[]{:S(2)}) collective-permute-start(bf16[320,1024]{1,0:T(8,128)(2,1)S(1)} %bitcast.54), channel_id=1, source_target_pairs={{0,8},{2,10},{4,12},{6,14},{1,9},{3,11},{5,13},{7,15},{8,16},{10,1... | collective-permute-start | bytes 1966088 | tf_op jit(solution)/shard_map/ppermute | solution.py:476
  8.5 2.4 %collective-permute-start.3 = (bf16[32,128]{1,0:T(8,128)(2,1)S(1)}, bf16[32,128]{1,0:T(8,128)(2,1)S(1)}, u32[]{:S(2)}, u32[]{:S(2)}) collective-permute-start(bf16[32,128]{1,0:T(8,128)(2,1)S(1)} %get-tuple-element.81.rest_0_), channel_id=1, source_target_pairs={{0,4},{2,6},{4,0},{6,2},{1,5},{3,7},{5,1},{7,3},{8,12},{10,14},{12... | collective-permute-start | bytes 24584 | tf_op jit(solution)/shard_map/ppermute | solution.py:468
  13.4 2.0 %collective-permute-start.2 = (bf16[352,128]{1,0:T(8,128)(2,1)S(1)}, bf16[352,128]{1,0:T(8,128)(2,1)S(1)}, u32[]{:S(2)}, u32[]{:S(2)}) collective-permute-start(bf16[352,128]{1,0:T(8,128)(2,1)S(1)} %get-tuple-element.88), channel_id=1, source_target_pairs={{0,6},{2,0},{4,2},{6,4},{1,7},{3,1},{5,3},{7,5},{8,14},{10,8},{12,... | collective-permute-start | bytes 270344 | tf_op jit(solution)/shard_map/ppermute | solution.py:468
  15.5 2.7 %collective-permute-done.1.up = bf16[352,128]{1,0:T(8,128)(2,1)S(1)} collective-permute-done((bf16[352,128]{1,0:T(8,128)(2,1)S(1)}, bf16[352,128]{1,0:T(8,128)(2,1)S(1)}, u32[]{:S(2)}, u32[]{:S(2)}) %collective-permute-start.1) | collective-permute-done | bytes 90144 | tf_op jit(solution)/shard_map/ppermute | solution.py:468
  23.0 1.6 %collective-permute-start.6 = (f32[8,1280]{1,0:T(8,128)S(1)}, f32[8,1280]{1,0:T(8,128)S(1)}, u32[]{:S(2)}, u32[]{:S(2)}) collective-permute-start(f32[8,1280]{1,0:T(8,128)S(1)} %get-tuple-element.91), channel_id=1, source_target_pairs={{0,12},{2,14},{4,8},{6,10},{1,13},{3,15},{5,9},{7,11},{8,20},{10,2... | collective-permute-start | bytes 122888 | tf_op jit(solution)/shard_map/ppermute | solution.py:484
  24.6 2.3 %collective-permute-start.7 = (f32[8,1280]{1,0:T(8,128)S(1)}, f32[8,1280]{1,0:T(8,128)S(1)}, u32[]{:S(2)}, u32[]{:S(2)}) collective-permute-start(f32[8,1280]{1,0:T(8,128)S(1)} %get-tuple-element.91), channel_id=1, source_target_pairs={{0,14},{2,8},{4,10},{6,12},{1,15},{3,9},{5,11},{7,13},{8,22},{10,1... | collective-permute-start | bytes 122888 | tf_op jit(solution)/shard_map/ppermute | solution.py:484
  27.9 2.3 %copy-done = bf16[1,2,9,320,320]{4,3,2,1,0:T(8,128)(2,1)S(1)} copy-done((bf16[1,2,9,320,320]{4,3,2,1,0:T(8,128)(2,1)S(1)}, bf16[1,2,9,320,320]{4,3,2,1,0:T(8,128)(2,1)}, u32[]{:S(2)}) %copy-start) | copy-done | bytes 3686424
  30.8 6.6 %shard_map.152 = (f32[320,1024]{1,0:T(8,128)S(1)}, bf16[320,1024]{1,0:T(8,128)(2,1)S(1)}, f32[8,4096]{1,0:T(8,128)S(1)}, f32[4,512]{1,0:T(4,128)}, f32[4,512]{1,...) custom-call(s32[7]{0:T(128)S(1)} %stack.61.ints, ...), custom_call_target="tpu_custom_call" | custom-call | flops 1887436800 | bytes 4000000 | tf_op jit(solution)/shard_map/pallas_call | solution.py:597
  39.0 2.0 %collective-permute-start.11 = (bf16[352,128]{1,0:T(8,128)(2,1)S(1)}, bf16[352,128]{1,0:T(8,128)(2,1)S(1)}, u32[]{:S(2)}, u32[]{:S(2)}) collective-permute-start(bf16[352,128]{1,0:T(8,128)(2,1)S(1)} %get-tuple-element.97), channel_id=1, source_target_pairs={{0,6},{2,0},{4,2},{6,4},{1,7},{3,1},{5,3},{7,5},{8,14},{10,8},{12,... | collective-permute-start | bytes 270344 | tf_op jit(solution)/shard_map/ppermute | solution.py:468
  42.5 2.3 %collective-permute-done.12.rest_2_ = bf16[32,128]{1,0:T(8,128)(2,1)S(1)} collective-permute-done((bf16[32,128]{1,0:T(8,128)(2,1)S(1)}, bf16[32,128]{1,0:T(8,128)(2,1)S(1)}, u32[]{:S(2)}, u32[]{:S(2)}) %collective-permute-start.12) | collective-permute-done | bytes 8224 | tf_op jit(solution)/shard_map/ppermute | solution.py:468
  44.9 4.2 %shard_map.154 = (bf16[320,1024]{1,0:T(8,128)(2,1)S(1)}, bf16[352,128]{1,0:T(8,128)(2,1)S(1)}, bf16[352,128]{1,0:T(8,128)(2,1)S(1)}, bf16[32,128]{1,0:T(8,128)(2,1)S(1)}) custom-call(s32[7]{0:T(128)S(1)} %stack.61.ints, f32[320,16]{1,0:T(8,128)S(1)} %bitcast.59, f32[320,1024]{1,0:T(8,128)S(1)} %get-tuple-element.95.own, ...), custom_call_target="tpu_custom_call" | custom-call | flops 1887436800 | bytes 4000000 | tf_op jit(solution)/shard_map/pallas_call | solution.py:647
  49.6 2.9 %collective-permute-start.14 = (bf16[352,128]{1,0:T(8,128)(2,1)S(1)}, bf16[352,128]{1,0:T(8,128)(2,1)S(1)}, u32[]{:S(2)}, u32[]{:S(2)}) collective-permute-start(bf16[352,128]{1,0:T(8,128)(2,1)S(1)} %get-tuple-element.103), channel_id=1, source_target_pairs={{0,6},{2,0},{4,2},{6,4},{1,7},{3,1},{5,3},{7,5},{8,14},{10,8},{12,... | collective-permute-start | bytes 270344 | tf_op jit(solution)/shard_map/ppermute | solution.py:468
  53.0 2.9 %collective-permute-done.15.rest_1_ = bf16[32,128]{1,0:T(8,128)(2,1)S(1)} collective-permute-done((bf16[32,128]{1,0:T(8,128)(2,1)S(1)}, bf16[32,128]{1,0:T(8,128)(2,1)S(1)}, u32[]{:S(2)}, u32[]{:S(2)}) %collective-permute-start.15) | collective-permute-done | bytes 8224 | tf_op jit(solution)/shard_map/ppermute | solution.py:468
  56.0 4.1 %shard_map.156 = (f32[320,1024]{1,0:T(8,128)S(1)}, bf16[352,128]{1,0:T(8,128)(2,1)S(1)}, bf16[352,128]{1,0:T(8,128)(2,1)S(1)}, bf16[32,128]{1,0:T(8,128)(2,1)S(1)}) custom-call(s32[7]{0:T(128)S(1)} %stack.61.ints, f32[320,16]{1,0:T(8,128)S(1)} %bitcast.60, bf16[320,1024]{1,0:T(8,128)(2,1)S(1)} %get-tuple-element.101.own.rest_0_, ...), custom_call_target="tpu_custom_call" | custom-call | flops 1887436800 | bytes 4000000 | tf_op jit(solution)/shard_map/pallas_call | solution.py:647
  60.2 3.3 %collective-permute-start.17 = (bf16[352,128]{1,0:T(8,128)(2,1)S(1)}, bf16[352,128]{1,0:T(8,128)(2,1)S(1)}, u32[]{:S(2)}, u32[]{:S(2)}) collective-permute-start(bf16[352,128]{1,0:T(8,128)(2,1)S(1)} %get-tuple-element.107), channel_id=1, source_target_pairs={{0,6},{2,0},{4,2},{6,4},{1,7},{3,1},{5,3},{7,5},{8,14},{10,8},{12,... | collective-permute-start | bytes 270344 | tf_op jit(solution)/shard_map/ppermute | solution.py:468
  64.0 2.8 %collective-permute-done.18.rest_2_ = bf16[32,128]{1,0:T(8,128)(2,1)S(1)} collective-permute-done((bf16[32,128]{1,0:T(8,128)(2,1)S(1)}, bf16[32,128]{1,0:T(8,128)(2,1)S(1)}, u32[]{:S(2)}, u32[]{:S(2)}) %collective-permute-start.18) | collective-permute-done | bytes 8224 | tf_op jit(solution)/shard_map/ppermute | solution.py:468
  66.8 4.4 %shard_map.158 = (bf16[320,1024]{1,0:T(8,128)(2,1)S(1)}, bf16[352,128]{1,0:T(8,128)(2,1)S(1)}, bf16[352,128]{1,0:T(8,128)(2,1)S(1)}, bf16[32,128]{1,0:T(8,128)(2,1)S(1)}) custom-call(s32[7]{0:T(128)S(1)} %stack.61.ints, f32[320,16]{1,0:T(8,128)S(1)} %bitcast.61, f32[320,1024]{1,0:T(8,128)S(1)} %get-tuple-element.105.own, ...), custom_call_target="tpu_custom_call" | custom-call | flops 1887436800 | bytes 4000000 | tf_op jit(solution)/shard_map/pallas_call | solution.py:647
  71.4 3.3 %collective-permute-start.20 = (bf16[352,128]{1,0:T(8,128)(2,1)S(1)}, bf16[352,128]{1,0:T(8,128)(2,1)S(1)}, u32[]{:S(2)}, u32[]{:S(2)}) collective-permute-start(bf16[352,128]{1,0:T(8,128)(2,1)S(1)} %get-tuple-element.111), channel_id=1, source_target_pairs={{0,6},{2,0},{4,2},{6,4},{1,7},{3,1},{5,3},{7,5},{8,14},{10,8},{12,... | collective-permute-start | bytes 270344 | tf_op jit(solution)/shard_map/ppermute | solution.py:468
  74.6 3.4 %collective-permute-done.21.rest_1_ = bf16[32,128]{1,0:T(8,128)(2,1)S(1)} collective-permute-done((bf16[32,128]{1,0:T(8,128)(2,1)S(1)}, bf16[32,128]{1,0:T(8,128)(2,1)S(1)}, u32[]{:S(2)}, u32[]{:S(2)}) %collective-permute-start.21) | collective-permute-done | bytes 8224 | tf_op jit(solution)/shard_map/ppermute | solution.py:468
  79.5 5.0 %collective-permute-start.23 = (f32[4,1280]{1,0:T(4,128)S(1)}, f32[4,1280]{1,0:T(4,128)S(1)}, u32[]{:S(2)}, u32[]{:S(2)}) collective-permute-start(f32[4,1280]{1,0:T(4,128)S(1)} %get-tuple-element.113), channel_id=1, source_target_pairs={{0,12},{2,14},{4,8},{6,10},{1,13},{3,15},{5,9},{7,11},{8,20},{10,2... | collective-permute-start | bytes 61448 | tf_op jit(solution)/shard_map/ppermute | solution.py:484
  86.4 2.6 %collective-permute-done.24.rest_2_ = f32[4,1280]{1,0:T(4,128)S(1)} collective-permute-done((f32[4,1280]{1,0:T(4,128)S(1)}, f32[4,1280]{1,0:T(4,128)S(1)}, u32[]{:S(2)}, u32[]{:S(2)}) %collective-permute-start.24) | collective-permute-done | bytes 20512 | tf_op jit(solution)/shard_map/ppermute | solution.py:484
  89.0 6.7 %shard_map.160 = (f32[320,1024]{1,0:T(8,128)S(1)}, bf16[320,1024]{1,0:T(8,128)(2,1)S(1)}, f32[8,4096]{1,0:T(8,128)}, f32[4,512]{1,0:T(4,128)S(1)}, f32[4,512]{1,...) custom-call(s32[7]{0:T(128)S(1)} %stack.61.ints, ...), custom_call_target="tpu_custom_call" | custom-call | flops 1887436800 | bytes 4000000 | tf_op jit(solution)/shard_map/pallas_call | solution.py:597
  97.2 1.8 %collective-permute-start.28 = (bf16[352,128]{1,0:T(8,128)(2,1)S(1)}, bf16[352,128]{1,0:T(8,128)(2,1)S(1)}, u32[]{:S(2)}, u32[]{:S(2)}) collective-permute-start(bf16[352,128]{1,0:T(8,128)(2,1)S(1)} %get-tuple-element.118), channel_id=1, source_target_pairs={{0,6},{2,0},{4,2},{6,4},{1,7},{3,1},{5,3},{7,5},{8,14},{10,8},{12,... | collective-permute-start | bytes 270344 | tf_op jit(solution)/shard_map/ppermute | solution.py:468
  99.1 3.3 %collective-permute-done.29.rest_2_ = bf16[32,128]{1,0:T(8,128)(2,1)S(1)} collective-permute-done((bf16[32,128]{1,0:T(8,128)(2,1)S(1)}, bf16[32,128]{1,0:T(8,128)(2,1)S(1)}, u32[]{:S(2)}, u32[]{:S(2)}) %collective-permute-start.29) | collective-permute-done | bytes 8224 | tf_op jit(solution)/shard_map/ppermute | solution.py:468
  102.4 4.3 %shard_map.161 = (bf16[320,1024]{1,0:T(8,128)(2,1)S(1)}, bf16[352,128]{1,0:T(8,128)(2,1)S(1)}, bf16[352,128]{1,0:T(8,128)(2,1)S(1)}, bf16[32,128]{1,0:T(8,128)(2,1)S(1)}) custom-call(s32[7]{0:T(128)S(1)} %stack.61.ints, f32[320,16]{1,0:T(8,128)S(1)} %bitcast.64, f32[320,1024]{1,0:T(8,128)S(1)} %get-tuple-element.116.own, ...), custom_call_target="tpu_custom_call" | custom-call | flops 1887436800 | bytes 4000000 | tf_op jit(solution)/shard_map/pallas_call | solution.py:647
  106.9 3.1 %collective-permute-start.31 = (bf16[352,128]{1,0:T(8,128)(2,1)S(1)}, bf16[352,128]{1,0:T(8,128)(2,1)S(1)}, u32[]{:S(2)}, u32[]{:S(2)}) collective-permute-start(bf16[352,128]{1,0:T(8,128)(2,1)S(1)} %get-tuple-element.123), channel_id=1, source_target_pairs={{0,6},{2,0},{4,2},{6,4},{1,7},{3,1},{5,3},{7,5},{8,14},{10,8},{12,... | collective-permute-start | bytes 270344 | tf_op jit(solution)/shard_map/ppermute | solution.py:468
  110.0 3.9 %collective-permute-done.32.rest_1_ = bf16[32,128]{1,0:T(8,128)(2,1)S(1)} collective-permute-done((bf16[32,128]{1,0:T(8,128)(2,1)S(1)}, bf16[32,128]{1,0:T(8,128)(2,1)S(1)}, u32[]{:S(2)}, u32[]{:S(2)}) %collective-permute-start.32) | collective-permute-done | bytes 8224 | tf_op jit(solution)/shard_map/ppermute | solution.py:468
  113.9 4.2 %shard_map.162 = (f32[320,1024]{1,0:T(8,128)S(1)}, bf16[352,128]{1,0:T(8,128)(2,1)S(1)}, bf16[352,128]{1,0:T(8,128)(2,1)S(1)}, bf16[32,128]{1,0:T(8,128)(2,1)S(1)}) custom-call(s32[7]{0:T(128)S(1)} %stack.61.ints, f32[320,16]{1,0:T(8,128)S(1)} %bitcast.65, bf16[320,1024]{1,0:T(8,128)(2,1)S(1)} %get-tuple-element.121.own.rest_0_, ...), custom_call_target="tpu_custom_call" | custom-call | flops 1887436800 | bytes 4000000 | tf_op jit(solution)/shard_map/pallas_call | solution.py:647
  119.1 2.3 %collective-permute-start.34 = (bf16[352,128]{1,0:T(8,128)(2,1)S(1)}, bf16[352,128]{1,0:T(8,128)(2,1)S(1)}, u32[]{:S(2)}, u32[]{:S(2)}) collective-permute-start(bf16[352,128]{1,0:T(8,128)(2,1)S(1)} %get-tuple-element.127), channel_id=1, source_target_pairs={{0,6},{2,0},{4,2},{6,4},{1,7},{3,1},{5,3},{7,5},{8,14},{10,8},{12,... | collective-permute-start | bytes 270344 | tf_op jit(solution)/shard_map/ppermute | solution.py:468
  121.4 14.4 %collective-permute-start.36 = (f32[4,512]{1,0:T(4,128)S(1)}, f32[4,512]{1,0:T(4,128)S(1)}, u32[]{:S(2)}, u32[]{:S(2)}) collective-permute-start(f32[4,512]{1,0:T(4,128)S(1)} %get-tuple-element.130), channel_id=1, source_target_pairs={{0,1},{1,0},{2,3},{3,2},{4,5},{5,4},{6,7},{7,6},{8,9},{9,8},{10,11... | collective-permute-start | bytes 24584 | tf_op jit(solution)/shard_map/ppermute | solution.py:457
  137.3 1.9 %collective-permute-done.35.rest_2_ = bf16[32,128]{1,0:T(8,128)(2,1)S(1)} collective-permute-done((bf16[32,128]{1,0:T(8,128)(2,1)S(1)}, bf16[32,128]{1,0:T(8,128)(2,1)S(1)}, u32[]{:S(2)}, u32[]{:S(2)}) %collective-permute-start.35) | collective-permute-done | bytes 8224 | tf_op jit(solution)/shard_map/ppermute | solution.py:468
  139.6 3.7 %shard_map.163 = bf16[320,1024]{1,0:T(8,128)(2,1)S(1)} custom-call(s32[7]{0:T(128)S(1)} %stack.61.ints, f32[320,16]{1,0:T(8,128)S(1)} %bitcast.66, f32[320,1024]{1,0:T(8,128)S(1)} %get-tuple-element.125.own, bf16[352,128]{1,0:T(8,128)(2,1)S(1)} %collective-permute-done.33.up, bf16[352,128]{1,0:T(8,128)(2,1)S(1)} %collective-permute-done.34.down, ...), custom_call_target="tpu_custom_call" | custom-call | flops 1887436800 | bytes 4000000 | tf_op jit(solution)/shard_map/pallas_call | solution.py:647
  (128 shorter events, 30.2 us)
Async XLA Ops:
  5.3 25.5 %collective-permute-start.8 = (bf16[320,1024]{1,0:T(8,128)(2,1)S(1)}, bf16[320,1024]{1,0:T(8,128)(2,1)S(1)}, u32[]{:S(2)}, u32[]{:S(2)}) collective-permute-start(bf16[320,1024]{1,0:T(8,128)(2,1)S(1)} %bitcast.54), channel_id=1, source_target_pairs={{0,8},{2,10},{4,12},{6,14},{1,9},{3,11},{5,13},{7,15},{8,16},{10,1... | collective-permute-start | bytes 1966088 | tf_op jit(solution)/shard_map/ppermute | solution.py:476
  8.5 7.0 %collective-permute-start.3 = (bf16[32,128]{1,0:T(8,128)(2,1)S(1)}, bf16[32,128]{1,0:T(8,128)(2,1)S(1)}, u32[]{:S(2)}, u32[]{:S(2)}) collective-permute-start(bf16[32,128]{1,0:T(8,128)(2,1)S(1)} %get-tuple-element.81.rest_0_), channel_id=1, source_target_pairs={{0,4},{2,6},{4,0},{6,2},{1,5},{3,7},{5,1},{7,3},{8,12},{10,14},{12... | collective-permute-start | bytes 24584 | tf_op jit(solution)/shard_map/ppermute | solution.py:468
  10.9 4.6 %collective-permute-start.4 = (f32[4,4,128]{2,1,0:T(4,128)S(1)}, f32[4,4,128]{2,1,0:T(4,128)S(1)}, u32[]{:S(2)}, u32[]{:S(2)}) collective-permute-start(f32[4,4,128]{2,1,0:T(4,128)S(1)} %dynamic-slice_bitcast_fusion.1), channel_id=1, source_target_pairs={{0,1},{1,0},{2,3},{3,2},{4,5},{5,4},{6,7},{7,6},{8,9},{9,8},{10,11... | collective-permute-start | bytes 24584 | tf_op jit(solution)/shard_map/ppermute | solution.py:457
  12.1 6.1 %collective-permute-start.1 = (bf16[352,128]{1,0:T(8,128)(2,1)S(1)}, bf16[352,128]{1,0:T(8,128)(2,1)S(1)}, u32[]{:S(2)}, u32[]{:S(2)}) collective-permute-start(bf16[352,128]{1,0:T(8,128)(2,1)S(1)} %get-tuple-element.87), channel_id=1, source_target_pairs={{0,2},{2,4},{4,6},{6,0},{1,3},{3,5},{5,7},{7,1},{8,10},{10,12},{12... | collective-permute-start | bytes 270344 | tf_op jit(solution)/shard_map/ppermute | solution.py:468
  13.4 6.0 %collective-permute-start.2 = (bf16[352,128]{1,0:T(8,128)(2,1)S(1)}, bf16[352,128]{1,0:T(8,128)(2,1)S(1)}, u32[]{:S(2)}, u32[]{:S(2)}) collective-permute-start(bf16[352,128]{1,0:T(8,128)(2,1)S(1)} %get-tuple-element.88), channel_id=1, source_target_pairs={{0,6},{2,0},{4,2},{6,4},{1,7},{3,1},{5,3},{7,5},{8,14},{10,8},{12,... | collective-permute-start | bytes 270344 | tf_op jit(solution)/shard_map/ppermute | solution.py:468
  20.6 10.2 %collective-permute-start.9 = (bf16[512,256]{1,0:T(8,128)(2,1)S(1)}, bf16[512,256]{1,0:T(8,128)(2,1)S(1)}, u32[]{:S(2)}, u32[]{:S(2)}) collective-permute-start(bf16[512,256]{1,0:T(8,128)(2,1)S(1)} %get-tuple-element.93), channel_id=1, source_target_pairs={{0,8},{2,10},{4,12},{6,14},{1,9},{3,11},{5,13},{7,15},{8,16},{10,1... | collective-permute-start | bytes 786440 | tf_op jit(solution)/shard_map/ppermute | solution.py:476
  21.8 8.9 %collective-permute-start.5 = (f32[8,1280]{1,0:T(8,128)S(1)}, f32[8,1280]{1,0:T(8,128)S(1)}, u32[]{:S(2)}, u32[]{:S(2)}) collective-permute-start(f32[8,1280]{1,0:T(8,128)S(1)} %get-tuple-element.91), channel_id=1, source_target_pairs={{0,10},{2,12},{4,14},{6,8},{1,11},{3,13},{5,15},{7,9},{8,18},{10,2... | collective-permute-start | bytes 122888 | tf_op jit(solution)/shard_map/ppermute | solution.py:484
  23.0 7.7 %collective-permute-start.6 = (f32[8,1280]{1,0:T(8,128)S(1)}, f32[8,1280]{1,0:T(8,128)S(1)}, u32[]{:S(2)}, u32[]{:S(2)}) collective-permute-start(f32[8,1280]{1,0:T(8,128)S(1)} %get-tuple-element.91), channel_id=1, source_target_pairs={{0,12},{2,14},{4,8},{6,10},{1,13},{3,15},{5,9},{7,11},{8,20},{10,2... | collective-permute-start | bytes 122888 | tf_op jit(solution)/shard_map/ppermute | solution.py:484
  24.6 6.1 %collective-permute-start.7 = (f32[8,1280]{1,0:T(8,128)S(1)}, f32[8,1280]{1,0:T(8,128)S(1)}, u32[]{:S(2)}, u32[]{:S(2)}) collective-permute-start(f32[8,1280]{1,0:T(8,128)S(1)} %get-tuple-element.91), channel_id=1, source_target_pairs={{0,14},{2,8},{4,10},{6,12},{1,15},{3,9},{5,11},{7,13},{8,22},{10,1... | collective-permute-start | bytes 122888 | tf_op jit(solution)/shard_map/ppermute | solution.py:484
  37.4 7.5 %collective-permute-start.10 = (bf16[352,128]{1,0:T(8,128)(2,1)S(1)}, bf16[352,128]{1,0:T(8,128)(2,1)S(1)}, u32[]{:S(2)}, u32[]{:S(2)}) collective-permute-start(bf16[352,128]{1,0:T(8,128)(2,1)S(1)} %get-tuple-element.96), channel_id=1, source_target_pairs={{0,2},{2,4},{4,6},{6,0},{1,3},{3,5},{5,7},{7,1},{8,10},{10,12},{12... | collective-permute-start | bytes 270344 | tf_op jit(solution)/shard_map/ppermute | solution.py:468
  39.0 5.8 %collective-permute-start.11 = (bf16[352,128]{1,0:T(8,128)(2,1)S(1)}, bf16[352,128]{1,0:T(8,128)(2,1)S(1)}, u32[]{:S(2)}, u32[]{:S(2)}) collective-permute-start(bf16[352,128]{1,0:T(8,128)(2,1)S(1)} %get-tuple-element.97), channel_id=1, source_target_pairs={{0,6},{2,0},{4,2},{6,4},{1,7},{3,1},{5,3},{7,5},{8,14},{10,8},{12,... | collective-permute-start | bytes 270344 | tf_op jit(solution)/shard_map/ppermute | solution.py:468
  49.1 6.8 %collective-permute-start.13 = (bf16[352,128]{1,0:T(8,128)(2,1)S(1)}, bf16[352,128]{1,0:T(8,128)(2,1)S(1)}, u32[]{:S(2)}, u32[]{:S(2)}) collective-permute-start(bf16[352,128]{1,0:T(8,128)(2,1)S(1)} %get-tuple-element.102), channel_id=1, source_target_pairs={{0,2},{2,4},{4,6},{6,0},{1,3},{3,5},{5,7},{7,1},{8,10},{10,12},{12... | collective-permute-start | bytes 270344 | tf_op jit(solution)/shard_map/ppermute | solution.py:468
  49.6 6.4 %collective-permute-start.14 = (bf16[352,128]{1,0:T(8,128)(2,1)S(1)}, bf16[352,128]{1,0:T(8,128)(2,1)S(1)}, u32[]{:S(2)}, u32[]{:S(2)}) collective-permute-start(bf16[352,128]{1,0:T(8,128)(2,1)S(1)} %get-tuple-element.103), channel_id=1, source_target_pairs={{0,6},{2,0},{4,2},{6,4},{1,7},{3,1},{5,3},{7,5},{8,14},{10,8},{12,... | collective-permute-start | bytes 270344 | tf_op jit(solution)/shard_map/ppermute | solution.py:468
  60.1 6.7 %collective-permute-start.16 = (bf16[352,128]{1,0:T(8,128)(2,1)S(1)}, bf16[352,128]{1,0:T(8,128)(2,1)S(1)}, u32[]{:S(2)}, u32[]{:S(2)}) collective-permute-start(bf16[352,128]{1,0:T(8,128)(2,1)S(1)} %get-tuple-element.106), channel_id=1, source_target_pairs={{0,2},{2,4},{4,6},{6,0},{1,3},{3,5},{5,7},{7,1},{8,10},{10,12},{12... | collective-permute-start | bytes 270344 | tf_op jit(solution)/shard_map/ppermute | solution.py:468
  60.2 6.7 %collective-permute-start.17 = (bf16[352,128]{1,0:T(8,128)(2,1)S(1)}, bf16[352,128]{1,0:T(8,128)(2,1)S(1)}, u32[]{:S(2)}, u32[]{:S(2)}) collective-permute-start(bf16[352,128]{1,0:T(8,128)(2,1)S(1)} %get-tuple-element.107), channel_id=1, source_target_pairs={{0,6},{2,0},{4,2},{6,4},{1,7},{3,1},{5,3},{7,5},{8,14},{10,8},{12,... | collective-permute-start | bytes 270344 | tf_op jit(solution)/shard_map/ppermute | solution.py:468
  71.2 17.8 %collective-permute-start.25 = (bf16[320,1024]{1,0:T(8,128)(2,1)S(1)}, bf16[320,1024]{1,0:T(8,128)(2,1)S(1)}, u32[]{:S(2)}, u32[]{:S(2)}) collective-permute-start(bf16[320,1024]{1,0:T(8,128)(2,1)S(1)} %get-tuple-element.109.own), channel_id=1, source_target_pairs={{0,8},{2,10},{4,12},{6,14},{1,9},{3,11},{5,13},{7,15},{8,16},{10,1... | collective-permute-start | bytes 1966088 | tf_op jit(solution)/shard_map/ppermute | solution.py:476
  71.3 6.7 %collective-permute-start.19 = (bf16[352,128]{1,0:T(8,128)(2,1)S(1)}, bf16[352,128]{1,0:T(8,128)(2,1)S(1)}, u32[]{:S(2)}, u32[]{:S(2)}) collective-permute-start(bf16[352,128]{1,0:T(8,128)(2,1)S(1)} %get-tuple-element.110), channel_id=1, source_target_pairs={{0,2},{2,4},{4,6},{6,0},{1,3},{3,5},{5,7},{7,1},{8,10},{10,12},{12... | collective-permute-start | bytes 270344 | tf_op jit(solution)/shard_map/ppermute | solution.py:468
  71.4 6.7 %collective-permute-start.20 = (bf16[352,128]{1,0:T(8,128)(2,1)S(1)}, bf16[352,128]{1,0:T(8,128)(2,1)S(1)}, u32[]{:S(2)}, u32[]{:S(2)}) collective-permute-start(bf16[352,128]{1,0:T(8,128)(2,1)S(1)} %get-tuple-element.111), channel_id=1, source_target_pairs={{0,6},{2,0},{4,2},{6,4},{1,7},{3,1},{5,3},{7,5},{8,14},{10,8},{12,... | collective-permute-start | bytes 270344 | tf_op jit(solution)/shard_map/ppermute | solution.py:468
  79.2 9.8 %collective-permute-start.26 = (bf16[512,256]{1,0:T(8,128)(2,1)S(1)}, bf16[512,256]{1,0:T(8,128)(2,1)S(1)}, u32[]{:S(2)}, u32[]{:S(2)}) collective-permute-start(bf16[512,256]{1,0:T(8,128)(2,1)S(1)} %get-tuple-element.115), channel_id=1, source_target_pairs={{0,8},{2,10},{4,12},{6,14},{1,9},{3,11},{5,13},{7,15},{8,16},{10,1... | collective-permute-start | bytes 786440 | tf_op jit(solution)/shard_map/ppermute | solution.py:476
  79.5 6.5 %collective-permute-start.22 = (f32[4,1280]{1,0:T(4,128)S(1)}, f32[4,1280]{1,0:T(4,128)S(1)}, u32[]{:S(2)}, u32[]{:S(2)}) collective-permute-start(f32[4,1280]{1,0:T(4,128)S(1)} %get-tuple-element.113), channel_id=1, source_target_pairs={{0,10},{2,12},{4,14},{6,8},{1,11},{3,13},{5,15},{7,9},{8,18},{10,2... | collective-permute-start | bytes 61448 | tf_op jit(solution)/shard_map/ppermute | solution.py:484
  79.5 6.9 %collective-permute-start.23 = (f32[4,1280]{1,0:T(4,128)S(1)}, f32[4,1280]{1,0:T(4,128)S(1)}, u32[]{:S(2)}, u32[]{:S(2)}) collective-permute-start(f32[4,1280]{1,0:T(4,128)S(1)} %get-tuple-element.113), channel_id=1, source_target_pairs={{0,12},{2,14},{4,8},{6,10},{1,13},{3,15},{5,9},{7,11},{8,20},{10,2... | collective-permute-start | bytes 61448 | tf_op jit(solution)/shard_map/ppermute | solution.py:484
  84.5 4.5 %collective-permute-start.24 = (f32[4,1280]{1,0:T(4,128)S(1)}, f32[4,1280]{1,0:T(4,128)S(1)}, u32[]{:S(2)}, u32[]{:S(2)}) collective-permute-start(f32[4,1280]{1,0:T(4,128)S(1)} %get-tuple-element.113), channel_id=1, source_target_pairs={{0,14},{2,8},{4,10},{6,12},{1,15},{3,9},{5,11},{7,13},{8,22},{10,1... | collective-permute-start | bytes 61448 | tf_op jit(solution)/shard_map/ppermute | solution.py:484
  95.7 6.7 %collective-permute-start.27 = (bf16[352,128]{1,0:T(8,128)(2,1)S(1)}, bf16[352,128]{1,0:T(8,128)(2,1)S(1)}, u32[]{:S(2)}, u32[]{:S(2)}) collective-permute-start(bf16[352,128]{1,0:T(8,128)(2,1)S(1)} %get-tuple-element.117), channel_id=1, source_target_pairs={{0,2},{2,4},{4,6},{6,0},{1,3},{3,5},{5,7},{7,1},{8,10},{10,12},{12... | collective-permute-start | bytes 270344 | tf_op jit(solution)/shard_map/ppermute | solution.py:468
  97.2 5.2 %collective-permute-start.28 = (bf16[352,128]{1,0:T(8,128)(2,1)S(1)}, bf16[352,128]{1,0:T(8,128)(2,1)S(1)}, u32[]{:S(2)}, u32[]{:S(2)}) collective-permute-start(bf16[352,128]{1,0:T(8,128)(2,1)S(1)} %get-tuple-element.118), channel_id=1, source_target_pairs={{0,6},{2,0},{4,2},{6,4},{1,7},{3,1},{5,3},{7,5},{8,14},{10,8},{12,... | collective-permute-start | bytes 270344 | tf_op jit(solution)/shard_map/ppermute | solution.py:468
  106.7 7.2 %collective-permute-start.30 = (bf16[352,128]{1,0:T(8,128)(2,1)S(1)}, bf16[352,128]{1,0:T(8,128)(2,1)S(1)}, u32[]{:S(2)}, u32[]{:S(2)}) collective-permute-start(bf16[352,128]{1,0:T(8,128)(2,1)S(1)} %get-tuple-element.122), channel_id=1, source_target_pairs={{0,2},{2,4},{4,6},{6,0},{1,3},{3,5},{5,7},{7,1},{8,10},{10,12},{12... | collective-permute-start | bytes 270344 | tf_op jit(solution)/shard_map/ppermute | solution.py:468
  106.9 7.0 %collective-permute-start.31 = (bf16[352,128]{1,0:T(8,128)(2,1)S(1)}, bf16[352,128]{1,0:T(8,128)(2,1)S(1)}, u32[]{:S(2)}, u32[]{:S(2)}) collective-permute-start(bf16[352,128]{1,0:T(8,128)(2,1)S(1)} %get-tuple-element.123), channel_id=1, source_target_pairs={{0,6},{2,0},{4,2},{6,4},{1,7},{3,1},{5,3},{7,5},{8,14},{10,8},{12,... | collective-permute-start | bytes 270344 | tf_op jit(solution)/shard_map/ppermute | solution.py:468
  118.1 21.5 %collective-permute-start.33 = (bf16[352,128]{1,0:T(8,128)(2,1)S(1)}, bf16[352,128]{1,0:T(8,128)(2,1)S(1)}, u32[]{:S(2)}, u32[]{:S(2)}) collective-permute-start(bf16[352,128]{1,0:T(8,128)(2,1)S(1)} %get-tuple-element.126), channel_id=1, source_target_pairs={{0,2},{2,4},{4,6},{6,0},{1,3},{3,5},{5,7},{7,1},{8,10},{10,12},{12... | collective-permute-start | bytes 270344 | tf_op jit(solution)/shard_map/ppermute | solution.py:468
  119.1 20.5 %collective-permute-start.34 = (bf16[352,128]{1,0:T(8,128)(2,1)S(1)}, bf16[352,128]{1,0:T(8,128)(2,1)S(1)}, u32[]{:S(2)}, u32[]{:S(2)}) collective-permute-start(bf16[352,128]{1,0:T(8,128)(2,1)S(1)} %get-tuple-element.127), channel_id=1, source_target_pairs={{0,6},{2,0},{4,2},{6,4},{1,7},{3,1},{5,3},{7,5},{8,14},{10,8},{12,... | collective-permute-start | bytes 270344 | tf_op jit(solution)/shard_map/ppermute | solution.py:468
  121.4 15.2 %collective-permute-start.36 = (f32[4,512]{1,0:T(4,128)S(1)}, f32[4,512]{1,0:T(4,128)S(1)}, u32[]{:S(2)}, u32[]{:S(2)}) collective-permute-start(f32[4,512]{1,0:T(4,128)S(1)} %get-tuple-element.130), channel_id=1, source_target_pairs={{0,1},{1,0},{2,3},{3,2},{4,5},{5,4},{6,7},{7,6},{8,9},{9,8},{10,11... | collective-permute-start | bytes 24584 | tf_op jit(solution)/shard_map/ppermute | solution.py:457
  137.2 6.1 %collective-permute-start.37 = (f32[8,512]{1,0:T(8,128)S(1)}, f32[8,512]{1,0:T(8,128)S(1)}, u32[]{:S(2)}, u32[]{:S(2)}) collective-permute-start(f32[8,512]{1,0:T(8,128)S(1)} %shard_map.164), channel_id=1, source_target_pairs={{0,8},{8,16},{16,24},{24,0},{1,9},{9,17},{17,25},{25,1},{2,10},{10... | collective-permute-start | bytes 49160 | tf_op jit(solution)/shard_map/ppermute | solution.py:638
  137.2 6.0 %collective-permute-start.38 = (f32[8,512]{1,0:T(8,128)S(1)}, f32[8,512]{1,0:T(8,128)S(1)}, u32[]{:S(2)}, u32[]{:S(2)}) collective-permute-start(f32[8,512]{1,0:T(8,128)S(1)} %shard_map.164), channel_id=1, source_target_pairs={{0,16},{8,24},{16,0},{24,8},{1,17},{9,25},{17,1},{25,9},{2,18},{10... | collective-permute-start | bytes 49160 | tf_op jit(solution)/shard_map/ppermute | solution.py:638
  139.2 4.1 %collective-permute-start.39 = (f32[8,512]{1,0:T(8,128)S(1)}, f32[8,512]{1,0:T(8,128)S(1)}, u32[]{:S(2)}, u32[]{:S(2)}) collective-permute-start(f32[8,512]{1,0:T(8,128)S(1)} %shard_map.164), channel_id=1, source_target_pairs={{0,24},{8,0},{16,8},{24,16},{1,25},{9,1},{17,9},{25,17},{2,26},{10... | collective-permute-start | bytes 49160 | tf_op jit(solution)/shard_map/ppermute | solution.py:638
  (24 other events, 170.6 us)

commit v3 on v2

--- a/solution.py
+++ b/solution.py
@@ -311,7 +311,8 @@
         later = sigma_at(position + 1.0)
         change = later - sigma_at(position)
         shrink = lax.rsqrt(later * later + 1.0)
-        field[...] = jnp.zeros_like(field)
+        for edge in (0, (full + 1) * 128):
+            field[:, pl.ds(edge, 128)] = jnp.zeros((24, 128), F32)
         for r in range(full):
             piece = noise[:, pl.ds((r + 1) * 128, 128)]
             if first_step:
@@ -338,7 +339,7 @@
             entry[:, pl.ds(z * cells + 128, cells)] = rows_out
             kept = [rows_out[:, r * 128 : (r + 1) * 128].astype(F32) for r in range(rows)]
             if z == 0:
-                pivot, center = pivot_of(kept, gather[...], spread[...], per_row)
+                pivot, center = pivot_of(kept[:2], gather[...], spread[...], per_row)
             sums = add_deviations(sums, kept, center)
         entry[:, pl.ds(0, 128)] = jnp.zeros((chans, 128), BF16)
         entry[:, pl.ds(full * 128 + 128, 128)] = jnp.zeros((chans, 128), BF16)
@@ -519,10 +520,13 @@
     conv_scratch = [pltpu.VMEM((3 * chans, cells + 256), BF16)]
 
     first_core = core == 0
-    mine = pick(features[0], core)
-    other = swap(pick(features[0], 1 - core))
+    mine, other = features[0], swap(features[0])
     own = jnp.concatenate(
-        [jnp.where(first_core, mine, other), jnp.where(first_core, other, mine)], axis=1
+        [
+            jnp.where(first_core, mine[0], other[1]),
+            jnp.where(first_core, other[0], mine[1]),
+        ],
+        axis=1,
     ).reshape(chans, cells)
     messages = call(
         enter_kernel, (rows_shape, rows_shape, stats_shape), [VM] * 3, [], 10_000_000

time: 148 us -> 147 us (level)
  no operation moved by 1% of the time
where the time goes in v3:
time: 147 us; the launch traced here: 146 us
  starting transfers between devices  62.6 us (43%)
  Pallas kernels  43.9 us (30%)
  waiting for transfers between devices  31.3 us (21%)
  other arithmetic  3.84 us (3%)
  local copies, waits for them, and re-layouts  3.15 us (2%)
  between operations  1.81 us (1%)
    ppermute x24, starting transfers between devices, around(): lax.ppermute(x, 'patch', [(layout(m, l), layout(m, l + by)) for m, l in b...  30.2 us
    pallas_call x6, Pallas kernels, conv(): call(functools.partial(conv_kernel, index, base is not None, last), (half...  24.9 us
    ppermute x24, waiting for transfers between devices, around(): lax.ppermute(x, 'patch', [(layout(m, l), layout(m, l + by)) for m, l in b...  24.4 us
    ppermute x4, starting transfers between devices, swap(): return lax.ppermute(x, 'patch', swap_pairs)  16.5 us
    pallas_call x2, Pallas kernels, per_device(): call(functools.partial(first_kernel, step, chips), (wide_shape, half_shap...  13.1 us
    ppermute x6, starting transfers between devices, to_first(): return lax.ppermute(x, joint, pairs)  11.2 us
    ppermute x4, starting transfers between devices, onward(): return lax.ppermute(x, joint, pairs)  4.15 us
    ppermute x4, waiting for transfers between devices, swap(): return lax.ppermute(x, 'patch', swap_pairs)  3.48 us
  transfers between devices with their start and end apart: 41, of which 15 were waited for; matrix products, arithmetic and copies ran while one was open for 1% of the time, Pallas kernels for 7%

profile of v3, /device:TPU:1, one launch (start us, length us, event | category | flops | bytes accessed | tf_op | source)
XLA Modules:
  0.0 146.5 jit_solution(3342113343716641812)
XLA Ops:
  0.8 2.3 %collective-permute-done = bf16[2,320,4,128]{3,2,1,0:T(4,128)(2,1)S(1)} collective-permute-done((bf16[2,320,4,128]{3,2,1,0:T(4,128)(2,1)}, bf16[2,320,4,128]{3,2,1,0:T(4,128)(2,1)S(1)}, u32[]{:S(2)}, u32[]{:S(2)}) %collective-permute-start) | collective-permute-done | bytes 655392 | tf_op jit(solution)/shard_map/ppermute | solution.py:458
  5.0 2.4 %collective-permute-start.8 = (bf16[320,1024]{1,0:T(8,128)(2,1)S(1)}, bf16[320,1024]{1,0:T(8,128)(2,1)S(1)}, u32[]{:S(2)}, u32[]{:S(2)}) collective-permute-start(bf16[320,1024]{1,0:T(8,128)(2,1)S(1)} %bitcast.62), channel_id=1, source_target_pairs={{0,8},{2,10},{4,12},{6,14},{1,9},{3,11},{5,13},{7,15},{8,16},{10,1... | collective-permute-start | bytes 1966088 | tf_op jit(solution)/shard_map/ppermute | solution.py:477
  8.2 2.4 %collective-permute-start.3 = (bf16[32,128]{1,0:T(8,128)(2,1)S(1)}, bf16[32,128]{1,0:T(8,128)(2,1)S(1)}, u32[]{:S(2)}, u32[]{:S(2)}) collective-permute-start(bf16[32,128]{1,0:T(8,128)(2,1)S(1)} %get-tuple-element.81.rest_0_), channel_id=1, source_target_pairs={{0,4},{2,6},{4,0},{6,2},{1,5},{3,7},{5,1},{7,3},{8,12},{10,14},{12... | collective-permute-start | bytes 24584 | tf_op jit(solution)/shard_map/ppermute | solution.py:469
  13.2 2.0 %collective-permute-start.2 = (bf16[352,128]{1,0:T(8,128)(2,1)S(1)}, bf16[352,128]{1,0:T(8,128)(2,1)S(1)}, u32[]{:S(2)}, u32[]{:S(2)}) collective-permute-start(bf16[352,128]{1,0:T(8,128)(2,1)S(1)} %get-tuple-element.88), channel_id=1, source_target_pairs={{0,6},{2,0},{4,2},{6,4},{1,7},{3,1},{5,3},{7,5},{8,14},{10,8},{12,... | collective-permute-start | bytes 270344 | tf_op jit(solution)/shard_map/ppermute | solution.py:469
  15.3 2.7 %collective-permute-done.1.up = bf16[352,128]{1,0:T(8,128)(2,1)S(1)} collective-permute-done((bf16[352,128]{1,0:T(8,128)(2,1)S(1)}, bf16[352,128]{1,0:T(8,128)(2,1)S(1)}, u32[]{:S(2)}, u32[]{:S(2)}) %collective-permute-start.1) | collective-permute-done | bytes 90144 | tf_op jit(solution)/shard_map/ppermute | solution.py:469
  24.4 2.3 %collective-permute-start.7 = (f32[8,1280]{1,0:T(8,128)S(1)}, f32[8,1280]{1,0:T(8,128)S(1)}, u32[]{:S(2)}, u32[]{:S(2)}) collective-permute-start(f32[8,1280]{1,0:T(8,128)S(1)} %get-tuple-element.91), channel_id=1, source_target_pairs={{0,14},{2,8},{4,10},{6,12},{1,15},{3,9},{5,11},{7,13},{8,22},{10,1... | collective-permute-start | bytes 122888 | tf_op jit(solution)/shard_map/ppermute | solution.py:485
  27.6 2.3 %copy-done = bf16[1,2,9,320,320]{4,3,2,1,0:T(8,128)(2,1)S(1)} copy-done((bf16[1,2,9,320,320]{4,3,2,1,0:T(8,128)(2,1)S(1)}, bf16[1,2,9,320,320]{4,3,2,1,0:T(8,128)(2,1)}, u32[]{:S(2)}) %copy-start) | copy-done | bytes 3686424
  30.6 6.5 %shard_map.152 = (f32[320,1024]{1,0:T(8,128)S(1)}, bf16[320,1024]{1,0:T(8,128)(2,1)S(1)}, f32[8,4096]{1,0:T(8,128)S(1)}, f32[4,512]{1,0:T(4,128)}, f32[4,512]{1,...) custom-call(s32[7]{0:T(128)S(1)} %stack.61.ints, ...), custom_call_target="tpu_custom_call" | custom-call | flops 1887436800 | bytes 4000000 | tf_op jit(solution)/shard_map/pallas_call | solution.py:601
  38.7 2.0 %collective-permute-start.11 = (bf16[352,128]{1,0:T(8,128)(2,1)S(1)}, bf16[352,128]{1,0:T(8,128)(2,1)S(1)}, u32[]{:S(2)}, u32[]{:S(2)}) collective-permute-start(bf16[352,128]{1,0:T(8,128)(2,1)S(1)} %get-tuple-element.97), channel_id=1, source_target_pairs={{0,6},{2,0},{4,2},{6,4},{1,7},{3,1},{5,3},{7,5},{8,14},{10,8},{12,... | collective-permute-start | bytes 270344 | tf_op jit(solution)/shard_map/ppermute | solution.py:469
  42.1 2.3 %collective-permute-done.12.rest_2_ = bf16[32,128]{1,0:T(8,128)(2,1)S(1)} collective-permute-done((bf16[32,128]{1,0:T(8,128)(2,1)S(1)}, bf16[32,128]{1,0:T(8,128)(2,1)S(1)}, u32[]{:S(2)}, u32[]{:S(2)}) %collective-permute-start.12) | collective-permute-done | bytes 8224 | tf_op jit(solution)/shard_map/ppermute | solution.py:469
  44.5 4.2 %shard_map.154 = (bf16[320,1024]{1,0:T(8,128)(2,1)S(1)}, bf16[352,128]{1,0:T(8,128)(2,1)S(1)}, bf16[352,128]{1,0:T(8,128)(2,1)S(1)}, bf16[32,128]{1,0:T(8,128)(2,1)S(1)}) custom-call(s32[7]{0:T(128)S(1)} %stack.61.ints, f32[320,16]{1,0:T(8,128)S(1)} %bitcast.67, f32[320,1024]{1,0:T(8,128)S(1)} %get-tuple-element.95.own, ...), custom_call_target="tpu_custom_call" | custom-call | flops 1887436800 | bytes 4000000 | tf_op jit(solution)/shard_map/pallas_call | solution.py:651
  49.1 2.9 %collective-permute-start.14 = (bf16[352,128]{1,0:T(8,128)(2,1)S(1)}, bf16[352,128]{1,0:T(8,128)(2,1)S(1)}, u32[]{:S(2)}, u32[]{:S(2)}) collective-permute-start(bf16[352,128]{1,0:T(8,128)(2,1)S(1)} %get-tuple-element.103), channel_id=1, source_target_pairs={{0,6},{2,0},{4,2},{6,4},{1,7},{3,1},{5,3},{7,5},{8,14},{10,8},{12,... | collective-permute-start | bytes 270344 | tf_op jit(solution)/shard_map/ppermute | solution.py:469
  52.6 2.9 %collective-permute-done.15.rest_1_ = bf16[32,128]{1,0:T(8,128)(2,1)S(1)} collective-permute-done((bf16[32,128]{1,0:T(8,128)(2,1)S(1)}, bf16[32,128]{1,0:T(8,128)(2,1)S(1)}, u32[]{:S(2)}, u32[]{:S(2)}) %collective-permute-start.15) | collective-permute-done | bytes 8224 | tf_op jit(solution)/shard_map/ppermute | solution.py:469
  55.6 4.1 %shard_map.156 = (f32[320,1024]{1,0:T(8,128)S(1)}, bf16[352,128]{1,0:T(8,128)(2,1)S(1)}, bf16[352,128]{1,0:T(8,128)(2,1)S(1)}, bf16[32,128]{1,0:T(8,128)(2,1)S(1)}) custom-call(s32[7]{0:T(128)S(1)} %stack.61.ints, f32[320,16]{1,0:T(8,128)S(1)} %bitcast.68, bf16[320,1024]{1,0:T(8,128)(2,1)S(1)} %get-tuple-element.101.own.rest_0_, ...), custom_call_target="tpu_custom_call" | custom-call | flops 1887436800 | bytes 4000000 | tf_op jit(solution)/shard_map/pallas_call | solution.py:651
  59.8 3.3 %collective-permute-start.17 = (bf16[352,128]{1,0:T(8,128)(2,1)S(1)}, bf16[352,128]{1,0:T(8,128)(2,1)S(1)}, u32[]{:S(2)}, u32[]{:S(2)}) collective-permute-start(bf16[352,128]{1,0:T(8,128)(2,1)S(1)} %get-tuple-element.107), channel_id=1, source_target_pairs={{0,6},{2,0},{4,2},{6,4},{1,7},{3,1},{5,3},{7,5},{8,14},{10,8},{12,... | collective-permute-start | bytes 270344 | tf_op jit(solution)/shard_map/ppermute | solution.py:469
  63.6 2.8 %collective-permute-done.18.rest_2_ = bf16[32,128]{1,0:T(8,128)(2,1)S(1)} collective-permute-done((bf16[32,128]{1,0:T(8,128)(2,1)S(1)}, bf16[32,128]{1,0:T(8,128)(2,1)S(1)}, u32[]{:S(2)}, u32[]{:S(2)}) %collective-permute-start.18) | collective-permute-done | bytes 8224 | tf_op jit(solution)/shard_map/ppermute | solution.py:469
  66.4 4.4 %shard_map.158 = (bf16[320,1024]{1,0:T(8,128)(2,1)S(1)}, bf16[352,128]{1,0:T(8,128)(2,1)S(1)}, bf16[352,128]{1,0:T(8,128)(2,1)S(1)}, bf16[32,128]{1,0:T(8,128)(2,1)S(1)}) custom-call(s32[7]{0:T(128)S(1)} %stack.61.ints, f32[320,16]{1,0:T(8,128)S(1)} %bitcast.69, f32[320,1024]{1,0:T(8,128)S(1)} %get-tuple-element.105.own, ...), custom_call_target="tpu_custom_call" | custom-call | flops 1887436800 | bytes 4000000 | tf_op jit(solution)/shard_map/pallas_call | solution.py:651
  71.0 3.3 %collective-permute-start.20 = (bf16[352,128]{1,0:T(8,128)(2,1)S(1)}, bf16[352,128]{1,0:T(8,128)(2,1)S(1)}, u32[]{:S(2)}, u32[]{:S(2)}) collective-permute-start(bf16[352,128]{1,0:T(8,128)(2,1)S(1)} %get-tuple-element.111), channel_id=1, source_target_pairs={{0,6},{2,0},{4,2},{6,4},{1,7},{3,1},{5,3},{7,5},{8,14},{10,8},{12,... | collective-permute-start | bytes 270344 | tf_op jit(solution)/shard_map/ppermute | solution.py:469
  74.2 3.4 %collective-permute-done.21.rest_1_ = bf16[32,128]{1,0:T(8,128)(2,1)S(1)} collective-permute-done((bf16[32,128]{1,0:T(8,128)(2,1)S(1)}, bf16[32,128]{1,0:T(8,128)(2,1)S(1)}, u32[]{:S(2)}, u32[]{:S(2)}) %collective-permute-start.21) | collective-permute-done | bytes 8224 | tf_op jit(solution)/shard_map/ppermute | solution.py:469
  79.2 4.9 %collective-permute-start.23 = (f32[4,1280]{1,0:T(4,128)S(1)}, f32[4,1280]{1,0:T(4,128)S(1)}, u32[]{:S(2)}, u32[]{:S(2)}) collective-permute-start(f32[4,1280]{1,0:T(4,128)S(1)} %get-tuple-element.113), channel_id=1, source_target_pairs={{0,12},{2,14},{4,8},{6,10},{1,13},{3,15},{5,9},{7,11},{8,20},{10,2... | collective-permute-start | bytes 61448 | tf_op jit(solution)/shard_map/ppermute | solution.py:485
  86.0 2.7 %collective-permute-done.24.rest_2_ = f32[4,1280]{1,0:T(4,128)S(1)} collective-permute-done((f32[4,1280]{1,0:T(4,128)S(1)}, f32[4,1280]{1,0:T(4,128)S(1)}, u32[]{:S(2)}, u32[]{:S(2)}) %collective-permute-start.24) | collective-permute-done | bytes 20512 | tf_op jit(solution)/shard_map/ppermute | solution.py:485
  88.6 6.6 %shard_map.160 = (f32[320,1024]{1,0:T(8,128)S(1)}, bf16[320,1024]{1,0:T(8,128)(2,1)S(1)}, f32[8,4096]{1,0:T(8,128)}, f32[4,512]{1,0:T(4,128)S(1)}, f32[4,512]{1,...) custom-call(s32[7]{0:T(128)S(1)} %stack.61.ints, ...), custom_call_target="tpu_custom_call" | custom-call | flops 1887436800 | bytes 4000000 | tf_op jit(solution)/shard_map/pallas_call | solution.py:601
  96.7 1.8 %collective-permute-start.28 = (bf16[352,128]{1,0:T(8,128)(2,1)S(1)}, bf16[352,128]{1,0:T(8,128)(2,1)S(1)}, u32[]{:S(2)}, u32[]{:S(2)}) collective-permute-start(bf16[352,128]{1,0:T(8,128)(2,1)S(1)} %get-tuple-element.118), channel_id=1, source_target_pairs={{0,6},{2,0},{4,2},{6,4},{1,7},{3,1},{5,3},{7,5},{8,14},{10,8},{12,... | collective-permute-start | bytes 270344 | tf_op jit(solution)/shard_map/ppermute | solution.py:469
  98.6 3.3 %collective-permute-done.29.rest_2_ = bf16[32,128]{1,0:T(8,128)(2,1)S(1)} collective-permute-done((bf16[32,128]{1,0:T(8,128)(2,1)S(1)}, bf16[32,128]{1,0:T(8,128)(2,1)S(1)}, u32[]{:S(2)}, u32[]{:S(2)}) %collective-permute-start.29) | collective-permute-done | bytes 8224 | tf_op jit(solution)/shard_map/ppermute | solution.py:469
  101.9 4.3 %shard_map.161 = (bf16[320,1024]{1,0:T(8,128)(2,1)S(1)}, bf16[352,128]{1,0:T(8,128)(2,1)S(1)}, bf16[352,128]{1,0:T(8,128)(2,1)S(1)}, bf16[32,128]{1,0:T(8,128)(2,1)S(1)}) custom-call(s32[7]{0:T(128)S(1)} %stack.61.ints, f32[320,16]{1,0:T(8,128)S(1)} %bitcast.72, f32[320,1024]{1,0:T(8,128)S(1)} %get-tuple-element.116.own, ...), custom_call_target="tpu_custom_call" | custom-call | flops 1887436800 | bytes 4000000 | tf_op jit(solution)/shard_map/pallas_call | solution.py:651
  106.4 3.1 %collective-permute-start.31 = (bf16[352,128]{1,0:T(8,128)(2,1)S(1)}, bf16[352,128]{1,0:T(8,128)(2,1)S(1)}, u32[]{:S(2)}, u32[]{:S(2)}) collective-permute-start(bf16[352,128]{1,0:T(8,128)(2,1)S(1)} %get-tuple-element.123), channel_id=1, source_target_pairs={{0,6},{2,0},{4,2},{6,4},{1,7},{3,1},{5,3},{7,5},{8,14},{10,8},{12,... | collective-permute-start | bytes 270344 | tf_op jit(solution)/shard_map/ppermute | solution.py:469
  109.5 3.8 %collective-permute-done.32.rest_1_ = bf16[32,128]{1,0:T(8,128)(2,1)S(1)} collective-permute-done((bf16[32,128]{1,0:T(8,128)(2,1)S(1)}, bf16[32,128]{1,0:T(8,128)(2,1)S(1)}, u32[]{:S(2)}, u32[]{:S(2)}) %collective-permute-start.32) | collective-permute-done | bytes 8224 | tf_op jit(solution)/shard_map/ppermute | solution.py:469
  113.3 4.2 %shard_map.162 = (f32[320,1024]{1,0:T(8,128)S(1)}, bf16[352,128]{1,0:T(8,128)(2,1)S(1)}, bf16[352,128]{1,0:T(8,128)(2,1)S(1)}, bf16[32,128]{1,0:T(8,128)(2,1)S(1)}) custom-call(s32[7]{0:T(128)S(1)} %stack.61.ints, f32[320,16]{1,0:T(8,128)S(1)} %bitcast.73, bf16[320,1024]{1,0:T(8,128)(2,1)S(1)} %get-tuple-element.121.own.rest_0_, ...), custom_call_target="tpu_custom_call" | custom-call | flops 1887436800 | bytes 4000000 | tf_op jit(solution)/shard_map/pallas_call | solution.py:651
  118.6 2.2 %collective-permute-start.34 = (bf16[352,128]{1,0:T(8,128)(2,1)S(1)}, bf16[352,128]{1,0:T(8,128)(2,1)S(1)}, u32[]{:S(2)}, u32[]{:S(2)}) collective-permute-start(bf16[352,128]{1,0:T(8,128)(2,1)S(1)} %get-tuple-element.127), channel_id=1, source_target_pairs={{0,6},{2,0},{4,2},{6,4},{1,7},{3,1},{5,3},{7,5},{8,14},{10,8},{12,... | collective-permute-start | bytes 270344 | tf_op jit(solution)/shard_map/ppermute | solution.py:469
  120.8 14.4 %collective-permute-start.36 = (f32[4,512]{1,0:T(4,128)S(1)}, f32[4,512]{1,0:T(4,128)S(1)}, u32[]{:S(2)}, u32[]{:S(2)}) collective-permute-start(f32[4,512]{1,0:T(4,128)S(1)} %get-tuple-element.130), channel_id=1, source_target_pairs={{0,1},{1,0},{2,3},{3,2},{4,5},{5,4},{6,7},{7,6},{8,9},{9,8},{10,11... | collective-permute-start | bytes 24584 | tf_op jit(solution)/shard_map/ppermute | solution.py:458
  136.8 1.9 %collective-permute-done.35.rest_2_ = bf16[32,128]{1,0:T(8,128)(2,1)S(1)} collective-permute-done((bf16[32,128]{1,0:T(8,128)(2,1)S(1)}, bf16[32,128]{1,0:T(8,128)(2,1)S(1)}, u32[]{:S(2)}, u32[]{:S(2)}) %collective-permute-start.35) | collective-permute-done | bytes 8224 | tf_op jit(solution)/shard_map/ppermute | solution.py:469
  139.1 3.7 %shard_map.163 = bf16[320,1024]{1,0:T(8,128)(2,1)S(1)} custom-call(s32[7]{0:T(128)S(1)} %stack.61.ints, f32[320,16]{1,0:T(8,128)S(1)} %bitcast.74, f32[320,1024]{1,0:T(8,128)S(1)} %get-tuple-element.125.own, bf16[352,128]{1,0:T(8,128)(2,1)S(1)} %collective-permute-done.33.up, bf16[352,128]{1,0:T(8,128)(2,1)S(1)} %collective-permute-done.34.down, ...), custom_call_target="tpu_custom_call" | custom-call | flops 1887436800 | bytes 4000000 | tf_op jit(solution)/shard_map/pallas_call | solution.py:651
  (127 shorter events, 29.5 us)
Async XLA Ops:
  5.0 25.5 %collective-permute-start.8 = (bf16[320,1024]{1,0:T(8,128)(2,1)S(1)}, bf16[320,1024]{1,0:T(8,128)(2,1)S(1)}, u32[]{:S(2)}, u32[]{:S(2)}) collective-permute-start(bf16[320,1024]{1,0:T(8,128)(2,1)S(1)} %bitcast.62), channel_id=1, source_target_pairs={{0,8},{2,10},{4,12},{6,14},{1,9},{3,11},{5,13},{7,15},{8,16},{10,1... | collective-permute-start | bytes 1966088 | tf_op jit(solution)/shard_map/ppermute | solution.py:477
  8.2 7.0 %collective-permute-start.3 = (bf16[32,128]{1,0:T(8,128)(2,1)S(1)}, bf16[32,128]{1,0:T(8,128)(2,1)S(1)}, u32[]{:S(2)}, u32[]{:S(2)}) collective-permute-start(bf16[32,128]{1,0:T(8,128)(2,1)S(1)} %get-tuple-element.81.rest_0_), channel_id=1, source_target_pairs={{0,4},{2,6},{4,0},{6,2},{1,5},{3,7},{5,1},{7,3},{8,12},{10,14},{12... | collective-permute-start | bytes 24584 | tf_op jit(solution)/shard_map/ppermute | solution.py:469
  10.6 4.6 %collective-permute-start.4 = (f32[4,4,128]{2,1,0:T(4,128)S(1)}, f32[4,4,128]{2,1,0:T(4,128)S(1)}, u32[]{:S(2)}, u32[]{:S(2)}) collective-permute-start(f32[4,4,128]{2,1,0:T(4,128)S(1)} %dynamic-slice_bitcast_fusion), channel_id=1, source_target_pairs={{0,1},{1,0},{2,3},{3,2},{4,5},{5,4},{6,7},{7,6},{8,9},{9,8},{10,11... | collective-permute-start | bytes 24584 | tf_op jit(solution)/shard_map/ppermute | solution.py:458
  11.9 6.1 %collective-permute-start.1 = (bf16[352,128]{1,0:T(8,128)(2,1)S(1)}, bf16[352,128]{1,0:T(8,128)(2,1)S(1)}, u32[]{:S(2)}, u32[]{:S(2)}) collective-permute-start(bf16[352,128]{1,0:T(8,128)(2,1)S(1)} %get-tuple-element.87), channel_id=1, source_target_pairs={{0,2},{2,4},{4,6},{6,0},{1,3},{3,5},{5,7},{7,1},{8,10},{10,12},{12... | collective-permute-start | bytes 270344 | tf_op jit(solution)/shard_map/ppermute | solution.py:469
  13.2 6.0 %collective-permute-start.2 = (bf16[352,128]{1,0:T(8,128)(2,1)S(1)}, bf16[352,128]{1,0:T(8,128)(2,1)S(1)}, u32[]{:S(2)}, u32[]{:S(2)}) collective-permute-start(bf16[352,128]{1,0:T(8,128)(2,1)S(1)} %get-tuple-element.88), channel_id=1, source_target_pairs={{0,6},{2,0},{4,2},{6,4},{1,7},{3,1},{5,3},{7,5},{8,14},{10,8},{12,... | collective-permute-start | bytes 270344 | tf_op jit(solution)/shard_map/ppermute | solution.py:469
  20.3 10.2 %collective-permute-start.9 = (bf16[512,256]{1,0:T(8,128)(2,1)S(1)}, bf16[512,256]{1,0:T(8,128)(2,1)S(1)}, u32[]{:S(2)}, u32[]{:S(2)}) collective-permute-start(bf16[512,256]{1,0:T(8,128)(2,1)S(1)} %get-tuple-element.93), channel_id=1, source_target_pairs={{0,8},{2,10},{4,12},{6,14},{1,9},{3,11},{5,13},{7,15},{8,16},{10,1... | collective-permute-start | bytes 786440 | tf_op jit(solution)/shard_map/ppermute | solution.py:477
  21.6 8.9 %collective-permute-start.5 = (f32[8,1280]{1,0:T(8,128)S(1)}, f32[8,1280]{1,0:T(8,128)S(1)}, u32[]{:S(2)}, u32[]{:S(2)}) collective-permute-start(f32[8,1280]{1,0:T(8,128)S(1)} %get-tuple-element.91), channel_id=1, source_target_pairs={{0,10},{2,12},{4,14},{6,8},{1,11},{3,13},{5,15},{7,9},{8,18},{10,2... | collective-permute-start | bytes 122888 | tf_op jit(solution)/shard_map/ppermute | solution.py:485
  22.8 7.7 %collective-permute-start.6 = (f32[8,1280]{1,0:T(8,128)S(1)}, f32[8,1280]{1,0:T(8,128)S(1)}, u32[]{:S(2)}, u32[]{:S(2)}) collective-permute-start(f32[8,1280]{1,0:T(8,128)S(1)} %get-tuple-element.91), channel_id=1, source_target_pairs={{0,12},{2,14},{4,8},{6,10},{1,13},{3,15},{5,9},{7,11},{8,20},{10,2... | collective-permute-start | bytes 122888 | tf_op jit(solution)/shard_map/ppermute | solution.py:485
  24.4 6.1 %collective-permute-start.7 = (f32[8,1280]{1,0:T(8,128)S(1)}, f32[8,1280]{1,0:T(8,128)S(1)}, u32[]{:S(2)}, u32[]{:S(2)}) collective-permute-start(f32[8,1280]{1,0:T(8,128)S(1)} %get-tuple-element.91), channel_id=1, source_target_pairs={{0,14},{2,8},{4,10},{6,12},{1,15},{3,9},{5,11},{7,13},{8,22},{10,1... | collective-permute-start | bytes 122888 | tf_op jit(solution)/shard_map/ppermute | solution.py:485
  37.0 7.4 %collective-permute-start.10 = (bf16[352,128]{1,0:T(8,128)(2,1)S(1)}, bf16[352,128]{1,0:T(8,128)(2,1)S(1)}, u32[]{:S(2)}, u32[]{:S(2)}) collective-permute-start(bf16[352,128]{1,0:T(8,128)(2,1)S(1)} %get-tuple-element.96), channel_id=1, source_target_pairs={{0,2},{2,4},{4,6},{6,0},{1,3},{3,5},{5,7},{7,1},{8,10},{10,12},{12... | collective-permute-start | bytes 270344 | tf_op jit(solution)/shard_map/ppermute | solution.py:469
  38.7 5.8 %collective-permute-start.11 = (bf16[352,128]{1,0:T(8,128)(2,1)S(1)}, bf16[352,128]{1,0:T(8,128)(2,1)S(1)}, u32[]{:S(2)}, u32[]{:S(2)}) collective-permute-start(bf16[352,128]{1,0:T(8,128)(2,1)S(1)} %get-tuple-element.97), channel_id=1, source_target_pairs={{0,6},{2,0},{4,2},{6,4},{1,7},{3,1},{5,3},{7,5},{8,14},{10,8},{12,... | collective-permute-start | bytes 270344 | tf_op jit(solution)/shard_map/ppermute | solution.py:469
  48.7 6.8 %collective-permute-start.13 = (bf16[352,128]{1,0:T(8,128)(2,1)S(1)}, bf16[352,128]{1,0:T(8,128)(2,1)S(1)}, u32[]{:S(2)}, u32[]{:S(2)}) collective-permute-start(bf16[352,128]{1,0:T(8,128)(2,1)S(1)} %get-tuple-element.102), channel_id=1, source_target_pairs={{0,2},{2,4},{4,6},{6,0},{1,3},{3,5},{5,7},{7,1},{8,10},{10,12},{12... | collective-permute-start | bytes 270344 | tf_op jit(solution)/shard_map/ppermute | solution.py:469
  49.1 6.4 %collective-permute-start.14 = (bf16[352,128]{1,0:T(8,128)(2,1)S(1)}, bf16[352,128]{1,0:T(8,128)(2,1)S(1)}, u32[]{:S(2)}, u32[]{:S(2)}) collective-permute-start(bf16[352,128]{1,0:T(8,128)(2,1)S(1)} %get-tuple-element.103), channel_id=1, source_target_pairs={{0,6},{2,0},{4,2},{6,4},{1,7},{3,1},{5,3},{7,5},{8,14},{10,8},{12,... | collective-permute-start | bytes 270344 | tf_op jit(solution)/shard_map/ppermute | solution.py:469
  59.7 6.7 %collective-permute-start.16 = (bf16[352,128]{1,0:T(8,128)(2,1)S(1)}, bf16[352,128]{1,0:T(8,128)(2,1)S(1)}, u32[]{:S(2)}, u32[]{:S(2)}) collective-permute-start(bf16[352,128]{1,0:T(8,128)(2,1)S(1)} %get-tuple-element.106), channel_id=1, source_target_pairs={{0,2},{2,4},{4,6},{6,0},{1,3},{3,5},{5,7},{7,1},{8,10},{10,12},{12... | collective-permute-start | bytes 270344 | tf_op jit(solution)/shard_map/ppermute | solution.py:469
  59.8 6.7 %collective-permute-start.17 = (bf16[352,128]{1,0:T(8,128)(2,1)S(1)}, bf16[352,128]{1,0:T(8,128)(2,1)S(1)}, u32[]{:S(2)}, u32[]{:S(2)}) collective-permute-start(bf16[352,128]{1,0:T(8,128)(2,1)S(1)} %get-tuple-element.107), channel_id=1, source_target_pairs={{0,6},{2,0},{4,2},{6,4},{1,7},{3,1},{5,3},{7,5},{8,14},{10,8},{12,... | collective-permute-start | bytes 270344 | tf_op jit(solution)/shard_map/ppermute | solution.py:469
  70.8 17.8 %collective-permute-start.25 = (bf16[320,1024]{1,0:T(8,128)(2,1)S(1)}, bf16[320,1024]{1,0:T(8,128)(2,1)S(1)}, u32[]{:S(2)}, u32[]{:S(2)}) collective-permute-start(bf16[320,1024]{1,0:T(8,128)(2,1)S(1)} %get-tuple-element.109.own), channel_id=1, source_target_pairs={{0,8},{2,10},{4,12},{6,14},{1,9},{3,11},{5,13},{7,15},{8,16},{10,1... | collective-permute-start | bytes 1966088 | tf_op jit(solution)/shard_map/ppermute | solution.py:477
  70.9 6.7 %collective-permute-start.19 = (bf16[352,128]{1,0:T(8,128)(2,1)S(1)}, bf16[352,128]{1,0:T(8,128)(2,1)S(1)}, u32[]{:S(2)}, u32[]{:S(2)}) collective-permute-start(bf16[352,128]{1,0:T(8,128)(2,1)S(1)} %get-tuple-element.110), channel_id=1, source_target_pairs={{0,2},{2,4},{4,6},{6,0},{1,3},{3,5},{5,7},{7,1},{8,10},{10,12},{12... | collective-permute-start | bytes 270344 | tf_op jit(solution)/shard_map/ppermute | solution.py:469
  71.0 6.7 %collective-permute-start.20 = (bf16[352,128]{1,0:T(8,128)(2,1)S(1)}, bf16[352,128]{1,0:T(8,128)(2,1)S(1)}, u32[]{:S(2)}, u32[]{:S(2)}) collective-permute-start(bf16[352,128]{1,0:T(8,128)(2,1)S(1)} %get-tuple-element.111), channel_id=1, source_target_pairs={{0,6},{2,0},{4,2},{6,4},{1,7},{3,1},{5,3},{7,5},{8,14},{10,8},{12,... | collective-permute-start | bytes 270344 | tf_op jit(solution)/shard_map/ppermute | solution.py:469
  78.8 9.8 %collective-permute-start.26 = (bf16[512,256]{1,0:T(8,128)(2,1)S(1)}, bf16[512,256]{1,0:T(8,128)(2,1)S(1)}, u32[]{:S(2)}, u32[]{:S(2)}) collective-permute-start(bf16[512,256]{1,0:T(8,128)(2,1)S(1)} %get-tuple-element.115), channel_id=1, source_target_pairs={{0,8},{2,10},{4,12},{6,14},{1,9},{3,11},{5,13},{7,15},{8,16},{10,1... | collective-permute-start | bytes 786440 | tf_op jit(solution)/shard_map/ppermute | solution.py:477
  79.2 6.5 %collective-permute-start.22 = (f32[4,1280]{1,0:T(4,128)S(1)}, f32[4,1280]{1,0:T(4,128)S(1)}, u32[]{:S(2)}, u32[]{:S(2)}) collective-permute-start(f32[4,1280]{1,0:T(4,128)S(1)} %get-tuple-element.113), channel_id=1, source_target_pairs={{0,10},{2,12},{4,14},{6,8},{1,11},{3,13},{5,15},{7,9},{8,18},{10,2... | collective-permute-start | bytes 61448 | tf_op jit(solution)/shard_map/ppermute | solution.py:485
  79.2 6.7 %collective-permute-start.23 = (f32[4,1280]{1,0:T(4,128)S(1)}, f32[4,1280]{1,0:T(4,128)S(1)}, u32[]{:S(2)}, u32[]{:S(2)}) collective-permute-start(f32[4,1280]{1,0:T(4,128)S(1)} %get-tuple-element.113), channel_id=1, source_target_pairs={{0,12},{2,14},{4,8},{6,10},{1,13},{3,15},{5,9},{7,11},{8,20},{10,2... | collective-permute-start | bytes 61448 | tf_op jit(solution)/shard_map/ppermute | solution.py:485
  84.1 4.5 %collective-permute-start.24 = (f32[4,1280]{1,0:T(4,128)S(1)}, f32[4,1280]{1,0:T(4,128)S(1)}, u32[]{:S(2)}, u32[]{:S(2)}) collective-permute-start(f32[4,1280]{1,0:T(4,128)S(1)} %get-tuple-element.113), channel_id=1, source_target_pairs={{0,14},{2,8},{4,10},{6,12},{1,15},{3,9},{5,11},{7,13},{8,22},{10,1... | collective-permute-start | bytes 61448 | tf_op jit(solution)/shard_map/ppermute | solution.py:485
  95.2 6.7 %collective-permute-start.27 = (bf16[352,128]{1,0:T(8,128)(2,1)S(1)}, bf16[352,128]{1,0:T(8,128)(2,1)S(1)}, u32[]{:S(2)}, u32[]{:S(2)}) collective-permute-start(bf16[352,128]{1,0:T(8,128)(2,1)S(1)} %get-tuple-element.117), channel_id=1, source_target_pairs={{0,2},{2,4},{4,6},{6,0},{1,3},{3,5},{5,7},{7,1},{8,10},{10,12},{12... | collective-permute-start | bytes 270344 | tf_op jit(solution)/shard_map/ppermute | solution.py:469
  96.7 5.2 %collective-permute-start.28 = (bf16[352,128]{1,0:T(8,128)(2,1)S(1)}, bf16[352,128]{1,0:T(8,128)(2,1)S(1)}, u32[]{:S(2)}, u32[]{:S(2)}) collective-permute-start(bf16[352,128]{1,0:T(8,128)(2,1)S(1)} %get-tuple-element.118), channel_id=1, source_target_pairs={{0,6},{2,0},{4,2},{6,4},{1,7},{3,1},{5,3},{7,5},{8,14},{10,8},{12,... | collective-permute-start | bytes 270344 | tf_op jit(solution)/shard_map/ppermute | solution.py:469
  106.2 7.2 %collective-permute-start.30 = (bf16[352,128]{1,0:T(8,128)(2,1)S(1)}, bf16[352,128]{1,0:T(8,128)(2,1)S(1)}, u32[]{:S(2)}, u32[]{:S(2)}) collective-permute-start(bf16[352,128]{1,0:T(8,128)(2,1)S(1)} %get-tuple-element.122), channel_id=1, source_target_pairs={{0,2},{2,4},{4,6},{6,0},{1,3},{3,5},{5,7},{7,1},{8,10},{10,12},{12... | collective-permute-start | bytes 270344 | tf_op jit(solution)/shard_map/ppermute | solution.py:469
  106.4 6.9 %collective-permute-start.31 = (bf16[352,128]{1,0:T(8,128)(2,1)S(1)}, bf16[352,128]{1,0:T(8,128)(2,1)S(1)}, u32[]{:S(2)}, u32[]{:S(2)}) collective-permute-start(bf16[352,128]{1,0:T(8,128)(2,1)S(1)} %get-tuple-element.123), channel_id=1, source_target_pairs={{0,6},{2,0},{4,2},{6,4},{1,7},{3,1},{5,3},{7,5},{8,14},{10,8},{12,... | collective-permute-start | bytes 270344 | tf_op jit(solution)/shard_map/ppermute | solution.py:469
  117.5 21.6 %collective-permute-start.33 = (bf16[352,128]{1,0:T(8,128)(2,1)S(1)}, bf16[352,128]{1,0:T(8,128)(2,1)S(1)}, u32[]{:S(2)}, u32[]{:S(2)}) collective-permute-start(bf16[352,128]{1,0:T(8,128)(2,1)S(1)} %get-tuple-element.126), channel_id=1, source_target_pairs={{0,2},{2,4},{4,6},{6,0},{1,3},{3,5},{5,7},{7,1},{8,10},{10,12},{12... | collective-permute-start | bytes 270344 | tf_op jit(solution)/shard_map/ppermute | solution.py:469
  118.6 20.5 %collective-permute-start.34 = (bf16[352,128]{1,0:T(8,128)(2,1)S(1)}, bf16[352,128]{1,0:T(8,128)(2,1)S(1)}, u32[]{:S(2)}, u32[]{:S(2)}) collective-permute-start(bf16[352,128]{1,0:T(8,128)(2,1)S(1)} %get-tuple-element.127), channel_id=1, source_target_pairs={{0,6},{2,0},{4,2},{6,4},{1,7},{3,1},{5,3},{7,5},{8,14},{10,8},{12,... | collective-permute-start | bytes 270344 | tf_op jit(solution)/shard_map/ppermute | solution.py:469
  120.8 15.3 %collective-permute-start.36 = (f32[4,512]{1,0:T(4,128)S(1)}, f32[4,512]{1,0:T(4,128)S(1)}, u32[]{:S(2)}, u32[]{:S(2)}) collective-permute-start(f32[4,512]{1,0:T(4,128)S(1)} %get-tuple-element.130), channel_id=1, source_target_pairs={{0,1},{1,0},{2,3},{3,2},{4,5},{5,4},{6,7},{7,6},{8,9},{9,8},{10,11... | collective-permute-start | bytes 24584 | tf_op jit(solution)/shard_map/ppermute | solution.py:458
  136.7 6.1 %collective-permute-start.37 = (f32[8,512]{1,0:T(8,128)S(1)}, f32[8,512]{1,0:T(8,128)S(1)}, u32[]{:S(2)}, u32[]{:S(2)}) collective-permute-start(f32[8,512]{1,0:T(8,128)S(1)} %shard_map.164), channel_id=1, source_target_pairs={{0,8},{8,16},{16,24},{24,0},{1,9},{9,17},{17,25},{25,1},{2,10},{10... | collective-permute-start | bytes 49160 | tf_op jit(solution)/shard_map/ppermute | solution.py:642
  136.7 6.0 %collective-permute-start.38 = (f32[8,512]{1,0:T(8,128)S(1)}, f32[8,512]{1,0:T(8,128)S(1)}, u32[]{:S(2)}, u32[]{:S(2)}) collective-permute-start(f32[8,512]{1,0:T(8,128)S(1)} %shard_map.164), channel_id=1, source_target_pairs={{0,16},{8,24},{16,0},{24,8},{1,17},{9,25},{17,1},{25,9},{2,18},{10... | collective-permute-start | bytes 49160 | tf_op jit(solution)/shard_map/ppermute | solution.py:642
  138.7 4.1 %collective-permute-start.39 = (f32[8,512]{1,0:T(8,128)S(1)}, f32[8,512]{1,0:T(8,128)S(1)}, u32[]{:S(2)}, u32[]{:S(2)}) collective-permute-start(f32[8,512]{1,0:T(8,128)S(1)} %shard_map.164), channel_id=1, source_target_pairs={{0,24},{8,0},{16,8},{24,16},{1,25},{9,1},{17,9},{25,17},{2,26},{10... | collective-permute-start | bytes 49160 | tf_op jit(solution)/shard_map/ppermute | solution.py:642
  (24 other events, 167.5 us)

commit v4 on v3

--- a/solution.py
+++ b/solution.py
@@ -668,9 +668,13 @@
 
     own, *shares = lax.optimization_barrier((own, *shares))
     low, high = own[:, :half], own[:, half:]
-    mine = jnp.where(first_core, low, high)
-    other = swap(jnp.where(first_core, high, low))
-    pair = jnp.where(first_core, jnp.stack([mine, other]), jnp.stack([other, mine]))
+    other = swap(own)
+    pair = jnp.stack(
+        [
+            jnp.where(first_core, low, other[:, half:]),
+            jnp.where(first_core, other[:, :half], high),
+        ]
+    )
     features_out = pair.reshape(1, batch, chans, own_rows, cols)
     share = cols // sections
     latent_out = None

time: 147 us -> 148 us (level)
  no operation moved by 1% of the time
where the time goes in v4:
time: 148 us; the launch traced here: 147 us
  starting transfers between devices  62.6 us (42%)
  Pallas kernels  43.9 us (30%)
  waiting for transfers between devices  31.8 us (21%)
  other arithmetic  3.86 us (3%)
  local copies, waits for them, and re-layouts  3.15 us (2%)
  between operations  1.8 us (1%)
    ppermute x24, starting transfers between devices, around(): lax.ppermute(x, 'patch', [(layout(m, l), layout(m, l + by)) for m, l in b...  30.2 us
    pallas_call x6, Pallas kernels, conv(): call(functools.partial(conv_kernel, index, base is not None, last), (half...  24.9 us
    ppermute x24, waiting for transfers between devices, around(): lax.ppermute(x, 'patch', [(layout(m, l), layout(m, l + by)) for m, l in b...  24.4 us
    ppermute x4, starting transfers between devices, swap(): return lax.ppermute(x, 'patch', swap_pairs)  16.5 us
    pallas_call x2, Pallas kernels, per_device(): call(functools.partial(first_kernel, step, chips), (wide_shape, half_shap...  13.1 us
    ppermute x6, starting transfers between devices, to_first(): return lax.ppermute(x, joint, pairs)  11.2 us
    ppermute x4, starting transfers between devices, onward(): return lax.ppermute(x, joint, pairs)  4.15 us
    ppermute x4, waiting for transfers between devices, swap(): return lax.ppermute(x, 'patch', swap_pairs)  4.05 us
  transfers between devices with their start and end apart: 41, of which 15 were waited for; matrix products, arithmetic and copies ran while one was open for 1% of the time, Pallas kernels for 7%

profile of v4, /device:TPU:1, one launch (start us, length us, event | category | flops | bytes accessed | tf_op | source)
XLA Modules:
  0.0 147.0 jit_solution(8656617666108781255)
XLA Ops:
  0.8 2.3 %collective-permute-done = bf16[2,320,4,128]{3,2,1,0:T(4,128)(2,1)S(1)} collective-permute-done((bf16[2,320,4,128]{3,2,1,0:T(4,128)(2,1)}, bf16[2,320,4,128]{3,2,1,0:T(4,128)(2,1)S(1)}, u32[]{:S(2)}, u32[]{:S(2)}) %collective-permute-start) | collective-permute-done | bytes 655392 | tf_op jit(solution)/shard_map/ppermute | solution.py:458
  5.0 2.4 %collective-permute-start.8 = (bf16[320,1024]{1,0:T(8,128)(2,1)S(1)}, bf16[320,1024]{1,0:T(8,128)(2,1)S(1)}, u32[]{:S(2)}, u32[]{:S(2)}) collective-permute-start(bf16[320,1024]{1,0:T(8,128)(2,1)S(1)} %bitcast.62), channel_id=1, source_target_pairs={{0,8},{2,10},{4,12},{6,14},{1,9},{3,11},{5,13},{7,15},{8,16},{10,1... | collective-permute-start | bytes 1966088 | tf_op jit(solution)/shard_map/ppermute | solution.py:477
  8.2 2.4 %collective-permute-start.3 = (bf16[32,128]{1,0:T(8,128)(2,1)S(1)}, bf16[32,128]{1,0:T(8,128)(2,1)S(1)}, u32[]{:S(2)}, u32[]{:S(2)}) collective-permute-start(bf16[32,128]{1,0:T(8,128)(2,1)S(1)} %get-tuple-element.81.rest_0_), channel_id=1, source_target_pairs={{0,4},{2,6},{4,0},{6,2},{1,5},{3,7},{5,1},{7,3},{8,12},{10,14},{12... | collective-permute-start | bytes 24584 | tf_op jit(solution)/shard_map/ppermute | solution.py:469
  13.2 2.0 %collective-permute-start.2 = (bf16[352,128]{1,0:T(8,128)(2,1)S(1)}, bf16[352,128]{1,0:T(8,128)(2,1)S(1)}, u32[]{:S(2)}, u32[]{:S(2)}) collective-permute-start(bf16[352,128]{1,0:T(8,128)(2,1)S(1)} %get-tuple-element.88), channel_id=1, source_target_pairs={{0,6},{2,0},{4,2},{6,4},{1,7},{3,1},{5,3},{7,5},{8,14},{10,8},{12,... | collective-permute-start | bytes 270344 | tf_op jit(solution)/shard_map/ppermute | solution.py:469
  15.3 2.7 %collective-permute-done.1.up = bf16[352,128]{1,0:T(8,128)(2,1)S(1)} collective-permute-done((bf16[352,128]{1,0:T(8,128)(2,1)S(1)}, bf16[352,128]{1,0:T(8,128)(2,1)S(1)}, u32[]{:S(2)}, u32[]{:S(2)}) %collective-permute-start.1) | collective-permute-done | bytes 90144 | tf_op jit(solution)/shard_map/ppermute | solution.py:469
  24.4 2.3 %collective-permute-start.7 = (f32[8,1280]{1,0:T(8,128)S(1)}, f32[8,1280]{1,0:T(8,128)S(1)}, u32[]{:S(2)}, u32[]{:S(2)}) collective-permute-start(f32[8,1280]{1,0:T(8,128)S(1)} %get-tuple-element.91), channel_id=1, source_target_pairs={{0,14},{2,8},{4,10},{6,12},{1,15},{3,9},{5,11},{7,13},{8,22},{10,1... | collective-permute-start | bytes 122888 | tf_op jit(solution)/shard_map/ppermute | solution.py:485
  27.6 2.3 %copy-done = bf16[1,2,9,320,320]{4,3,2,1,0:T(8,128)(2,1)S(1)} copy-done((bf16[1,2,9,320,320]{4,3,2,1,0:T(8,128)(2,1)S(1)}, bf16[1,2,9,320,320]{4,3,2,1,0:T(8,128)(2,1)}, u32[]{:S(2)}) %copy-start) | copy-done | bytes 3686424
  30.6 6.5 %shard_map.152 = (f32[320,1024]{1,0:T(8,128)S(1)}, bf16[320,1024]{1,0:T(8,128)(2,1)S(1)}, f32[8,4096]{1,0:T(8,128)S(1)}, f32[4,512]{1,0:T(4,128)}, f32[4,512]{1,...) custom-call(s32[7]{0:T(128)S(1)} %stack.56.ints, ...), custom_call_target="tpu_custom_call" | custom-call | flops 1887436800 | bytes 4000000 | tf_op jit(solution)/shard_map/pallas_call | solution.py:601
  38.7 2.0 %collective-permute-start.11 = (bf16[352,128]{1,0:T(8,128)(2,1)S(1)}, bf16[352,128]{1,0:T(8,128)(2,1)S(1)}, u32[]{:S(2)}, u32[]{:S(2)}) collective-permute-start(bf16[352,128]{1,0:T(8,128)(2,1)S(1)} %get-tuple-element.97), channel_id=1, source_target_pairs={{0,6},{2,0},{4,2},{6,4},{1,7},{3,1},{5,3},{7,5},{8,14},{10,8},{12,... | collective-permute-start | bytes 270344 | tf_op jit(solution)/shard_map/ppermute | solution.py:469
  42.1 2.3 %collective-permute-done.12.rest_2_ = bf16[32,128]{1,0:T(8,128)(2,1)S(1)} collective-permute-done((bf16[32,128]{1,0:T(8,128)(2,1)S(1)}, bf16[32,128]{1,0:T(8,128)(2,1)S(1)}, u32[]{:S(2)}, u32[]{:S(2)}) %collective-permute-start.12) | collective-permute-done | bytes 8224 | tf_op jit(solution)/shard_map/ppermute | solution.py:469
  44.5 4.2 %shard_map.154 = (bf16[320,1024]{1,0:T(8,128)(2,1)S(1)}, bf16[352,128]{1,0:T(8,128)(2,1)S(1)}, bf16[352,128]{1,0:T(8,128)(2,1)S(1)}, bf16[32,128]{1,0:T(8,128)(2,1)S(1)}) custom-call(s32[7]{0:T(128)S(1)} %stack.56.ints, f32[320,16]{1,0:T(8,128)S(1)} %bitcast.67, f32[320,1024]{1,0:T(8,128)S(1)} %get-tuple-element.95.own, ...), custom_call_target="tpu_custom_call" | custom-call | flops 1887436800 | bytes 4000000 | tf_op jit(solution)/shard_map/pallas_call | solution.py:651
  49.1 2.9 %collective-permute-start.14 = (bf16[352,128]{1,0:T(8,128)(2,1)S(1)}, bf16[352,128]{1,0:T(8,128)(2,1)S(1)}, u32[]{:S(2)}, u32[]{:S(2)}) collective-permute-start(bf16[352,128]{1,0:T(8,128)(2,1)S(1)} %get-tuple-element.103), channel_id=1, source_target_pairs={{0,6},{2,0},{4,2},{6,4},{1,7},{3,1},{5,3},{7,5},{8,14},{10,8},{12,... | collective-permute-start | bytes 270344 | tf_op jit(solution)/shard_map/ppermute | solution.py:469
  52.6 2.9 %collective-permute-done.15.rest_1_ = bf16[32,128]{1,0:T(8,128)(2,1)S(1)} collective-permute-done((bf16[32,128]{1,0:T(8,128)(2,1)S(1)}, bf16[32,128]{1,0:T(8,128)(2,1)S(1)}, u32[]{:S(2)}, u32[]{:S(2)}) %collective-permute-start.15) | collective-permute-done | bytes 8224 | tf_op jit(solution)/shard_map/ppermute | solution.py:469
  55.6 4.1 %shard_map.156 = (f32[320,1024]{1,0:T(8,128)S(1)}, bf16[352,128]{1,0:T(8,128)(2,1)S(1)}, bf16[352,128]{1,0:T(8,128)(2,1)S(1)}, bf16[32,128]{1,0:T(8,128)(2,1)S(1)}) custom-call(s32[7]{0:T(128)S(1)} %stack.56.ints, f32[320,16]{1,0:T(8,128)S(1)} %bitcast.68, bf16[320,1024]{1,0:T(8,128)(2,1)S(1)} %get-tuple-element.101.own.rest_0_, ...), custom_call_target="tpu_custom_call" | custom-call | flops 1887436800 | bytes 4000000 | tf_op jit(solution)/shard_map/pallas_call | solution.py:651
  59.8 3.3 %collective-permute-start.17 = (bf16[352,128]{1,0:T(8,128)(2,1)S(1)}, bf16[352,128]{1,0:T(8,128)(2,1)S(1)}, u32[]{:S(2)}, u32[]{:S(2)}) collective-permute-start(bf16[352,128]{1,0:T(8,128)(2,1)S(1)} %get-tuple-element.107), channel_id=1, source_target_pairs={{0,6},{2,0},{4,2},{6,4},{1,7},{3,1},{5,3},{7,5},{8,14},{10,8},{12,... | collective-permute-start | bytes 270344 | tf_op jit(solution)/shard_map/ppermute | solution.py:469
  63.6 2.8 %collective-permute-done.18.rest_2_ = bf16[32,128]{1,0:T(8,128)(2,1)S(1)} collective-permute-done((bf16[32,128]{1,0:T(8,128)(2,1)S(1)}, bf16[32,128]{1,0:T(8,128)(2,1)S(1)}, u32[]{:S(2)}, u32[]{:S(2)}) %collective-permute-start.18) | collective-permute-done | bytes 8224 | tf_op jit(solution)/shard_map/ppermute | solution.py:469
  66.4 4.4 %shard_map.158 = (bf16[320,1024]{1,0:T(8,128)(2,1)S(1)}, bf16[352,128]{1,0:T(8,128)(2,1)S(1)}, bf16[352,128]{1,0:T(8,128)(2,1)S(1)}, bf16[32,128]{1,0:T(8,128)(2,1)S(1)}) custom-call(s32[7]{0:T(128)S(1)} %stack.56.ints, f32[320,16]{1,0:T(8,128)S(1)} %bitcast.69, f32[320,1024]{1,0:T(8,128)S(1)} %get-tuple-element.105.own, ...), custom_call_target="tpu_custom_call" | custom-call | flops 1887436800 | bytes 4000000 | tf_op jit(solution)/shard_map/pallas_call | solution.py:651
  71.0 3.3 %collective-permute-start.20 = (bf16[352,128]{1,0:T(8,128)(2,1)S(1)}, bf16[352,128]{1,0:T(8,128)(2,1)S(1)}, u32[]{:S(2)}, u32[]{:S(2)}) collective-permute-start(bf16[352,128]{1,0:T(8,128)(2,1)S(1)} %get-tuple-element.111), channel_id=1, source_target_pairs={{0,6},{2,0},{4,2},{6,4},{1,7},{3,1},{5,3},{7,5},{8,14},{10,8},{12,... | collective-permute-start | bytes 270344 | tf_op jit(solution)/shard_map/ppermute | solution.py:469
  74.2 3.4 %collective-permute-done.21.rest_1_ = bf16[32,128]{1,0:T(8,128)(2,1)S(1)} collective-permute-done((bf16[32,128]{1,0:T(8,128)(2,1)S(1)}, bf16[32,128]{1,0:T(8,128)(2,1)S(1)}, u32[]{:S(2)}, u32[]{:S(2)}) %collective-permute-start.21) | collective-permute-done | bytes 8224 | tf_op jit(solution)/shard_map/ppermute | solution.py:469
  79.2 4.9 %collective-permute-start.23 = (f32[4,1280]{1,0:T(4,128)S(1)}, f32[4,1280]{1,0:T(4,128)S(1)}, u32[]{:S(2)}, u32[]{:S(2)}) collective-permute-start(f32[4,1280]{1,0:T(4,128)S(1)} %get-tuple-element.113), channel_id=1, source_target_pairs={{0,12},{2,14},{4,8},{6,10},{1,13},{3,15},{5,9},{7,11},{8,20},{10,2... | collective-permute-start | bytes 61448 | tf_op jit(solution)/shard_map/ppermute | solution.py:485
  86.0 2.7 %collective-permute-done.24.rest_2_ = f32[4,1280]{1,0:T(4,128)S(1)} collective-permute-done((f32[4,1280]{1,0:T(4,128)S(1)}, f32[4,1280]{1,0:T(4,128)S(1)}, u32[]{:S(2)}, u32[]{:S(2)}) %collective-permute-start.24) | collective-permute-done | bytes 20512 | tf_op jit(solution)/shard_map/ppermute | solution.py:485
  88.6 6.6 %shard_map.160 = (f32[320,1024]{1,0:T(8,128)S(1)}, bf16[320,1024]{1,0:T(8,128)(2,1)S(1)}, f32[8,4096]{1,0:T(8,128)}, f32[4,512]{1,0:T(4,128)S(1)}, f32[4,512]{1,...) custom-call(s32[7]{0:T(128)S(1)} %stack.56.ints, ...), custom_call_target="tpu_custom_call" | custom-call | flops 1887436800 | bytes 4000000 | tf_op jit(solution)/shard_map/pallas_call | solution.py:601
  96.7 1.8 %collective-permute-start.28 = (bf16[352,128]{1,0:T(8,128)(2,1)S(1)}, bf16[352,128]{1,0:T(8,128)(2,1)S(1)}, u32[]{:S(2)}, u32[]{:S(2)}) collective-permute-start(bf16[352,128]{1,0:T(8,128)(2,1)S(1)} %get-tuple-element.118), channel_id=1, source_target_pairs={{0,6},{2,0},{4,2},{6,4},{1,7},{3,1},{5,3},{7,5},{8,14},{10,8},{12,... | collective-permute-start | bytes 270344 | tf_op jit(solution)/shard_map/ppermute | solution.py:469
  98.6 3.3 %collective-permute-done.29.rest_2_ = bf16[32,128]{1,0:T(8,128)(2,1)S(1)} collective-permute-done((bf16[32,128]{1,0:T(8,128)(2,1)S(1)}, bf16[32,128]{1,0:T(8,128)(2,1)S(1)}, u32[]{:S(2)}, u32[]{:S(2)}) %collective-permute-start.29) | collective-permute-done | bytes 8224 | tf_op jit(solution)/shard_map/ppermute | solution.py:469
  101.9 4.3 %shard_map.161 = (bf16[320,1024]{1,0:T(8,128)(2,1)S(1)}, bf16[352,128]{1,0:T(8,128)(2,1)S(1)}, bf16[352,128]{1,0:T(8,128)(2,1)S(1)}, bf16[32,128]{1,0:T(8,128)(2,1)S(1)}) custom-call(s32[7]{0:T(128)S(1)} %stack.56.ints, f32[320,16]{1,0:T(8,128)S(1)} %bitcast.72, f32[320,1024]{1,0:T(8,128)S(1)} %get-tuple-element.116.own, ...), custom_call_target="tpu_custom_call" | custom-call | flops 1887436800 | bytes 4000000 | tf_op jit(solution)/shard_map/pallas_call | solution.py:651
  106.4 3.1 %collective-permute-start.31 = (bf16[352,128]{1,0:T(8,128)(2,1)S(1)}, bf16[352,128]{1,0:T(8,128)(2,1)S(1)}, u32[]{:S(2)}, u32[]{:S(2)}) collective-permute-start(bf16[352,128]{1,0:T(8,128)(2,1)S(1)} %get-tuple-element.123), channel_id=1, source_target_pairs={{0,6},{2,0},{4,2},{6,4},{1,7},{3,1},{5,3},{7,5},{8,14},{10,8},{12,... | collective-permute-start | bytes 270344 | tf_op jit(solution)/shard_map/ppermute | solution.py:469
  109.5 3.8 %collective-permute-done.32.rest_1_ = bf16[32,128]{1,0:T(8,128)(2,1)S(1)} collective-permute-done((bf16[32,128]{1,0:T(8,128)(2,1)S(1)}, bf16[32,128]{1,0:T(8,128)(2,1)S(1)}, u32[]{:S(2)}, u32[]{:S(2)}) %collective-permute-start.32) | collective-permute-done | bytes 8224 | tf_op jit(solution)/shard_map/ppermute | solution.py:469
  113.3 4.2 %shard_map.162 = (f32[320,1024]{1,0:T(8,128)S(1)}, bf16[352,128]{1,0:T(8,128)(2,1)S(1)}, bf16[352,128]{1,0:T(8,128)(2,1)S(1)}, bf16[32,128]{1,0:T(8,128)(2,1)S(1)}) custom-call(s32[7]{0:T(128)S(1)} %stack.56.ints, f32[320,16]{1,0:T(8,128)S(1)} %bitcast.73, bf16[320,1024]{1,0:T(8,128)(2,1)S(1)} %get-tuple-element.121.own.rest_0_, ...), custom_call_target="tpu_custom_call" | custom-call | flops 1887436800 | bytes 4000000 | tf_op jit(solution)/shard_map/pallas_call | solution.py:651
  118.6 2.2 %collective-permute-start.34 = (bf16[352,128]{1,0:T(8,128)(2,1)S(1)}, bf16[352,128]{1,0:T(8,128)(2,1)S(1)}, u32[]{:S(2)}, u32[]{:S(2)}) collective-permute-start(bf16[352,128]{1,0:T(8,128)(2,1)S(1)} %get-tuple-element.127), channel_id=1, source_target_pairs={{0,6},{2,0},{4,2},{6,4},{1,7},{3,1},{5,3},{7,5},{8,14},{10,8},{12,... | collective-permute-start | bytes 270344 | tf_op jit(solution)/shard_map/ppermute | solution.py:469
  120.8 14.4 %collective-permute-start.36 = (f32[4,512]{1,0:T(4,128)S(1)}, f32[4,512]{1,0:T(4,128)S(1)}, u32[]{:S(2)}, u32[]{:S(2)}) collective-permute-start(f32[4,512]{1,0:T(4,128)S(1)} %get-tuple-element.130), channel_id=1, source_target_pairs={{0,1},{1,0},{2,3},{3,2},{4,5},{5,4},{6,7},{7,6},{8,9},{9,8},{10,11... | collective-permute-start | bytes 24584 | tf_op jit(solution)/shard_map/ppermute | solution.py:458
  136.8 1.9 %collective-permute-done.35.rest_2_ = bf16[32,128]{1,0:T(8,128)(2,1)S(1)} collective-permute-done((bf16[32,128]{1,0:T(8,128)(2,1)S(1)}, bf16[32,128]{1,0:T(8,128)(2,1)S(1)}, u32[]{:S(2)}, u32[]{:S(2)}) %collective-permute-start.35) | collective-permute-done | bytes 8224 | tf_op jit(solution)/shard_map/ppermute | solution.py:469
  139.1 3.7 %shard_map.163 = bf16[320,1024]{1,0:T(8,128)(2,1)S(1)} custom-call(s32[7]{0:T(128)S(1)} %stack.56.ints, f32[320,16]{1,0:T(8,128)S(1)} %bitcast.74, f32[320,1024]{1,0:T(8,128)S(1)} %get-tuple-element.125.own, bf16[352,128]{1,0:T(8,128)(2,1)S(1)} %collective-permute-done.33.up, bf16[352,128]{1,0:T(8,128)(2,1)S(1)} %collective-permute-done.34.down, ...), custom_call_target="tpu_custom_call" | custom-call | flops 1887436800 | bytes 4000000 | tf_op jit(solution)/shard_map/pallas_call | solution.py:651
  (127 shorter events, 30.1 us)
Async XLA Ops:
  5.0 25.5 %collective-permute-start.8 = (bf16[320,1024]{1,0:T(8,128)(2,1)S(1)}, bf16[320,1024]{1,0:T(8,128)(2,1)S(1)}, u32[]{:S(2)}, u32[]{:S(2)}) collective-permute-start(bf16[320,1024]{1,0:T(8,128)(2,1)S(1)} %bitcast.62), channel_id=1, source_target_pairs={{0,8},{2,10},{4,12},{6,14},{1,9},{3,11},{5,13},{7,15},{8,16},{10,1... | collective-permute-start | bytes 1966088 | tf_op jit(solution)/shard_map/ppermute | solution.py:477
  8.2 7.0 %collective-permute-start.3 = (bf16[32,128]{1,0:T(8,128)(2,1)S(1)}, bf16[32,128]{1,0:T(8,128)(2,1)S(1)}, u32[]{:S(2)}, u32[]{:S(2)}) collective-permute-start(bf16[32,128]{1,0:T(8,128)(2,1)S(1)} %get-tuple-element.81.rest_0_), channel_id=1, source_target_pairs={{0,4},{2,6},{4,0},{6,2},{1,5},{3,7},{5,1},{7,3},{8,12},{10,14},{12... | collective-permute-start | bytes 24584 | tf_op jit(solution)/shard_map/ppermute | solution.py:469
  10.6 4.6 %collective-permute-start.4 = (f32[4,4,128]{2,1,0:T(4,128)S(1)}, f32[4,4,128]{2,1,0:T(4,128)S(1)}, u32[]{:S(2)}, u32[]{:S(2)}) collective-permute-start(f32[4,4,128]{2,1,0:T(4,128)S(1)} %dynamic-slice_bitcast_fusion), channel_id=1, source_target_pairs={{0,1},{1,0},{2,3},{3,2},{4,5},{5,4},{6,7},{7,6},{8,9},{9,8},{10,11... | collective-permute-start | bytes 24584 | tf_op jit(solution)/shard_map/ppermute | solution.py:458
  11.9 6.1 %collective-permute-start.1 = (bf16[352,128]{1,0:T(8,128)(2,1)S(1)}, bf16[352,128]{1,0:T(8,128)(2,1)S(1)}, u32[]{:S(2)}, u32[]{:S(2)}) collective-permute-start(bf16[352,128]{1,0:T(8,128)(2,1)S(1)} %get-tuple-element.87), channel_id=1, source_target_pairs={{0,2},{2,4},{4,6},{6,0},{1,3},{3,5},{5,7},{7,1},{8,10},{10,12},{12... | collective-permute-start | bytes 270344 | tf_op jit(solution)/shard_map/ppermute | solution.py:469
  13.2 6.0 %collective-permute-start.2 = (bf16[352,128]{1,0:T(8,128)(2,1)S(1)}, bf16[352,128]{1,0:T(8,128)(2,1)S(1)}, u32[]{:S(2)}, u32[]{:S(2)}) collective-permute-start(bf16[352,128]{1,0:T(8,128)(2,1)S(1)} %get-tuple-element.88), channel_id=1, source_target_pairs={{0,6},{2,0},{4,2},{6,4},{1,7},{3,1},{5,3},{7,5},{8,14},{10,8},{12,... | collective-permute-start | bytes 270344 | tf_op jit(solution)/shard_map/ppermute | solution.py:469
  20.3 10.2 %collective-permute-start.9 = (bf16[512,256]{1,0:T(8,128)(2,1)S(1)}, bf16[512,256]{1,0:T(8,128)(2,1)S(1)}, u32[]{:S(2)}, u32[]{:S(2)}) collective-permute-start(bf16[512,256]{1,0:T(8,128)(2,1)S(1)} %get-tuple-element.93), channel_id=1, source_target_pairs={{0,8},{2,10},{4,12},{6,14},{1,9},{3,11},{5,13},{7,15},{8,16},{10,1... | collective-permute-start | bytes 786440 | tf_op jit(solution)/shard_map/ppermute | solution.py:477
  21.6 8.9 %collective-permute-start.5 = (f32[8,1280]{1,0:T(8,128)S(1)}, f32[8,1280]{1,0:T(8,128)S(1)}, u32[]{:S(2)}, u32[]{:S(2)}) collective-permute-start(f32[8,1280]{1,0:T(8,128)S(1)} %get-tuple-element.91), channel_id=1, source_target_pairs={{0,10},{2,12},{4,14},{6,8},{1,11},{3,13},{5,15},{7,9},{8,18},{10,2... | collective-permute-start | bytes 122888 | tf_op jit(solution)/shard_map/ppermute | solution.py:485
  22.8 7.7 %collective-permute-start.6 = (f32[8,1280]{1,0:T(8,128)S(1)}, f32[8,1280]{1,0:T(8,128)S(1)}, u32[]{:S(2)}, u32[]{:S(2)}) collective-permute-start(f32[8,1280]{1,0:T(8,128)S(1)} %get-tuple-element.91), channel_id=1, source_target_pairs={{0,12},{2,14},{4,8},{6,10},{1,13},{3,15},{5,9},{7,11},{8,20},{10,2... | collective-permute-start | bytes 122888 | tf_op jit(solution)/shard_map/ppermute | solution.py:485
  24.4 6.1 %collective-permute-start.7 = (f32[8,1280]{1,0:T(8,128)S(1)}, f32[8,1280]{1,0:T(8,128)S(1)}, u32[]{:S(2)}, u32[]{:S(2)}) collective-permute-start(f32[8,1280]{1,0:T(8,128)S(1)} %get-tuple-element.91), channel_id=1, source_target_pairs={{0,14},{2,8},{4,10},{6,12},{1,15},{3,9},{5,11},{7,13},{8,22},{10,1... | collective-permute-start | bytes 122888 | tf_op jit(solution)/shard_map/ppermute | solution.py:485
  37.0 7.4 %collective-permute-start.10 = (bf16[352,128]{1,0:T(8,128)(2,1)S(1)}, bf16[352,128]{1,0:T(8,128)(2,1)S(1)}, u32[]{:S(2)}, u32[]{:S(2)}) collective-permute-start(bf16[352,128]{1,0:T(8,128)(2,1)S(1)} %get-tuple-element.96), channel_id=1, source_target_pairs={{0,2},{2,4},{4,6},{6,0},{1,3},{3,5},{5,7},{7,1},{8,10},{10,12},{12... | collective-permute-start | bytes 270344 | tf_op jit(solution)/shard_map/ppermute | solution.py:469
  38.7 5.8 %collective-permute-start.11 = (bf16[352,128]{1,0:T(8,128)(2,1)S(1)}, bf16[352,128]{1,0:T(8,128)(2,1)S(1)}, u32[]{:S(2)}, u32[]{:S(2)}) collective-permute-start(bf16[352,128]{1,0:T(8,128)(2,1)S(1)} %get-tuple-element.97), channel_id=1, source_target_pairs={{0,6},{2,0},{4,2},{6,4},{1,7},{3,1},{5,3},{7,5},{8,14},{10,8},{12,... | collective-permute-start | bytes 270344 | tf_op jit(solution)/shard_map/ppermute | solution.py:469
  48.7 6.8 %collective-permute-start.13 = (bf16[352,128]{1,0:T(8,128)(2,1)S(1)}, bf16[352,128]{1,0:T(8,128)(2,1)S(1)}, u32[]{:S(2)}, u32[]{:S(2)}) collective-permute-start(bf16[352,128]{1,0:T(8,128)(2,1)S(1)} %get-tuple-element.102), channel_id=1, source_target_pairs={{0,2},{2,4},{4,6},{6,0},{1,3},{3,5},{5,7},{7,1},{8,10},{10,12},{12... | collective-permute-start | bytes 270344 | tf_op jit(solution)/shard_map/ppermute | solution.py:469
  49.1 6.4 %collective-permute-start.14 = (bf16[352,128]{1,0:T(8,128)(2,1)S(1)}, bf16[352,128]{1,0:T(8,128)(2,1)S(1)}, u32[]{:S(2)}, u32[]{:S(2)}) collective-permute-start(bf16[352,128]{1,0:T(8,128)(2,1)S(1)} %get-tuple-element.103), channel_id=1, source_target_pairs={{0,6},{2,0},{4,2},{6,4},{1,7},{3,1},{5,3},{7,5},{8,14},{10,8},{12,... | collective-permute-start | bytes 270344 | tf_op jit(solution)/shard_map/ppermute | solution.py:469
  59.7 6.7 %collective-permute-start.16 = (bf16[352,128]{1,0:T(8,128)(2,1)S(1)}, bf16[352,128]{1,0:T(8,128)(2,1)S(1)}, u32[]{:S(2)}, u32[]{:S(2)}) collective-permute-start(bf16[352,128]{1,0:T(8,128)(2,1)S(1)} %get-tuple-element.106), channel_id=1, source_target_pairs={{0,2},{2,4},{4,6},{6,0},{1,3},{3,5},{5,7},{7,1},{8,10},{10,12},{12... | collective-permute-start | bytes 270344 | tf_op jit(solution)/shard_map/ppermute | solution.py:469
  59.8 6.7 %collective-permute-start.17 = (bf16[352,128]{1,0:T(8,128)(2,1)S(1)}, bf16[352,128]{1,0:T(8,128)(2,1)S(1)}, u32[]{:S(2)}, u32[]{:S(2)}) collective-permute-start(bf16[352,128]{1,0:T(8,128)(2,1)S(1)} %get-tuple-element.107), channel_id=1, source_target_pairs={{0,6},{2,0},{4,2},{6,4},{1,7},{3,1},{5,3},{7,5},{8,14},{10,8},{12,... | collective-permute-start | bytes 270344 | tf_op jit(solution)/shard_map/ppermute | solution.py:469
  70.8 17.8 %collective-permute-start.25 = (bf16[320,1024]{1,0:T(8,128)(2,1)S(1)}, bf16[320,1024]{1,0:T(8,128)(2,1)S(1)}, u32[]{:S(2)}, u32[]{:S(2)}) collective-permute-start(bf16[320,1024]{1,0:T(8,128)(2,1)S(1)} %get-tuple-element.109.own), channel_id=1, source_target_pairs={{0,8},{2,10},{4,12},{6,14},{1,9},{3,11},{5,13},{7,15},{8,16},{10,1... | collective-permute-start | bytes 1966088 | tf_op jit(solution)/shard_map/ppermute | solution.py:477
  70.9 6.7 %collective-permute-start.19 = (bf16[352,128]{1,0:T(8,128)(2,1)S(1)}, bf16[352,128]{1,0:T(8,128)(2,1)S(1)}, u32[]{:S(2)}, u32[]{:S(2)}) collective-permute-start(bf16[352,128]{1,0:T(8,128)(2,1)S(1)} %get-tuple-element.110), channel_id=1, source_target_pairs={{0,2},{2,4},{4,6},{6,0},{1,3},{3,5},{5,7},{7,1},{8,10},{10,12},{12... | collective-permute-start | bytes 270344 | tf_op jit(solution)/shard_map/ppermute | solution.py:469
  71.0 6.7 %collective-permute-start.20 = (bf16[352,128]{1,0:T(8,128)(2,1)S(1)}, bf16[352,128]{1,0:T(8,128)(2,1)S(1)}, u32[]{:S(2)}, u32[]{:S(2)}) collective-permute-start(bf16[352,128]{1,0:T(8,128)(2,1)S(1)} %get-tuple-element.111), channel_id=1, source_target_pairs={{0,6},{2,0},{4,2},{6,4},{1,7},{3,1},{5,3},{7,5},{8,14},{10,8},{12,... | collective-permute-start | bytes 270344 | tf_op jit(solution)/shard_map/ppermute | solution.py:469
  78.8 9.8 %collective-permute-start.26 = (bf16[512,256]{1,0:T(8,128)(2,1)S(1)}, bf16[512,256]{1,0:T(8,128)(2,1)S(1)}, u32[]{:S(2)}, u32[]{:S(2)}) collective-permute-start(bf16[512,256]{1,0:T(8,128)(2,1)S(1)} %get-tuple-element.115), channel_id=1, source_target_pairs={{0,8},{2,10},{4,12},{6,14},{1,9},{3,11},{5,13},{7,15},{8,16},{10,1... | collective-permute-start | bytes 786440 | tf_op jit(solution)/shard_map/ppermute | solution.py:477
  79.2 6.5 %collective-permute-start.22 = (f32[4,1280]{1,0:T(4,128)S(1)}, f32[4,1280]{1,0:T(4,128)S(1)}, u32[]{:S(2)}, u32[]{:S(2)}) collective-permute-start(f32[4,1280]{1,0:T(4,128)S(1)} %get-tuple-element.113), channel_id=1, source_target_pairs={{0,10},{2,12},{4,14},{6,8},{1,11},{3,13},{5,15},{7,9},{8,18},{10,2... | collective-permute-start | bytes 61448 | tf_op jit(solution)/shard_map/ppermute | solution.py:485
  79.2 6.7 %collective-permute-start.23 = (f32[4,1280]{1,0:T(4,128)S(1)}, f32[4,1280]{1,0:T(4,128)S(1)}, u32[]{:S(2)}, u32[]{:S(2)}) collective-permute-start(f32[4,1280]{1,0:T(4,128)S(1)} %get-tuple-element.113), channel_id=1, source_target_pairs={{0,12},{2,14},{4,8},{6,10},{1,13},{3,15},{5,9},{7,11},{8,20},{10,2... | collective-permute-start | bytes 61448 | tf_op jit(solution)/shard_map/ppermute | solution.py:485
  84.1 4.5 %collective-permute-start.24 = (f32[4,1280]{1,0:T(4,128)S(1)}, f32[4,1280]{1,0:T(4,128)S(1)}, u32[]{:S(2)}, u32[]{:S(2)}) collective-permute-start(f32[4,1280]{1,0:T(4,128)S(1)} %get-tuple-element.113), channel_id=1, source_target_pairs={{0,14},{2,8},{4,10},{6,12},{1,15},{3,9},{5,11},{7,13},{8,22},{10,1... | collective-permute-start | bytes 61448 | tf_op jit(solution)/shard_map/ppermute | solution.py:485
  95.2 6.7 %collective-permute-start.27 = (bf16[352,128]{1,0:T(8,128)(2,1)S(1)}, bf16[352,128]{1,0:T(8,128)(2,1)S(1)}, u32[]{:S(2)}, u32[]{:S(2)}) collective-permute-start(bf16[352,128]{1,0:T(8,128)(2,1)S(1)} %get-tuple-element.117), channel_id=1, source_target_pairs={{0,2},{2,4},{4,6},{6,0},{1,3},{3,5},{5,7},{7,1},{8,10},{10,12},{12... | collective-permute-start | bytes 270344 | tf_op jit(solution)/shard_map/ppermute | solution.py:469
  96.7 5.2 %collective-permute-start.28 = (bf16[352,128]{1,0:T(8,128)(2,1)S(1)}, bf16[352,128]{1,0:T(8,128)(2,1)S(1)}, u32[]{:S(2)}, u32[]{:S(2)}) collective-permute-start(bf16[352,128]{1,0:T(8,128)(2,1)S(1)} %get-tuple-element.118), channel_id=1, source_target_pairs={{0,6},{2,0},{4,2},{6,4},{1,7},{3,1},{5,3},{7,5},{8,14},{10,8},{12,... | collective-permute-start | bytes 270344 | tf_op jit(solution)/shard_map/ppermute | solution.py:469
  106.2 7.2 %collective-permute-start.30 = (bf16[352,128]{1,0:T(8,128)(2,1)S(1)}, bf16[352,128]{1,0:T(8,128)(2,1)S(1)}, u32[]{:S(2)}, u32[]{:S(2)}) collective-permute-start(bf16[352,128]{1,0:T(8,128)(2,1)S(1)} %get-tuple-element.122), channel_id=1, source_target_pairs={{0,2},{2,4},{4,6},{6,0},{1,3},{3,5},{5,7},{7,1},{8,10},{10,12},{12... | collective-permute-start | bytes 270344 | tf_op jit(solution)/shard_map/ppermute | solution.py:469
  106.4 6.9 %collective-permute-start.31 = (bf16[352,128]{1,0:T(8,128)(2,1)S(1)}, bf16[352,128]{1,0:T(8,128)(2,1)S(1)}, u32[]{:S(2)}, u32[]{:S(2)}) collective-permute-start(bf16[352,128]{1,0:T(8,128)(2,1)S(1)} %get-tuple-element.123), channel_id=1, source_target_pairs={{0,6},{2,0},{4,2},{6,4},{1,7},{3,1},{5,3},{7,5},{8,14},{10,8},{12,... | collective-permute-start | bytes 270344 | tf_op jit(solution)/shard_map/ppermute | solution.py:469
  117.5 21.6 %collective-permute-start.33 = (bf16[352,128]{1,0:T(8,128)(2,1)S(1)}, bf16[352,128]{1,0:T(8,128)(2,1)S(1)}, u32[]{:S(2)}, u32[]{:S(2)}) collective-permute-start(bf16[352,128]{1,0:T(8,128)(2,1)S(1)} %get-tuple-element.126), channel_id=1, source_target_pairs={{0,2},{2,4},{4,6},{6,0},{1,3},{3,5},{5,7},{7,1},{8,10},{10,12},{12... | collective-permute-start | bytes 270344 | tf_op jit(solution)/shard_map/ppermute | solution.py:469
  118.6 20.5 %collective-permute-start.34 = (bf16[352,128]{1,0:T(8,128)(2,1)S(1)}, bf16[352,128]{1,0:T(8,128)(2,1)S(1)}, u32[]{:S(2)}, u32[]{:S(2)}) collective-permute-start(bf16[352,128]{1,0:T(8,128)(2,1)S(1)} %get-tuple-element.127), channel_id=1, source_target_pairs={{0,6},{2,0},{4,2},{6,4},{1,7},{3,1},{5,3},{7,5},{8,14},{10,8},{12,... | collective-permute-start | bytes 270344 | tf_op jit(solution)/shard_map/ppermute | solution.py:469
  120.8 15.3 %collective-permute-start.36 = (f32[4,512]{1,0:T(4,128)S(1)}, f32[4,512]{1,0:T(4,128)S(1)}, u32[]{:S(2)}, u32[]{:S(2)}) collective-permute-start(f32[4,512]{1,0:T(4,128)S(1)} %get-tuple-element.130), channel_id=1, source_target_pairs={{0,1},{1,0},{2,3},{3,2},{4,5},{5,4},{6,7},{7,6},{8,9},{9,8},{10,11... | collective-permute-start | bytes 24584 | tf_op jit(solution)/shard_map/ppermute | solution.py:458
  136.7 6.1 %collective-permute-start.37 = (f32[8,512]{1,0:T(8,128)S(1)}, f32[8,512]{1,0:T(8,128)S(1)}, u32[]{:S(2)}, u32[]{:S(2)}) collective-permute-start(f32[8,512]{1,0:T(8,128)S(1)} %shard_map.164), channel_id=1, source_target_pairs={{0,8},{8,16},{16,24},{24,0},{1,9},{9,17},{17,25},{25,1},{2,10},{10... | collective-permute-start | bytes 49160 | tf_op jit(solution)/shard_map/ppermute | solution.py:642
  136.7 6.0 %collective-permute-start.38 = (f32[8,512]{1,0:T(8,128)S(1)}, f32[8,512]{1,0:T(8,128)S(1)}, u32[]{:S(2)}, u32[]{:S(2)}) collective-permute-start(f32[8,512]{1,0:T(8,128)S(1)} %shard_map.164), channel_id=1, source_target_pairs={{0,16},{8,24},{16,0},{24,8},{1,17},{9,25},{17,1},{25,9},{2,18},{10... | collective-permute-start | bytes 49160 | tf_op jit(solution)/shard_map/ppermute | solution.py:642
  138.7 4.1 %collective-permute-start.39 = (f32[8,512]{1,0:T(8,128)S(1)}, f32[8,512]{1,0:T(8,128)S(1)}, u32[]{:S(2)}, u32[]{:S(2)}) collective-permute-start(f32[8,512]{1,0:T(8,128)S(1)} %shard_map.164), channel_id=1, source_target_pairs={{0,24},{8,0},{16,8},{24,16},{1,25},{9,1},{17,9},{25,17},{2,26},{10... | collective-permute-start | bytes 49160 | tf_op jit(solution)/shard_map/ppermute | solution.py:642
  (24 other events, 167.9 us)
